TPU v7x, 32 devices: a whole 2x2x4 slice. The times are simulated.
32 devices in a mesh: row: 16 (over z, y, x), col: 2 (over core).
Axes of the slice: x: 2, y: 2, z: 4, core: 2. Of those that a mesh axis runs over, the one named last changes fastest.
Arguments:
- slab: bfloat16 [65536, 2048], P('row', 'col'), may hold values from -6 to 6
- gauss: bfloat16 [2048, 1024], P('col'), may hold values from -0.125 to 0.125
- pivots: int32 [1024], replicated, may hold values from 0 to 65535, as said below
- block_inverses: float32 [8, 128, 128], replicated, may hold values from -2 to 2
Outputs:
- factor_rows: float32 [65536, 1024], P(('row', 'col'))
- pivot_block: float32 [1024, 1024], P(('row', 'col'))
Inputs may be any that keep to these rules, and one draw needn't show every extreme that they name: `pivots`: distinct row numbers; each aligned block of 2048 rows holds at most 128 of them, and some block holds exactly 128.
All inputs are finite; a program needn't handle non-finite values.
Results may differ from a plain program's by a relative error of at most 0.0003.
Values may be sent and summed in bfloat16 or wider, within the bound.
No kernel may reach another device: no remote copies, remote signals or barrier semaphores. Data moves between devices by JAX's collectives and lax.ppermute only.
A program may use at most 128 MiB of HBM per device.

v0:
```python
import jax
import jax.numpy as jnp
from jax import lax
from jax.sharding import PartitionSpec as P

K = 1024
BLK = 128


def on_device(slab, gauss, pivots, block_inverses):
    col_count = lax.axis_size("col")
    devices = lax.axis_size("row") * col_count
    shard_rows = slab.shape[0] // col_count
    width = gauss.shape[1]
    sketch = lax.psum_scatter(
        jnp.dot(slab, gauss, preferred_element_type=jnp.float32),
        "col",
        scatter_dimension=0,
        tiled=True,
    )
    owner = lax.axis_index("row") * col_count + lax.axis_index("col")
    local_rows = pivots - owner * shard_rows
    present = (local_rows >= 0) & (local_rows < shard_rows)
    picked = jnp.take(sketch, jnp.clip(local_rows, 0, shard_rows - 1), axis=0)
    picked = jnp.where(present[:, None], picked, 0.0)
    share = width // devices
    pivot_block = lax.psum(picked, ("row", "col"))
    own_pivots = lax.dynamic_slice_in_dim(pivot_block, owner * share, share, 0)
    factor = 1.0 / K**0.5
    solved = []
    for block in range(K // BLK):
        acc = sketch[:, block * BLK : (block + 1) * BLK]
        if block > 0:
            earlier = jnp.concatenate(solved, axis=1)
            coupling = pivot_block[: block * BLK, block * BLK : (block + 1) * BLK]
            acc = acc - factor * jnp.dot(earlier, coupling, precision=lax.Precision.HIGHEST)
        solved.append(jnp.dot(acc, block_inverses[block], precision=lax.Precision.HIGHEST))
    factor_rows = jnp.concatenate(solved, axis=1)
    return (factor_rows, own_pivots)


def solution(mesh):
    return jax.shard_map(
        on_device,
        mesh=mesh,
        in_specs=(P("row", "col"), P("col", None), P(), P()),
        out_specs=(P(("row", "col"), None), P(("row", "col"), None)),
        check_vma=False,
    )
```

profile of v0, /device:TPU:0, one launch (start us, length us, event | category | flops | bytes accessed | tf_op | source)
XLA Modules:
  0.0 304.2 jit_solution(6258736372025824150)
XLA Ops:
  7.2 1.5 copy-done
  8.8 14.5 %fusion.69 = f32[4096,1024]{1,0:T(8,128)} fusion(bf16[4096,1024]{1,0:T(8,128)(2,1)} %param.4, bf16[1024,1024]{1,0:T(8,128)(2,1)S(1)} %copy-done), kind=kOutput, calls=%fused_computation.98 | convolution fusion | flops 8589934592 | bytes 27262976 | tf_op jit(solution)/shard_map/dot_general | solution.py:16
  23.3 0.6 copy-done.5
  24.0 28.4 %reduce-scatter.2.cloned.1.call-done = f32[2048,1024]{1,0:T(8,128)} async-done(((f32[4096,1024]{1,0:T(8,128)}), f32[2048,1024]{1,0:T(8,128)}) %reduce-scatter.2.cloned.1.call-update) | async-done | bytes 8388624 | tf_op jit(solution)/shard_map/reduce_scatter | solution.py:15
  52.4 9.7 %gather_fusion = f32[1024,1024]{1,0:T(8,128)} fusion(f32[2048,1024]{1,0:T(8,128)} %reduce-scatter.2.cloned.1.call-done, s32[1024]{0:T(1024)S(1)} %fusion.65), kind=kCustom, calls=%fused_computation | custom fusion | bytes 8392704 | tf_op jit(solution)/shard_map/jit(_take)/gather | solution.py:24
  62.1 4.3 %select_select_fusion = f32[1024,1024]{1,0:T(8,128)} fusion(f32[1024,1024]{1,0:T(8,128)} %gather_fusion, pred[1024]{0:T(1024)(128)(4,1)S(1)} %get-tuple-element.30, pred[1024]{0:T(1024)(128)(4,1)S(1)} %get-tuple-element.29), kind=kLoop, calls=%fused_computation.9 | loop fusion | flops 2097152 | bytes 8390656 | tf_op jit(solution)/shard_map/jit(_where)/select_n | solution.py:25
  66.5 4.5 %constant_dynamic-update-slice_fusion.17 = (f32[2048,896]{0,1:T(8,128)}, f32[2048,1024]{0,1:T(8,128)}, f32[2048,768]{0,1:T(8,128)}, f32[2048,640]{0,1:T(8,128)}, f32[2048,128]{0,1:T(8,128)S(1)}) fusion(f32[8,128,128]{2,1,0:T(8,128)S(1)} %copy-done.4, f32[2048,1024]{1,0:T(8,128)} %reduce-scatter.2.cloned.1.call-done), kind=kOutput, calls=%fused_computation.82 | convolution fusion | flops 402653184 | bytes 6356992 | tf_op jit(solution)/shard_map/dot_general | solution.py:37
  71.0 138.6 %all-reduce.2.cloned.1.call-done = f32[1024,1024]{1,0:T(8,128)} async-done(((f32[1024,1024]{1,0:T(8,128)}), f32[1024,1024]{1,0:T(8,128)}) %all-reduce.2.cloned.1.call-update) | async-done | bytes 4194320 | tf_op jit(solution)/shard_map/psum | solution.py:27
  209.6 3.1 %fusion.21 = f32[2048,128]{1,0:T(8,128)S(1)} fusion(f32[2048,128]{0,1:T(8,128)S(1)} %get-tuple-element.31, f32[2048,1024]{1,0:T(8,128)} %reduce-scatter.2.cloned.1.call-done, f32[1024,1024]{1,0:T(8,128)} %all-reduce.2.cloned.1.call-done), kind=kOutput, calls=%fused_computation.27 | convolution fusion | flops 403177472 | bytes 3211264 | tf_op jit(solution)/shard_map/dot_general | solution.py:36
  212.8 3.3 %constant_dynamic-update-slice_fusion.16 = (f32[2048,896]{0,1:T(8,128)}, f32[2048,1024]{0,1:T(8,128)}, f32[2048,768]{0,1:T(8,128)}, f32[2048,640]{0,1:T(8,128)}, f32[2048,128]{0,1:T(8,128)S(1)}) fusion(f32[2048,896]{0,1:T(8,128)} %get-tuple-element.25, f32[2048,1024]{0,1:T(8,128)} %get-tuple-element.26, f32[2048,768]{0,1:T(8,128)} %get-tuple-element.27, ...), kind=kOutput, calls=%fused_computation.81 | convolution fusion | flops 402653184 | bytes 6356992 | tf_op jit(solution)/shard_map/dot_general | solution.py:37
  216.1 4.9 %fusion.19 = f32[2048,128]{1,0:T(8,128)S(1)} fusion(f32[2048,128]{0,1:T(8,128)S(1)} %get-tuple-element.32, f32[2048,128]{0,1:T(8,128)S(1)} %get-tuple-element.31, f32[2048,1024]{1,0:T(8,128)} %reduce-scatter.2.cloned.1.call-done, f32[1024,1024]{1,0:T(8,128)} %all-reduce.2.cloned.1.call-done), kind=kOutput, calls=%fused_computation.24 | convolution fusion | flops 806354944 | bytes 4325376 | tf_op jit(solution)/shard_map/dot_general | solution.py:36
  221.0 3.3 %constant_dynamic-update-slice_fusion.15 = (f32[2048,896]{0,1:T(8,128)}, f32[2048,1024]{0,1:T(8,128)}, f32[2048,768]{0,1:T(8,128)}, f32[2048,640]{0,1:T(8,128)}, f32[2048,128]{0,1:T(8,128)S(1)}) fusion(f32[2048,896]{0,1:T(8,128)} %get-tuple-element.21, f32[2048,1024]{0,1:T(8,128)} %get-tuple-element.22, f32[2048,768]{0,1:T(8,128)} %get-tuple-element.23, ...), kind=kOutput, calls=%fused_computation.80 | convolution fusion | flops 402653184 | bytes 6356992 | tf_op jit(solution)/shard_map/dot_general | solution.py:37
  224.3 6.7 %fusion.22 = f32[2048,128]{1,0:T(8,128)S(1)} fusion(f32[2048,128]{0,1:T(8,128)S(1)} %get-tuple-element.33, f32[2048,128]{0,1:T(8,128)S(1)} %get-tuple-element.32, f32[2048,128]{0,1:T(8,128)S(1)} %get-tuple-element.31, f32[2048,1024]{1,0:T(8,128)S(1)} %bitcast.52, f32[1024,1024]{1,0:T(8,128)} %all-reduce.2.cloned.1.call-done), kind=kOutput, calls=%fused_computation.28 | convolution fusion | flops 1210056704 | bytes 5439488 | tf_op jit(solution)/shard_map/dot_general | solution.py:36
  231.0 3.3 %constant_dynamic-update-slice_fusion.14 = (f32[2048,896]{0,1:T(8,128)}, f32[2048,1024]{0,1:T(8,128)}, f32[2048,768]{0,1:T(8,128)}, f32[2048,640]{0,1:T(8,128)}, f32[2048,128]{0,1:T(8,128)S(1)}) fusion(f32[2048,896]{0,1:T(8,128)} %get-tuple-element.17, f32[2048,1024]{0,1:T(8,128)} %get-tuple-element.18, f32[2048,768]{0,1:T(8,128)} %get-tuple-element.19, ...), kind=kOutput, calls=%fused_computation.79 | convolution fusion | flops 402653184 | bytes 6356992 | tf_op jit(solution)/shard_map/dot_general | solution.py:37
  234.3 7.8 %fusion.28 = f32[2048,128]{1,0:T(8,128)S(1)} fusion(f32[2048,128]{0,1:T(8,128)S(1)} %get-tuple-element.34, f32[2048,128]{0,1:T(8,128)S(1)} %get-tuple-element.33, f32[2048,128]{0,1:T(8,128)S(1)} %get-tuple-element.32, f32[2048,128]{0,1:T(8,128)S(1)} %get-tuple-element.31, f32[2048,1024]{1,0:T(8,128)S(1)} %bitcast.52, ...), kind=kOutput, calls=%fused_computation.30 | convolution fusion | flops 1614282752 | bytes 6553600 | tf_op jit(solution)/shard_map/dot_general | solution.py:36
  242.2 2.9 constant_dynamic-update-slice_fusion.13
  245.0 10.7 %fusion.18 = f32[2048,128]{1,0:T(8,128)S(1)} fusion(f32[2048,640]{0,1:T(8,128)} %get-tuple-element.12, f32[2048,1024]{1,0:T(8,128)S(1)} %bitcast.52, f32[1024,1024]{1,0:T(8,128)} %all-reduce.2.cloned.1.call-done), kind=kOutput, calls=%fused_computation.22 | convolution fusion | flops 2013790208 | bytes 7667712 | tf_op jit(solution)/shard_map/dot_general | solution.py:36
  255.8 2.1 constant_dynamic-update-slice_fusion.12
  257.9 10.9 %fusion.14 = f32[2048,128]{1,0:T(8,128)S(1)} fusion(f32[2048,768]{0,1:T(8,128)S(1)} %get-tuple-element.8, f32[2048,1024]{1,0:T(8,128)S(1)} %bitcast.52, f32[1024,1024]{1,0:T(8,128)} %all-reduce.2.cloned.1.call-done), kind=kOutput, calls=%fused_computation.18 | convolution fusion | flops 2416443392 | bytes 8781824 | tf_op jit(solution)/shard_map/dot_general | solution.py:36
  268.9 2.3 constant_dynamic-update-slice_fusion.11
  271.2 13.0 %fusion.20 = f32[2048,128]{1,0:T(8,128)S(1)} fusion(f32[2048,896]{0,1:T(8,128)S(1)} %get-tuple-element.4, f32[2048,1024]{1,0:T(8,128)S(1)} %bitcast.52, f32[1024,1024]{1,0:T(8,128)} %all-reduce.2.cloned.1.call-done), kind=kOutput, calls=%fused_computation.25 | convolution fusion | flops 2819096576 | bytes 9895936 | tf_op jit(solution)/shard_map/dot_general | solution.py:36
  284.2 2.1 convolution_dynamic-update-slice_fusion
  286.3 9.2 %copy.6 = f32[2048,1024]{1,0:T(8,128)} copy(f32[2048,1024]{0,1:T(8,128)} %convolution_dynamic-update-slice_fusion) | data formatting | bytes 16777216
  295.6 1.6 constant_dynamic-slice_fusion
  (21 shorter events, 0.2 us)
Async XLA Ops:
  7.2 1.6 copy-start
  7.2 45.2 %reduce-scatter.2.cloned.1.call-start = ((), (), s32[]{:S(2)}) async-start(), calls=%async_computation.1 | async-start | bytes 25165824 | tf_op jit(solution)/shard_map/reduce_scatter | solution.py:15
  23.3 0.7 copy-start.5
  23.3 186.4 %all-reduce.2.cloned.1.call-start = ((), (), s32[]{:S(2)}) async-start(), calls=%async_computation.2 | async-start | bytes 8388608 | tf_op jit(solution)/shard_map/psum | solution.py:27
  62.1 4.3 %copy-start.4 = (f32[8,128,128]{2,1,0:T(8,128)S(1)}, f32[8,128,128]{2,1,0:T(8,128)}, u32[]{:S(2)}) copy-start(f32[8,128,128]{2,1,0:T(8,128)} %param.7) | copy-start | bytes 1572868
  212.8 11.5 %slice-start = ((s8[8388608]{0:T(1024)(128)(4,1)}), s8[4194304]{0:T(1024)(128)(4,1)S(1)}, s32[]{:S(2)}) async-start(s8[8388608]{0:T(1024)(128)(4,1)} %bitcast.51), calls=%async_computation.3 | async-start | bytes 8388608
  216.1 8.2 %slice-start.1 = ((s8[8388608]{0:T(1024)(128)(4,1)}), s8[4194304]{0:T(1024)(128)(4,1)S(1)}, s32[]{:S(2)}) async-start(s8[8388608]{0:T(1024)(128)(4,1)} %bitcast.51), calls=%async_computation.4 | async-start | bytes 8388608
  234.3 7.8 %copy-start.2 = (f32[2048,896]{0,1:T(8,128)S(1)}, f32[2048,896]{0,1:T(8,128)}, u32[]{:S(2)}) copy-start(f32[2048,896]{0,1:T(8,128)} %get-tuple-element.13) | copy-start | bytes 22020100
  245.0 10.7 %copy-start.3 = (f32[2048,768]{0,1:T(8,128)S(1)}, f32[2048,768]{0,1:T(8,128)}, u32[]{:S(2)}) copy-start(f32[2048,768]{0,1:T(8,128)} %get-tuple-element.11) | copy-start | bytes 18874372
  284.2 12.9 %copy-start.1 = (bf16[1024,1024]{1,0:T(8,128)(2,1)S(1)}, bf16[1024,1024]{1,0:T(8,128)(2,1)}, u32[]{:S(2)}) copy-start(bf16[1024,1024]{1,0:T(8,128)(2,1)} %param.5) | copy-start | bytes 6291460
Sparse Core Ops, SparseCore 0:
  23.4 28.9 reduce-scatter.1
  66.6 142.9 all-reduce.1
where the time goes:
time: 309 us; the launch traced here: 304 us
  waiting for transfers between devices  167 us (54%)
  matrix products  95.6 us (31%)
  local copies, waits for them, and re-layouts  22.7 us (7%)
  between operations  14.4 us (5%)
  other arithmetic  4.34 us (1%)
    psum x1, waiting for transfers between devices, on_device(): pivot_block = lax.psum(picked, ('row', 'col'))  139 us
    dot_general x7, matrix products, on_device(): jnp.dot(earlier, coupling, precision=lax.Precision.HIGHEST)  57.2 us
    reduce_scatter x1, waiting for transfers between devices, on_device(): lax.psum_scatter(jnp.dot(slab, gauss, preferred_element_type=jnp.float32)...  28.4 us
    dot_general x8, matrix products, on_device(): jnp.dot(acc, block_inverses[block], precision=lax.Precision.HIGHEST)  23.9 us
    dot_general x1, matrix products, on_device(): jnp.dot(slab, gauss, preferred_element_type=jnp.float32)  14.5 us
    unnamed x17, local copies, waits for them, and re-layouts  11.4 us
    gather x1, local copies, waits for them, and re-layouts, on_device(): picked = jnp.take(sketch, jnp.clip(local_rows, 0, shard_rows - 1), axis=0)  9.71 us
  transfers between devices with their start and end apart: 2, of which 2 were waited for; matrix products, arithmetic and copies ran while one was open for 1% of the time, Pallas kernels for 0%

commit v1 on v0

v1 whole, which is shorter than its diff:
```python
import jax
import jax.numpy as jnp
from jax import lax
from jax.experimental import pallas as pl
from jax.experimental.pallas import tpu as pltpu
from jax.sharding import PartitionSpec as P

K = 1024
BLK = 128
NBLK = K // BLK
SHARD_ROWS = 2048
PIV_MOST = 128
SUB = 16
UPPER = [(i, j) for i in range(NBLK) for j in range(i + 1, NBLK)]
F32 = jnp.float32
BF16 = jnp.bfloat16
MIB = 1 << 20


def dot(a, b, dims=((1,), (0,))):
    return lax.dot_general(a, b, (dims, ((), ())), preferred_element_type=F32)


def split(a):
    high = a.astype(BF16)
    return high, (a - high.astype(F32)).astype(BF16)


def group_slot(group, x, y, c):
    gy, gx, gc = group >> 2, (group >> 1) & 1, group & 1
    dx, dy, dc = gx ^ x, gy ^ y, gc ^ c
    return dc * 4 + (dx * 2 + dy if gc == 0 else dy * 2 + dx)


def slot_group(slot, x, y, c):
    dc, high, low = slot >> 2, (slot >> 1) & 1, slot & 1
    gc = c ^ dc
    dx = jnp.where(gc == 0, high, low)
    dy = jnp.where(gc == 0, low, high)
    return (y ^ dy) * 4 + (x ^ dx) * 2 + gc


def lower_layout(share):
    tops = K // (8 * share)
    return [-(-((z + 1) * 8 * share) // BLK) for z in range(tops)]


def pick_kernel(share, meta, piv, slab, gauss, u_keep, u_send, l_keep, l_send,
                slab_v, gauss_v, rows_v, u_scr, l_scr, sems):
    r, c = meta[0], meta[1]
    x, y = r & 1, (r >> 1) & 1
    copies = [
        pltpu.make_async_copy(
            slab.at[pl.ds(t * 1024, 1024)], slab_v.at[pl.ds(t * 1024, 1024)], sems.at[t])
        for t in range(4)
    ]
    copies.append(pltpu.make_async_copy(gauss, gauss_v, sems.at[4]))
    for copy in copies:
        copy.start()

    half = lax.broadcasted_iota(jnp.int32, (8, K), 0)
    local = piv[...] - (r * (2 * SHARD_ROWS) + half * SHARD_ROWS)
    inside = (local >= 0) & (local < SHARD_ROWS) & (half < 2)
    earlier = lax.broadcasted_iota(jnp.int32, (K, K), 0) < lax.broadcasted_iota(jnp.int32, (K, K), 1)
    rank = dot(jnp.where(inside, 1.0, 0.0).astype(BF16), jnp.where(earlier, 1.0, 0.0).astype(BF16))
    rank = jnp.where(inside, rank, -1.0)
    order = lax.broadcasted_iota(jnp.int32, (PIV_MOST, K), 0).astype(F32)
    rows = lax.broadcasted_iota(jnp.int32, (PIV_MOST, SHARD_ROWS), 1).astype(F32)
    place, picks = [], []
    for b in range(2):
        hit = rank[b:b + 1, :] == order
        place.append(jnp.where(hit, 1.0, 0.0).astype(BF16))
        row = jnp.sum(jnp.where(hit, local[b:b + 1, :].astype(F32), 0.0), axis=1, keepdims=True)
        picks.append(jnp.where(rows == row, 1.0, 0.0).astype(BF16))
    packed = []
    for b in range(2):
        copies[2 * b].wait()
        part = dot(picks[b][:, :1024], slab_v[pl.ds(b * 2048, 1024), :])
        copies[2 * b + 1].wait()
        part = part + dot(picks[b][:, 1024:], slab_v[pl.ds(b * 2048 + 1024, 1024), :])
        packed.append(part.astype(BF16))
    packed = jnp.concatenate(packed, axis=0)
    place = jnp.concatenate(place, axis=0)
    copies[4].wait()
    for t in range(4):
        spread = dot(place[:, t * 256:(t + 1) * 256], packed, ((0,), (0,))).astype(BF16)
        rows_v[pl.ds(t * 256, 256), :] = dot(spread, gauss_v[...])

    columns = lower_layout(share)
    for group in range(8):
        slot = group_slot(group, x, y, c)
        for n, (i, j) in enumerate(UPPER):
            u_scr[slot, n] = rows_v[pl.ds(i * BLK + group * SUB, SUB), pl.ds(j * BLK, BLK)]
        n = 0
        for z, count in enumerate(columns):
            for j in range(count):
                l_scr[slot, n] = rows_v[pl.ds((z * 8 + group) * share, share), pl.ds(j * BLK, BLK)]
                n += 1
    u_keep[...] = u_scr[0:4]
    u_send[...] = u_scr[4:8]
    l_keep[...] = l_scr[0:4]
    l_send[...] = l_scr[4:8]


def pick(meta, piv, slab, gauss, share):
    units = sum(lower_layout(share))
    u_shape = jax.ShapeDtypeStruct((4, len(UPPER), SUB, BLK), F32)
    l_shape = jax.ShapeDtypeStruct((4, units, share, BLK), F32)
    vmem = pl.BlockSpec(memory_space=pltpu.VMEM)
    return pl.pallas_call(
        lambda *refs: pick_kernel(share, *refs),
        out_shape=(u_shape, u_shape, l_shape, l_shape),
        in_specs=[pl.BlockSpec(memory_space=pltpu.SMEM), vmem,
                  pl.BlockSpec(memory_space=pl.ANY), pl.BlockSpec(memory_space=pl.ANY)],
        out_specs=(vmem,) * 4,
        scratch_shapes=[
            pltpu.VMEM((2 * SHARD_ROWS, K), BF16),
            pltpu.VMEM((K, K), BF16),
            pltpu.VMEM((K, K), F32),
            pltpu.VMEM((8, len(UPPER), SUB, BLK), F32),
            pltpu.VMEM((8, units, share, BLK), F32),
            pltpu.SemaphoreType.DMA((5,)),
        ],
        compiler_params=pltpu.CompilerParams(vmem_limit_bytes=44 * MIB),
        cost_estimate=pl.CostEstimate(flops=6 * 10**9, bytes_accessed=16 * MIB, transcendentals=0),
        name="pick_pivot_rows",
    )(meta, piv, slab, gauss)


def sketch_kernel(meta, mine, theirs, gauss_mine, gauss_theirs, out):
    out[...] = dot(mine[...], gauss_mine[...]) + dot(theirs[...], gauss_theirs[...])


def sketch_rows(meta, slab, theirs, gauss_mine, gauss_theirs):
    rows, depth = theirs.shape
    tile = 256
    whole = pl.BlockSpec((depth, K), lambda t, meta: (0, 0))
    return pl.pallas_call(
        sketch_kernel,
        out_shape=jax.ShapeDtypeStruct((rows, K), F32),
        grid_spec=pltpu.PrefetchScalarGridSpec(
            num_scalar_prefetch=1,
            grid=(rows // tile,),
            in_specs=[
                pl.BlockSpec((tile, depth), lambda t, meta: (meta[1] * (rows // tile) + t, 0)),
                pl.BlockSpec((tile, depth), lambda t, meta: (t, 0)),
                whole, whole,
            ],
            out_specs=pl.BlockSpec((tile, K), lambda t, meta: (t, 0)),
        ),
        compiler_params=pltpu.CompilerParams(vmem_limit_bytes=32 * MIB),
        cost_estimate=pl.CostEstimate(
            flops=4 * rows * depth * K, bytes_accessed=20 * MIB, transcendentals=0),
        name="sketch_rows",
    )(meta, slab, theirs, gauss_mine, gauss_theirs)


def product(a, b):
    return dot(a[0], b[0]) + (dot(a[1], b[0]) + dot(a[0], b[1]))


def solve_kernel(share, meta, sketch, inverses, p0, p1, p2, p3, out, own_rows,
                 coupling, c_high, c_low, d_high, d_low, f_high, f_low):
    r, c = meta[0], meta[1]
    x, y = r & 1, (r >> 1) & 1

    @pl.when(pl.program_id(0) == 0)
    def _():
        coupling[...] = jnp.zeros_like(coupling)
        slot = 0
        for piece in (p0, p1, p2, p3):
            for k in range(piece.shape[0]):
                group = slot_group(slot, x, y, c)
                for n, (i, j) in enumerate(UPPER):
                    at = pl.multiple_of(i * BLK + group * SUB, SUB)
                    coupling[pl.ds(at, SUB), pl.ds(j * BLK, BLK)] = piece[k, n]
                slot += 1
        own = pl.multiple_of((r * 2 + c) * share, share)
        own_rows[...] = coupling[pl.ds(own, share), :]
        scaled = coupling[...] * (-1.0 / K**0.5)
        c_high[...], c_low[...] = split(scaled)
        for s in range(NBLK // 2):
            first, second = inverses[2 * s], inverses[2 * s + 1]
            link = coupling[pl.ds(2 * s * BLK, BLK), pl.ds((2 * s + 1) * BLK, BLK)]
            link = link * (-1.0 / K**0.5)
            highest = dict(precision=lax.Precision.HIGHEST, preferred_element_type=F32)
            corner = jnp.dot(first, jnp.dot(link, second, **highest), **highest)
            for at, value in ((0, first), (1, corner), (3, second), (2, jnp.zeros_like(first))):
                high, low = split(value)
                spot = (s, pl.ds((at >> 1) * BLK, BLK), pl.ds((at & 1) * BLK, BLK))
                d_high[spot] = high
                d_low[spot] = low

    wide = 2 * BLK
    for s in range(NBLK // 2):
        cols = pl.ds(s * wide, wide)
        acc = sketch[:, cols]
        if s > 0:
            before = pl.ds(0, s * wide)
            acc = acc + product((f_high[:, before], f_low[:, before]),
                                (c_high[before, cols], c_low[before, cols]))
        solved = product(split(acc), (d_high[s], d_low[s]))
        out[:, cols] = solved
        if s < NBLK // 2 - 1:
            f_high[:, cols], f_low[:, cols] = split(solved)


def solve(meta, sketch, inverses, pieces, share):
    rows = sketch.shape[0]
    tile = 512
    wide = 2 * BLK

    def whole(a):
        return pl.BlockSpec(a.shape, lambda t, meta, n=a.ndim: (0,) * n)

    return pl.pallas_call(
        lambda *refs: solve_kernel(share, *refs),
        out_shape=(jax.ShapeDtypeStruct((rows, K), F32), jax.ShapeDtypeStruct((share, K), F32)),
        grid_spec=pltpu.PrefetchScalarGridSpec(
            num_scalar_prefetch=1,
            grid=(rows // tile,),
            in_specs=[pl.BlockSpec((tile, K), lambda t, meta: (t, 0)), whole(inverses)]
            + [whole(p) for p in pieces],
            out_specs=(pl.BlockSpec((tile, K), lambda t, meta: (t, 0)),
                       pl.BlockSpec((share, K), lambda t, meta: (0, 0))),
            scratch_shapes=[
                pltpu.VMEM((K, K), F32),
                pltpu.VMEM((K, K), BF16),
                pltpu.VMEM((K, K), BF16),
                pltpu.VMEM((NBLK // 2, wide, wide), BF16),
                pltpu.VMEM((NBLK // 2, wide, wide), BF16),
                pltpu.VMEM((tile, K), BF16),
                pltpu.VMEM((tile, K), BF16),
            ],
        ),
        compiler_params=pltpu.CompilerParams(vmem_limit_bytes=48 * MIB),
        cost_estimate=pl.CostEstimate(flops=8 * 10**9, bytes_accessed=20 * MIB, transcendentals=0),
        name="blocked_solve",
    )(meta, sketch, inverses, *pieces)


def on_device(slab, gauss, pivots, block_inverses):
    rows = lax.axis_size("row")
    cols = lax.axis_size("col")
    bits = rows.bit_length() - 1
    share = K // (rows * cols)
    r, c = lax.axis_index("row"), lax.axis_index("col")
    meta = jnp.stack([r, c]).astype(jnp.int32)

    def swap(value, bit_of):
        perm = [(2 * i + k, 2 * (i ^ (1 << bit_of[k])) + k) for i in range(rows) for k in range(2)]
        return lax.ppermute(value, ("row", "col"), perm)

    def swap_cores(value):
        return lax.ppermute(value, "col", [(0, 1), (1, 0)])

    near, far = (0, 1), (1, 0)
    tops = bits - 2
    climb = [(2 + s, 2 + (s + 1) % tops) for s in range(tops)]

    u_keep, u_send, l_keep, l_send = pick(meta, pivots.reshape(1, K), slab, gauss, share)

    u_got = swap_cores(u_send)
    send = u_keep[2:4] + u_got[2:4]
    got = swap(send, near)
    send = (u_keep[1:2] + u_got[1:2]) + got[1:2]
    kept = (u_keep[0:1] + u_got[0:1]) + got[0:1]
    total = kept + swap(send, far)
    for bit_of in climb:
        total = total + swap(total, bit_of)
    piece1 = swap(total, far)
    pair = jnp.concatenate([total, piece1], axis=0)
    piece2 = swap(pair, near)
    piece3 = swap_cores(jnp.concatenate([pair, piece2], axis=0))

    own = slab.shape[0] // cols
    slab_theirs = swap_cores(lax.dynamic_slice_in_dim(slab, (1 - c) * own, own, 0))
    gauss_theirs = swap_cores(gauss)
    sketch = sketch_rows(meta, slab, slab_theirs, gauss, gauss_theirs)

    l_got = swap_cores(l_send)
    got = swap(l_keep[2:4] + l_got[2:4], near)
    low = (l_keep[0] + l_got[0]) + got[0]
    low = low + swap((l_keep[1] + l_got[1]) + got[1], far)
    columns = lower_layout(share)
    spread, n = [], 0
    for count in columns:
        spread.append(jnp.pad(low[n:n + count], ((0, NBLK - count), (0, 0), (0, 0))))
        n += count
    low = jnp.stack(spread)
    for s in range(tops):
        bit = (r >> (bits - 1 - s)) & 1
        halves = low.reshape((2, low.shape[0] // 2) + low.shape[1:])
        away = lax.dynamic_index_in_dim(halves, 1 - bit, 0, keepdims=False)
        stay = lax.dynamic_index_in_dim(halves, bit, 0, keepdims=False)
        low = stay + swap(away, (bits - 1 - s,) * 2)
    low_rows = low[0].transpose(1, 0, 2).reshape(share, K)

    factor_rows, up_rows = solve(meta, sketch, block_inverses, (total, piece1, piece2, piece3), share)
    diagonal = (r * 2 + c) * share // BLK
    column = lax.broadcasted_iota(jnp.int32, (share, K), 1) // BLK
    return factor_rows, jnp.where(column > diagonal, up_rows, low_rows)


def solution(mesh):
    return jax.shard_map(
        on_device,
        mesh=mesh,
        in_specs=(P("row", "col"), P("col", None), P(), P()),
        out_specs=(P(("row", "col"), None), P(("row", "col"), None)),
        check_vma=False,
    )
```

time: 309 us -> 114 us (0.37); the launches traced: 304 us -> 113 us
  waiting for transfers between devices: 167 us -> 34 us
  matrix products: 95.6 us -> 0 us
  Pallas kernels: 0 us -> 44.1 us
  starting transfers between devices: 0.08 us -> 18.1 us
  local copies, waits for them, and re-layouts: 22.7 us -> 8.83 us
  between operations: 14.4 us -> 0.83 us
  other arithmetic: 4.34 us -> 7.61 us
    psum x1 -> x0, waiting for transfers between devices: 139 us -> none  [on_device(): pivot_block = lax.psum(picked, ('row', 'col'))]
    dot_general x16 -> x0, matrix products: 95.6 us -> none  [the longest x7 57.2 us: on_device(): jnp.dot(earlier, coupling, precision=lax.Precision.HIGHEST)]
    pallas_call x0 -> x3, Pallas kernels: none -> 44.1 us  [the longest x1 21.3 us: solve(): pl.pallas_call(lambda *refs: solve_kernel(share, *refs), out_shape=(jax.S...]
    ppermute x0 -> x15, waiting for transfers between devices: none -> 34 us  [the longest x10 34 us: swap(): return lax.ppermute(value, ('row', 'col'), perm)]
    reduce_scatter x1 -> x0, waiting for transfers between devices: 28.4 us -> none  [on_device(): lax.psum_scatter(jnp.dot(slab, gauss, preferred_element_type=jnp.float32)...]
    ppermute x0 -> x15, starting transfers between devices: none -> 18.1 us  [the longest x10 17 us: swap(): return lax.ppermute(value, ('row', 'col'), perm)]
    gather x1 -> x0, local copies, waits for them, and re-layouts: 9.71 us -> none  [on_device(): picked = jnp.take(sketch, jnp.clip(local_rows, 0, shard_rows - 1), axis=0)]
    unnamed x17 -> x8, local copies, waits for them, and re-layouts: 11.4 us -> 3.95 us
  transfers between devices with their start and end apart: 2 -> 15, of which waited for: 2 -> 7; matrix products, arithmetic and copies ran while one was open for 1% -> 10% of each run, Pallas kernels for 0% -> 12%
where the time goes in v1:
time: 114 us; the launch traced here: 113 us
  Pallas kernels  44.1 us (39%)
  waiting for transfers between devices  34 us (30%)
  starting transfers between devices  18.1 us (16%)
  local copies, waits for them, and re-layouts  8.83 us (8%)
  other arithmetic  7.61 us (7%)
    ppermute x10, waiting for transfers between devices, swap(): return lax.ppermute(value, ('row', 'col'), perm)  34 us
    pallas_call x1, Pallas kernels, solve(): pl.pallas_call(lambda *refs: solve_kernel(share, *refs), out_shape=(jax.S...  21.3 us
    ppermute x10, starting transfers between devices, swap(): return lax.ppermute(value, ('row', 'col'), perm)  17 us
    pallas_call x1, Pallas kernels, sketch_rows(): pl.pallas_call(sketch_kernel, out_shape=jax.ShapeDtypeStruct((rows, K), F...  13.5 us
    pallas_call x1, Pallas kernels, pick(): pl.pallas_call(lambda *refs: pick_kernel(share, *refs), out_shape=(u_shap...  9.31 us
    dynamic_slice x1, local copies, waits for them, and re-layouts, on_device(): lax.dynamic_slice_in_dim(slab, (1 - c) * own, own, 0)  4.64 us
    unnamed x8, local copies, waits for them, and re-layouts  3.95 us
  transfers between devices with their start and end apart: 15, of which 7 were waited for; matrix products, arithmetic and copies ran while one was open for 10% of the time, Pallas kernels for 12%

profile of v1, /device:TPU:0, one launch (start us, length us, event | category | flops | bytes accessed | tf_op | source)
XLA Modules:
  0.0 113.5 jit_solution(8267258952402776751)
XLA Ops:
  1.4 9.3 %pick_pivot_rows.1 = (f32[4,28,16,128]{3,2,1,0:T(8,128)S(1)}, f32[4,28,16,128]{3,2,1,0:T(8,128)S(1)}, f32[4,20,32,128]{3,2,1,0:T(8,128)S(1)}, f32[4,20,32,128]{3,2,1,0:T(8,128)}) custom-call(s32[2]{0:T(128)S(1)} %pad_add_fusion.meta.refs_0_, s32[1,1024]{1,0:T(1,128)S(1)} %bitcast.29, bf16[4096,1024]{1,0:T(8,128)(2,1)} %refs_2_.2, bf16[1024,1024]{1,0:T(8,128)(2,1)} %refs_3_.1), custom_call_target="tpu_custom_call" | custom-call | flops 6000000000 | bytes 16777216 | tf_op jit(solution)/shard_map/pick_pivot_rows/pallas_call | solution.py:110
  11.3 4.6 %constant_dynamic-slice_fusion.3 = bf16[2048,1024]{1,0:T(8,128)(2,1)} fusion(bf16[4096,1024]{1,0:T(8,128)(2,1)} %refs_2_.2, s32[]{:T(128)S(6)} %select_n.31), kind=kLoop, calls=%fused_computation.37 | loop fusion | bytes 8388612 | tf_op jit(solution)/shard_map/dynamic_slice | solution.py:277
  16.4 1.1 slice_add_fusion.1
  17.5 2.6 %collective-permute-start.3 = (f32[2,28,16,128]{3,2,1,0:T(8,128)S(1)}, f32[2,28,16,128]{3,2,1,0:T(8,128)S(1)}, u32[]{:S(2)}, u32[]{:S(2)}) collective-permute-start(f32[2,28,16,128]{3,2,1,0:T(8,128)S(1)} %slice_add_fusion.1), channel_id=1, source_target_pairs={{0,2},{1,5},{2,0},{3,7},{4,6},{5,1},{6,4},{7,3},{8,10},{9,13},{10,... | collective-permute-start | bytes 1376264 | tf_op jit(solution)/shard_map/ppermute | solution.py:252
  20.1 1.2 %slice_add_fusion = f32[2,20,32,128]{3,2,1,0:T(8,128)S(1)} fusion(f32[4,20,32,128]{3,2,1,0:T(8,128)} %collective-permute-done.10, f32[4,20,32,128]{3,2,1,0:T(8,128)S(1)} %get-tuple-element.12), kind=kLoop, calls=%fused_computation.1 | loop fusion | flops 163840 | bytes 1966080 | tf_op jit(solution)/shard_map/add | solution.py:282
  21.4 5.2 %collective-permute-done.3 = f32[2,28,16,128]{3,2,1,0:T(8,128)S(1)} collective-permute-done((f32[2,28,16,128]{3,2,1,0:T(8,128)S(1)}, f32[2,28,16,128]{3,2,1,0:T(8,128)S(1)}, u32[]{:S(2)}, u32[]{:S(2)}) %collective-permute-start.3) | collective-permute-done | bytes 458784 | tf_op jit(solution)/shard_map/ppermute | solution.py:252
  27.5 2.1 %collective-permute-start.4 = (f32[1,28,16,128]{3,2,1,0:T(8,128)S(1)}, f32[1,28,16,128]{3,2,1,0:T(8,128)S(1)}, u32[]{:S(2)}, u32[]{:S(2)}) collective-permute-start(f32[1,28,16,128]{3,2,1,0:T(8,128)S(1)} %slice_add_fusion.6), channel_id=1, source_target_pairs={{0,4},{1,3},{2,6},{3,1},{4,0},{5,7},{6,2},{7,5},{8,12},{9,11},{10,... | collective-permute-start | bytes 688136 | tf_op jit(solution)/shard_map/ppermute | solution.py:252
  29.7 6.1 %collective-permute-done.4 = f32[1,28,16,128]{3,2,1,0:T(8,128)S(1)} collective-permute-done((f32[1,28,16,128]{3,2,1,0:T(8,128)S(1)}, f32[1,28,16,128]{3,2,1,0:T(8,128)S(1)}, u32[]{:S(2)}, u32[]{:S(2)}) %collective-permute-start.4) | collective-permute-done | bytes 229408 | tf_op jit(solution)/shard_map/ppermute | solution.py:252
  35.8 1.0 fusion.3
  36.8 1.9 %collective-permute-start.5 = (f32[1,28,16,128]{3,2,1,0:T(8,128)S(1)}, f32[1,28,16,128]{3,2,1,0:T(8,128)S(1)}, u32[]{:S(2)}, u32[]{:S(2)}) collective-permute-start(f32[1,28,16,128]{3,2,1,0:T(8,128)S(1)} %fusion.3), channel_id=1, source_target_pairs={{0,8},{1,17},{2,10},{3,19},{4,12},{5,21},{6,14},{7,23},{8,0},{9,25... | collective-permute-start | bytes 688136 | tf_op jit(solution)/shard_map/ppermute | solution.py:252
  38.7 1.0 fusion
  39.7 1.6 %collective-permute-start.12 = (f32[20,32,128]{2,1,0:T(8,128)S(1)}, f32[20,32,128]{2,1,0:T(8,128)S(1)}, u32[]{:S(2)}, u32[]{:S(2)}) collective-permute-start(f32[20,32,128]{2,1,0:T(8,128)S(1)} %fusion), channel_id=1, source_target_pairs={{0,4},{1,3},{2,6},{3,1},{4,0},{5,7},{6,2},{7,5},{8,12},{9,11},{10,... | collective-permute-start | bytes 983048 | tf_op jit(solution)/shard_map/ppermute | solution.py:252
  41.3 2.9 %collective-permute-done.5 = f32[1,28,16,128]{3,2,1,0:T(8,128)S(1)} collective-permute-done((f32[1,28,16,128]{3,2,1,0:T(8,128)S(1)}, f32[1,28,16,128]{3,2,1,0:T(8,128)S(1)}, u32[]{:S(2)}, u32[]{:S(2)}) %collective-permute-start.5) | collective-permute-done | bytes 229408 | tf_op jit(solution)/shard_map/ppermute | solution.py:252
  44.2 3.0 %collective-permute-start.6 = (f32[1,28,16,128]{3,2,1,0:T(8,128)S(1)}, f32[1,28,16,128]{3,2,1,0:T(8,128)S(1)}, u32[]{:S(2)}, u32[]{:S(2)}) collective-permute-start(f32[1,28,16,128]{3,2,1,0:T(8,128)S(1)} %add.92), channel_id=1, source_target_pairs={{0,16},{1,9},{2,18},{3,11},{4,20},{5,13},{6,22},{7,15},{8,24},{9,1... | collective-permute-start | bytes 688136 | tf_op jit(solution)/shard_map/ppermute | solution.py:252
  47.3 4.6 %collective-permute-done.6 = f32[1,28,16,128]{3,2,1,0:T(8,128)S(1)} collective-permute-done((f32[1,28,16,128]{3,2,1,0:T(8,128)S(1)}, f32[1,28,16,128]{3,2,1,0:T(8,128)S(1)}, u32[]{:S(2)}, u32[]{:S(2)}) %collective-permute-start.6) | collective-permute-done | bytes 229408 | tf_op jit(solution)/shard_map/ppermute | solution.py:252
  51.9 1.6 %collective-permute-start.7 = (f32[1,28,16,128]{3,2,1,0:T(8,128)S(1)}, f32[1,28,16,128]{3,2,1,0:T(8,128)S(1)}, u32[]{:S(2)}, u32[]{:S(2)}) collective-permute-start(f32[1,28,16,128]{3,2,1,0:T(8,128)S(1)} %add.93.refs_3_), channel_id=1, source_target_pairs={{0,4},{1,3},{2,6},{3,1},{4,0},{5,7},{6,2},{7,5},{8,12},{9,11},{10,... | collective-permute-start | bytes 688136 | tf_op jit(solution)/shard_map/ppermute | solution.py:252
  53.5 1.1 fusion.2
  55.0 2.5 %collective-permute-start.13 = (f32[2,8,32,128]{3,1,2,0:T(8,128)S(1)}, f32[2,8,32,128]{3,1,2,0:T(8,128)S(1)}, u32[]{:S(2)}, u32[]{:S(2)}) collective-permute-start(f32[2,8,32,128]{3,1,2,0:T(8,128)S(1)} %bitcast.32), channel_id=1, source_target_pairs={{0,16},{1,17},{2,18},{3,19},{4,20},{5,21},{6,22},{7,23},{8,24},{9,... | collective-permute-start | bytes 786440 | tf_op jit(solution)/shard_map/ppermute | solution.py:252
  58.0 1.5 %collective-permute-start.8 = (f32[2,28,16,128]{3,2,1,0:T(8,128)S(1)}, f32[2,28,16,128]{3,2,1,0:T(8,128)S(1)}, u32[]{:S(2)}, u32[]{:S(2)}) collective-permute-start(f32[2,28,16,128]{3,2,1,0:T(8,128)S(1)} %pad_maximum_fusion.2), channel_id=1, source_target_pairs={{0,2},{1,5},{2,0},{3,7},{4,6},{5,1},{6,4},{7,3},{8,10},{9,13},{10,... | collective-permute-start | bytes 1376264 | tf_op jit(solution)/shard_map/ppermute | solution.py:252
  59.6 9.4 %collective-permute-done.13 = f32[2,8,32,128]{3,1,2,0:T(8,128)S(1)} collective-permute-done((f32[2,8,32,128]{3,1,2,0:T(8,128)S(1)}, f32[2,8,32,128]{3,1,2,0:T(8,128)S(1)}, u32[]{:S(2)}, u32[]{:S(2)}) %collective-permute-start.13) | collective-permute-done | bytes 262176 | tf_op jit(solution)/shard_map/ppermute | solution.py:252
  69.4 5.2 %collective-permute-done.14 = f32[1,8,32,128]{3,1,2,0:T(8,128)S(1)} collective-permute-done((f32[1,8,32,128]{3,1,2,0:T(8,128)S(1)}, f32[1,8,32,128]{3,1,2,0:T(8,128)S(1)}, u32[]{:S(2)}, u32[]{:S(2)}) %collective-permute-start.14) | collective-permute-done | bytes 131104 | tf_op jit(solution)/shard_map/ppermute | solution.py:252
  74.7 13.5 %sketch_rows.1.refs_1_ = f32[2048,1024]{1,0:T(8,128)S(1)} custom-call(s32[2]{0:T(128)S(1)} %pad_add_fusion.meta.refs_0_, bf16[4096,1024]{1,0:T(8,128)(2,1)} %refs_2_.2, bf16[2048,1024]{1,0:T(8,128)(2,1)} %collective-permute-done.theirs, bf16[1024,1024]{1,0:T(8,128)(2,1)} %refs_3_.1, bf16[1024,1024]{1,0:T(8,128)(2,1)} %collective-permute-done.1.gauss_theirs), custom_call_target="tpu_custom_call" | custom-call | flops 8589934592 | bytes 20971520 | tf_op jit(solution)/shard_map/sketch_rows/pallas_call | solution.py:138
  88.2 3.2 %copy-done.2 = f32[2048,1024]{1,0:T(8,128)} copy-done((f32[2048,1024]{1,0:T(8,128)}, f32[2048,1024]{1,0:T(8,128)S(1)}, u32[]{:S(2)}) %copy-start.2) | copy-done | bytes 8388632
  91.5 21.3 %blocked_solve.1 = (f32[2048,1024]{1,0:T(8,128)}, f32[32,1024]{1,0:T(8,128)S(1)}) custom-call(s32[2]{0:T(128)S(1)} %pad_add_fusion.meta.refs_0_, f32[2048,1024]{1,0:T(8,128)} %copy-done.2, f32[8,128,128]{2,1,0:T(8,128)S(1)} %copy-done, f32[1,28,16,128]{3,2,1,0:T(8,128)S(1)} %add.93.refs_3_, f32[1,28,16,128]{3,2,1,0:T(8,128)S(1)} %collective-permute-done.7.refs_4_, ...), custom_call_target="tpu_custom_call" | custom-call | flops 8000000000 | bytes 20971520 | tf_op jit(solution)/shard_map/blocked_solve/pallas_call | solution.py:216
  (42 shorter events, 5.0 us)
Async XLA Ops:
  0.7 0.7 copy-start.1
  10.7 5.7 %collective-permute-start.2 = (f32[4,28,16,128]{3,2,1,0:T(8,128)S(1)}, f32[4,28,16,128]{3,2,1,0:T(8,128)}, u32[]{:S(2)}, u32[]{:S(2)}) collective-permute-start(f32[4,28,16,128]{3,2,1,0:T(8,128)S(1)} %get-tuple-element.9), channel_id=1, source_target_pairs={{0,1},{1,0},{2,3},{3,2},{4,5},{5,4},{6,7},{7,6},{8,9},{9,8},{10,11... | collective-permute-start | bytes 2752520 | tf_op jit(solution)/shard_map/ppermute | solution.py:255
  11.2 8.9 %collective-permute-start.10 = (f32[4,20,32,128]{3,2,1,0:T(8,128)}, f32[4,20,32,128]{3,2,1,0:T(8,128)}, u32[]{:S(2)}, u32[]{:S(2)}) collective-permute-start(f32[4,20,32,128]{3,2,1,0:T(8,128)} %get-tuple-element.13), channel_id=1, source_target_pairs={{0,1},{1,0},{2,3},{3,2},{4,5},{5,4},{6,7},{7,6},{8,9},{9,8},{10,11... | collective-permute-start | bytes 3932168 | tf_op jit(solution)/shard_map/ppermute | solution.py:255
  15.9 58.8 %collective-permute-start = (bf16[2048,1024]{1,0:T(8,128)(2,1)}, bf16[2048,1024]{1,0:T(8,128)(2,1)}, u32[]{:S(2)}, u32[]{:S(2)}) collective-permute-start(bf16[2048,1024]{1,0:T(8,128)(2,1)} %constant_dynamic-slice_fusion.3), channel_id=1, source_target_pairs={{0,1},{1,0},{2,3},{3,2},{4,5},{5,4},{6,7},{7,6},{8,9},{9,8},{10,11... | collective-permute-start | bytes 12582920 | tf_op jit(solution)/shard_map/ppermute | solution.py:255
  17.5 9.1 %collective-permute-start.3 = (f32[2,28,16,128]{3,2,1,0:T(8,128)S(1)}, f32[2,28,16,128]{3,2,1,0:T(8,128)S(1)}, u32[]{:S(2)}, u32[]{:S(2)}) collective-permute-start(f32[2,28,16,128]{3,2,1,0:T(8,128)S(1)} %slice_add_fusion.1), channel_id=1, source_target_pairs={{0,2},{1,5},{2,0},{3,7},{4,6},{5,1},{6,4},{7,3},{8,10},{9,13},{10,... | collective-permute-start | bytes 1376264 | tf_op jit(solution)/shard_map/ppermute | solution.py:252
  21.3 17.4 %collective-permute-start.11 = (f32[2,20,32,128]{3,2,1,0:T(8,128)S(1)}, f32[2,20,32,128]{3,2,1,0:T(8,128)S(1)}, u32[]{:S(2)}, u32[]{:S(2)}) collective-permute-start(f32[2,20,32,128]{3,2,1,0:T(8,128)S(1)} %slice_add_fusion), channel_id=1, source_target_pairs={{0,2},{1,5},{2,0},{3,7},{4,6},{5,1},{6,4},{7,3},{8,10},{9,13},{10,... | collective-permute-start | bytes 1966088 | tf_op jit(solution)/shard_map/ppermute | solution.py:252
  27.5 8.3 %collective-permute-start.4 = (f32[1,28,16,128]{3,2,1,0:T(8,128)S(1)}, f32[1,28,16,128]{3,2,1,0:T(8,128)S(1)}, u32[]{:S(2)}, u32[]{:S(2)}) collective-permute-start(f32[1,28,16,128]{3,2,1,0:T(8,128)S(1)} %slice_add_fusion.6), channel_id=1, source_target_pairs={{0,4},{1,3},{2,6},{3,1},{4,0},{5,7},{6,2},{7,5},{8,12},{9,11},{10,... | collective-permute-start | bytes 688136 | tf_op jit(solution)/shard_map/ppermute | solution.py:252
  36.8 7.4 %collective-permute-start.5 = (f32[1,28,16,128]{3,2,1,0:T(8,128)S(1)}, f32[1,28,16,128]{3,2,1,0:T(8,128)S(1)}, u32[]{:S(2)}, u32[]{:S(2)}) collective-permute-start(f32[1,28,16,128]{3,2,1,0:T(8,128)S(1)} %fusion.3), channel_id=1, source_target_pairs={{0,8},{1,17},{2,10},{3,19},{4,12},{5,21},{6,14},{7,23},{8,0},{9,25... | collective-permute-start | bytes 688136 | tf_op jit(solution)/shard_map/ppermute | solution.py:252
  39.7 14.9 %copy-start.3 = (pred[8]{0:T(512)(128)(4,1)S(1)}, pred[8]{0:T(512)(128)(4,1)}, u32[]{:S(2)}) copy-start(pred[8]{0:T(512)(128)(4,1)} %constant.64.clone.1) | copy-start | bytes 28
  39.7 13.7 %collective-permute-start.12 = (f32[20,32,128]{2,1,0:T(8,128)S(1)}, f32[20,32,128]{2,1,0:T(8,128)S(1)}, u32[]{:S(2)}, u32[]{:S(2)}) collective-permute-start(f32[20,32,128]{2,1,0:T(8,128)S(1)} %fusion), channel_id=1, source_target_pairs={{0,4},{1,3},{2,6},{3,1},{4,0},{5,7},{6,2},{7,5},{8,12},{9,11},{10,... | collective-permute-start | bytes 983048 | tf_op jit(solution)/shard_map/ppermute | solution.py:252
  44.2 7.6 %collective-permute-start.6 = (f32[1,28,16,128]{3,2,1,0:T(8,128)S(1)}, f32[1,28,16,128]{3,2,1,0:T(8,128)S(1)}, u32[]{:S(2)}, u32[]{:S(2)}) collective-permute-start(f32[1,28,16,128]{3,2,1,0:T(8,128)S(1)} %add.92), channel_id=1, source_target_pairs={{0,16},{1,9},{2,18},{3,11},{4,20},{5,13},{6,22},{7,15},{8,24},{9,1... | collective-permute-start | bytes 688136 | tf_op jit(solution)/shard_map/ppermute | solution.py:252
  47.2 27.5 %collective-permute-start.1 = (bf16[1024,1024]{1,0:T(8,128)(2,1)}, bf16[1024,1024]{1,0:T(8,128)(2,1)}, u32[]{:S(2)}, u32[]{:S(2)}) collective-permute-start(bf16[1024,1024]{1,0:T(8,128)(2,1)} %refs_3_.1), channel_id=1, source_target_pairs={{0,1},{1,0},{2,3},{3,2},{4,5},{5,4},{6,7},{7,6},{8,9},{9,8},{10,11... | collective-permute-start | bytes 6291464 | tf_op jit(solution)/shard_map/ppermute | solution.py:255
  51.9 6.1 %collective-permute-start.7 = (f32[1,28,16,128]{3,2,1,0:T(8,128)S(1)}, f32[1,28,16,128]{3,2,1,0:T(8,128)S(1)}, u32[]{:S(2)}, u32[]{:S(2)}) collective-permute-start(f32[1,28,16,128]{3,2,1,0:T(8,128)S(1)} %add.93.refs_3_), channel_id=1, source_target_pairs={{0,4},{1,3},{2,6},{3,1},{4,0},{5,7},{6,2},{7,5},{8,12},{9,11},{10,... | collective-permute-start | bytes 688136 | tf_op jit(solution)/shard_map/ppermute | solution.py:252
  55.0 14.0 %collective-permute-start.13 = (f32[2,8,32,128]{3,1,2,0:T(8,128)S(1)}, f32[2,8,32,128]{3,1,2,0:T(8,128)S(1)}, u32[]{:S(2)}, u32[]{:S(2)}) collective-permute-start(f32[2,8,32,128]{3,1,2,0:T(8,128)S(1)} %bitcast.32), channel_id=1, source_target_pairs={{0,16},{1,17},{2,18},{3,19},{4,20},{5,21},{6,22},{7,23},{8,24},{9,... | collective-permute-start | bytes 786440 | tf_op jit(solution)/shard_map/ppermute | solution.py:252
  58.0 11.3 %collective-permute-start.8 = (f32[2,28,16,128]{3,2,1,0:T(8,128)S(1)}, f32[2,28,16,128]{3,2,1,0:T(8,128)S(1)}, u32[]{:S(2)}, u32[]{:S(2)}) collective-permute-start(f32[2,28,16,128]{3,2,1,0:T(8,128)S(1)} %pad_maximum_fusion.2), channel_id=1, source_target_pairs={{0,2},{1,5},{2,0},{3,7},{4,6},{5,1},{6,4},{7,3},{8,10},{9,13},{10,... | collective-permute-start | bytes 1376264 | tf_op jit(solution)/shard_map/ppermute | solution.py:252
  69.2 5.5 %collective-permute-start.14 = (f32[1,8,32,128]{3,1,2,0:T(8,128)S(1)}, f32[1,8,32,128]{3,1,2,0:T(8,128)S(1)}, u32[]{:S(2)}, u32[]{:S(2)}) collective-permute-start(f32[1,8,32,128]{3,1,2,0:T(8,128)S(1)} %constant_dynamic-slice_fusion), channel_id=1, source_target_pairs={{0,8},{1,9},{2,10},{3,11},{4,12},{5,13},{6,14},{7,15},{8,0},{9,1},... | collective-permute-start | bytes 393224 | tf_op jit(solution)/shard_map/ppermute | solution.py:252
  69.3 22.1 %collective-permute-start.9 = (f32[4,28,16,128]{3,2,1,0:T(8,128)S(1)}, f32[4,28,16,128]{3,2,1,0:T(8,128)S(1)}, u32[]{:S(2)}, u32[]{:S(2)}) collective-permute-start(f32[4,28,16,128]{3,2,1,0:T(8,128)S(1)} %pad_maximum_fusion), channel_id=1, source_target_pairs={{0,1},{1,0},{2,3},{3,2},{4,5},{5,4},{6,7},{7,6},{8,9},{9,8},{10,11... | collective-permute-start | bytes 2752520 | tf_op jit(solution)/shard_map/ppermute | solution.py:255
  74.7 16.8 %copy-start = (f32[8,128,128]{2,1,0:T(8,128)S(1)}, f32[8,128,128]{2,1,0:T(8,128)}, u32[]{:S(2)}) copy-start(f32[8,128,128]{2,1,0:T(8,128)} %refs_2_.3) | copy-start | bytes 1572868
  88.2 3.3 %copy-start.2 = (f32[2048,1024]{1,0:T(8,128)}, f32[2048,1024]{1,0:T(8,128)S(1)}, u32[]{:S(2)}) copy-start(f32[2048,1024]{1,0:T(8,128)S(1)} %sketch_rows.1.refs_1_) | copy-start | bytes 25165828

commit v2 on v0

v2 whole, which is shorter than its diff:
```python
import jax
import jax.numpy as jnp
from jax import lax
from jax.experimental import pallas as pl
from jax.experimental.pallas import tpu as pltpu
from jax.sharding import PartitionSpec as P

K = 1024
BLK = 128
NBLK = K // BLK
WIDE = 2 * BLK
NWIDE = K // WIDE
SHARD_ROWS = 2048
PIV_MOST = 128
PICKS = 2 * PIV_MOST
SUB = 16
UPPER = [(i, j) for i in range(NBLK) for j in range(i + 1, NBLK)]
F32 = jnp.float32
BF16 = jnp.bfloat16
I16 = jnp.int16
I32 = jnp.int32
MIB = 1 << 20
VMEM = pl.BlockSpec(memory_space=pltpu.VMEM)
SMEM = pl.BlockSpec(memory_space=pltpu.SMEM)
HBM = pl.BlockSpec(memory_space=pltpu.HBM)


def dot(a, b, dims=((1,), (0,))):
    return lax.dot_general(a, b, (dims, ((), ())), preferred_element_type=F32)


def split(a):
    high = a.astype(BF16)
    return high, (a - high.astype(F32)).astype(BF16)


def product(a, b):
    (ah, al), (bh, bl) = split(a), split(b)
    return dot(ah, bh) + (dot(al, bh) + dot(ah, bl))


def quarter_slot(gx, gy, x, y, c):
    dx, dy = gx ^ x, gy ^ y
    return jnp.where(c == 0, dx * 2 + dy, dy * 2 + dx)


class Copies:
    def __init__(self, source, target, sems):
        count = sems.shape[0]
        rows = target.shape[0] // count
        self.parts = [
            pltpu.make_async_copy(source.at[pl.ds(t * rows, rows)], target.at[pl.ds(t * rows, rows)], sems.at[t])
            for t in range(count)
        ]

    def start(self):
        for part in self.parts:
            part.start()

    def wait(self):
        for part in self.parts:
            part.wait()


def lower_layout(share):
    tops = K // (8 * share)
    return [-(-((z + 1) * 8 * share) // BLK) for z in range(tops)]


def by_core(row, share):
    count = row.shape[1] // (2 * share)
    return jnp.concatenate(
        [row[:, (2 * k + core) * share:(2 * k + core + 1) * share] for core in range(2) for k in range(count)], axis=1)


def pick_kernel(share, meta, piv, slab, packed, place, away, sem):
    r, c = meta[0], meta[1]
    part = SHARD_ROWS // 8
    copies = [
        pltpu.make_async_copy(
            slab.at[pl.ds(pl.multiple_of((1 - c) * SHARD_ROWS + t * part, part), part)],
            away.at[pl.ds(t * part, part)], sem.at[t])
        for t in range(8)
    ]
    for copy in copies:
        copy.start()
    half = lax.broadcasted_iota(I32, (8, K), 0)
    local = by_core(piv[...], share) - (r * (2 * SHARD_ROWS) + half * SHARD_ROWS)
    inside = (local >= 0) & (local < SHARD_ROWS) & (half < 2)
    earlier = lax.broadcasted_iota(I32, (K, K), 0) < lax.broadcasted_iota(I32, (K, K), 1)
    rank = dot(jnp.where(inside, 1.0, 0.0).astype(BF16), jnp.where(earlier, 1.0, 0.0).astype(BF16))
    rank = jnp.where(inside, rank, -1.0)
    order = lax.broadcasted_iota(I32, (PIV_MOST, K), 0).astype(F32)
    rows = lax.broadcasted_iota(I32, (PIV_MOST, SHARD_ROWS), 1).astype(F32)
    for b in range(2):
        hit = rank[b:b + 1, :] == order
        one = jnp.where(hit, 1.0, 0.0).astype(BF16)
        for core in range(2):
            place[core, pl.ds(b * PIV_MOST, PIV_MOST), :] = one[:, core * (K // 2):(core + 1) * (K // 2)]
        row = jnp.sum(jnp.where(hit, local[b:b + 1, :].astype(F32), 0.0), axis=1, keepdims=True)
        part = dot(jnp.where(rows == row, 1.0, 0.0).astype(BF16), slab[pl.ds(b * SHARD_ROWS, SHARD_ROWS), :])
        packed[pl.ds(b * PIV_MOST, PIV_MOST), :] = part.astype(BF16)
    for copy in copies:
        copy.wait()


def pick(meta, piv, slab, share):
    depth = slab.shape[1]
    return pl.pallas_call(
        lambda *refs: pick_kernel(share, *refs),
        out_shape=(
            jax.ShapeDtypeStruct((PICKS, depth), BF16),
            jax.ShapeDtypeStruct((2, PICKS, K // 2), BF16),
            jax.ShapeDtypeStruct((SHARD_ROWS, depth), BF16),
        ),
        in_specs=[SMEM, VMEM, VMEM],
        out_specs=(VMEM, VMEM, HBM),
        scratch_shapes=[pltpu.SemaphoreType.DMA((8,))],
        compiler_params=pltpu.CompilerParams(vmem_limit_bytes=28 * MIB),
        cost_estimate=pl.CostEstimate(flops=4 * 10**9, bytes_accessed=14 * MIB, transcendentals=0),
        name="pick_pivot_rows",
    )(meta, piv, slab)


def pivot_kernel(share, meta, place, packed, packed_theirs, gauss, gauss_theirs,
                 u_keep, u_send, l_keep, l_send, code_v, power_v, u_scr, l_scr):
    r, c = meta[0], meta[1]
    x, y = r & 1, (r >> 1) & 1
    spread = [dot(place[c], p[...], ((0,), (0,))).astype(BF16) for p in (packed, packed_theirs)]
    rows = dot(spread[0], gauss[...]) + dot(spread[1], gauss_theirs[...])
    lane = lax.broadcasted_iota(I32, (K // 2, BLK), 1)
    powers = jnp.zeros((K // 2, BLK), F32)
    for j in range(NBLK):
        part = rows[:, j * BLK:(j + 1) * BLK]
        most = jnp.max(jnp.abs(part), axis=1, keepdims=True)
        power = jnp.where(most > 0.0, jnp.ceil(jnp.log2(jnp.maximum(most, 1e-30)) + 0.001), 0.0)
        code = jnp.floor(part * jnp.exp2(15.0 - power) + 0.5)
        code = jnp.clip(code, -32767.0, 32767.0)
        code_v[:, pl.ds(j * BLK, BLK)] = code.astype(I32).astype(I16)
        powers = jnp.where(lane == j, power, powers)
    power_v[...] = powers

    columns = lower_layout(share)
    lane = lax.broadcasted_iota(I32, (SUB, BLK), 1)
    lane_l = lax.broadcasted_iota(I32, (share, BLK), 1)
    for quarter in range(4):
        gy, gx = quarter >> 1, quarter & 1
        slot = quarter_slot(gx, gy, x, y, c)
        tail = jnp.zeros((SUB, BLK), F32)
        for n, (i, j) in enumerate(UPPER):
            at = pl.ds(i * (BLK // 2) + quarter * SUB, SUB)
            u_scr[slot, n] = code_v[at, pl.ds(j * BLK, BLK)]
            tail = jnp.where(lane == n, power_v[at, j:j + 1], tail)
        u_scr[slot, len(UPPER)] = tail.astype(I32).astype(I16)
        n = 0
        tail = jnp.zeros((share, BLK), F32)
        for z, count in enumerate(columns):
            at = pl.ds((z * 4 + quarter) * share, share)
            for j in range(count):
                l_scr[slot, n] = code_v[at, pl.ds(j * BLK, BLK)].astype(l_scr.dtype)
                tail = jnp.where(lane_l == z * NBLK + j, power_v[at, j:j + 1], tail)
                n += 1
        l_scr[slot, n] = tail.astype(I32).astype(l_scr.dtype)
    u_keep[...] = u_scr[0:2]
    u_send[...] = u_scr[2:4]
    l_keep[...] = l_scr[0:2]
    l_send[...] = l_scr[2:4]


def pivot_rows(meta, place, packed, packed_theirs, gauss, gauss_theirs, share):
    units = sum(lower_layout(share)) + 1
    u_shape = (len(UPPER) + 1, SUB, BLK)
    l_shape = (units, share, BLK)
    l_type = I16 if share % SUB == 0 else I32
    u_out = jax.ShapeDtypeStruct((2,) + u_shape, I16)
    l_out = jax.ShapeDtypeStruct((2,) + l_shape, l_type)
    return pl.pallas_call(
        lambda *refs: pivot_kernel(share, *refs),
        out_shape=(u_out, u_out, l_out, l_out),
        in_specs=[SMEM] + [VMEM] * 5,
        out_specs=(VMEM,) * 4,
        scratch_shapes=[
            pltpu.VMEM((K // 2, K), I16),
            pltpu.VMEM((K // 2, BLK), F32),
            pltpu.VMEM((4,) + u_shape, I16),
            pltpu.VMEM((4,) + l_shape, l_type),
        ],
        compiler_params=pltpu.CompilerParams(vmem_limit_bytes=32 * MIB),
        cost_estimate=pl.CostEstimate(flops=3 * 10**9, bytes_accessed=8 * MIB, transcendentals=0),
        name="pivot_rows",
    )(meta, place, packed, packed_theirs, gauss, gauss_theirs)


def sketch_kernel(part, meta, slab, theirs, gauss, gauss_theirs, later, out, mark, theirs_v, sems):
    rows = out.shape[0]
    tile = theirs_v.shape[1]
    steps = rows // tile
    here = [part * rows + t * tile for t in range(steps)]
    loads = [Copies(theirs.at[pl.ds(here[t], tile)], theirs_v.at[t], sems.at[t]) for t in range(steps)]
    for copy in loads:
        copy.start()
    mark[...] = jnp.zeros_like(mark)
    for t in range(steps):
        mine = pl.ds(pl.multiple_of(meta[1] * theirs.shape[0] + here[t], tile), tile)
        total = dot(slab[mine, :], gauss[...])
        loads[t].wait()
        high, low = split(total + dot(theirs_v[t], gauss_theirs[...]))
        for s in range(NWIDE):
            cols = slice(s * WIDE, (s + 1) * WIDE)
            out[pl.ds(t * tile, tile), pl.ds(2 * s * WIDE, WIDE)] = high[:, cols]
            out[pl.ds(t * tile, tile), pl.ds((2 * s + 1) * WIDE, WIDE)] = low[:, cols]


def sketch_rows(meta, slab, theirs, gauss, gauss_theirs, part, parts, later):
    rows, depth = theirs.shape
    tile = 512
    steps = rows // parts // tile
    return pl.pallas_call(
        lambda *refs: sketch_kernel(part, *refs),
        out_shape=(jax.ShapeDtypeStruct((rows // parts, 2 * K), BF16), jax.ShapeDtypeStruct((SUB, BLK), I16)),
        in_specs=[SMEM, VMEM, HBM, VMEM, VMEM, HBM],
        out_specs=(VMEM, VMEM),
        scratch_shapes=[pltpu.VMEM((steps, tile, depth), BF16), pltpu.SemaphoreType.DMA((steps, 4))],
        compiler_params=pltpu.CompilerParams(vmem_limit_bytes=32 * MIB),
        cost_estimate=pl.CostEstimate(
            flops=4 * rows * depth * K // parts, bytes_accessed=20 * MIB // parts, transcendentals=0),
        name="sketch_rows",
    )(meta, slab, theirs, gauss, gauss_theirs, later)


def store_three(weights, row, cols, value):
    high, low = split(value)
    weights[pl.ds(row, WIDE), cols] = high
    weights[pl.ds(row + WIDE, WIDE), cols] = high
    weights[pl.ds(row + 2 * WIDE, WIDE), cols] = low


def prepare(share, r, c, inverses, pieces, low, own_rows, coupling, weights):
    x, y = r & 1, (r >> 1) & 1
    lane = lax.broadcasted_iota(I32, (SUB, BLK), 1)
    coupling[...] = jnp.zeros_like(coupling)
    slot = 0
    chunk = min(SUB, share)
    for piece in pieces:
        for k in range(piece.shape[0]):
            gc = c ^ (slot >> 2)
            high, less = (slot >> 1) & 1, slot & 1
            dx, dy = jnp.where(gc == 0, high, less), jnp.where(gc == 0, less, high)
            quarter = (y ^ dy) * 2 + (x ^ dx)
            tail = piece[k, len(UPPER)].astype(I32).astype(F32)
            for i in range(NBLK - 1):
                starts = []
                for part in range(SUB // chunk):
                    s = i * (BLK // 2) + quarter * SUB + part * chunk
                    owner = lax.div(s, share)
                    starts.append(pl.multiple_of((owner * 2 + gc) * share + (s - owner * share), 8))
                for n, (row_block, j) in enumerate(UPPER):
                    if row_block != i:
                        continue
                    scale = jnp.exp2(tail[:, n:n + 1] - 15.0) * (-1.0 / K**0.5)
                    value = piece[k, n].astype(I32).astype(F32) * scale
                    for part in range(SUB // chunk):
                        coupling[pl.ds(starts[part], chunk), pl.ds(j * BLK, BLK)] = (
                            value[part * chunk:(part + 1) * chunk])
            slot += 1

    own = (r * 2 + c) * share
    up = coupling[pl.ds(pl.multiple_of(own, 8), share), :] * (-(K**0.5))
    tail = low[NBLK].astype(I32)
    place = lax.broadcasted_iota(I32, (share, BLK), 1) - (r >> 2) * NBLK
    diagonal = lax.div(own, BLK)
    for j in range(NBLK):
        power = jnp.sum(jnp.where(place == j, tail, 0), axis=1, keepdims=True).astype(F32)
        value = low[j].astype(I32).astype(F32) * jnp.exp2(power - 15.0)
        cols = pl.ds(j * BLK, BLK)
        own_rows[:, cols] = jnp.where(j > diagonal, up[:, j * BLK:(j + 1) * BLK], value)

    for s in range(NWIDE):
        first, second = inverses[2 * s], inverses[2 * s + 1]
        link = coupling[pl.ds(2 * s * BLK, BLK), pl.ds((2 * s + 1) * BLK, BLK)]
        corner = product(first, product(link, second))
        block = jnp.concatenate([
            jnp.concatenate([first, corner], axis=1),
            jnp.concatenate([jnp.zeros_like(first), second], axis=1)], axis=0)
        cols = pl.ds(s * WIDE, WIDE)
        store_three(weights, 0, cols, block)
        if s > 0:
            turned = product(coupling[pl.ds(0, s * WIDE), cols], block)
            for e in range(s):
                store_three(weights, 3 * (e + 1) * WIDE, cols, turned[e * WIDE:(e + 1) * WIDE])


def solve_kernel(share, parts, meta, *refs):
    sketches, refs = refs[:parts], refs[parts:]
    (inverses, p0, p1, p2, p3, low, out, own_rows,
     coupling, weights, earlier, pair_v, out_v, in_sems, out_sems) = refs
    tile = out_v.shape[1]
    each = sketches[0].shape[0] // tile
    steps = each * parts

    def start_in(step):
        slot = lax.rem(step, 2)
        for part in range(parts):
            @pl.when(lax.div(step, each) == part)
            def _():
                where = pl.ds(pl.multiple_of((step - part * each) * tile, tile), tile)
                pltpu.make_async_copy(sketches[part].at[where], pair_v.at[slot], in_sems.at[slot]).start()

    def copy_out(step):
        slot = lax.rem(step, 2)
        where = pl.ds(pl.multiple_of(step * tile, tile), tile)
        return pltpu.make_async_copy(out_v.at[slot], out.at[where], out_sems.at[slot])

    start_in(jnp.int32(0))
    start_in(jnp.int32(1))
    prepare(share, meta[0], meta[1], inverses, (p0, p1, p2, p3), low, own_rows, coupling, weights)
    sub = 256

    @pl.loop(0, steps)
    def _(step):
        slot = lax.rem(step, 2)

        @pl.when(step >= 2)
        def _():
            copy_out(step - 2).wait()

        pltpu.make_async_copy(sketches[0].at[pl.ds(0, tile)], pair_v.at[slot], in_sems.at[slot]).wait()
        for s in range(NWIDE):
            cols = pl.ds(s * WIDE, WIDE)
            for q in range(tile // sub):
                here = pl.ds(q * sub, sub)
                pair = pair_v[slot, here, pl.ds(2 * s * WIDE, 2 * WIDE)]
                high = pair_v[slot, here, pl.ds(2 * s * WIDE, WIDE)]
                acc = dot(pair, weights[pl.ds(0, 2 * WIDE), cols]) + dot(high, weights[pl.ds(2 * WIDE, WIDE), cols])
                if s > 0:
                    depth = 3 * s * WIDE
                    acc = acc + dot(earlier[here, pl.ds(0, depth)], weights[pl.ds(3 * WIDE, depth), cols])
                out_v[slot, here, cols] = acc
                if s < NWIDE - 1:
                    high, low_part = split(acc)
                    to = 3 * s * WIDE
                    earlier[here, pl.ds(to, WIDE)] = high
                    earlier[here, pl.ds(to + WIDE, WIDE)] = low_part
                    earlier[here, pl.ds(to + 2 * WIDE, WIDE)] = high
        copy_out(step).start()

        @pl.when(step + 2 < steps)
        def _():
            start_in(step + 2)

    for step in range(2):
        copy_out(jnp.int32(steps - 2 + step)).wait()


def solve(meta, sketches, inverses, pieces, low, share):
    parts = len(sketches)
    rows = sum(s.shape[0] for s in sketches)
    tile = 512
    return pl.pallas_call(
        lambda *refs: solve_kernel(share, parts, *refs),
        out_shape=(jax.ShapeDtypeStruct((rows, K), F32), jax.ShapeDtypeStruct((share, K), F32)),
        in_specs=[SMEM] + [HBM] * parts + [VMEM] * (2 + len(pieces)),
        out_specs=(HBM, VMEM),
        scratch_shapes=[
            pltpu.VMEM((K, K), F32),
            pltpu.VMEM((3 * K, K), BF16),
            pltpu.VMEM((tile, 3 * (NWIDE - 1) * WIDE), BF16),
            pltpu.VMEM((2, tile, 2 * K), BF16),
            pltpu.VMEM((2, tile, K), F32),
            pltpu.SemaphoreType.DMA((2,)),
            pltpu.SemaphoreType.DMA((2,)),
        ],
        compiler_params=pltpu.CompilerParams(vmem_limit_bytes=58 * MIB),
        cost_estimate=pl.CostEstimate(flops=8 * 10**9, bytes_accessed=20 * MIB, transcendentals=0),
        name="blocked_solve",
    )(meta, *sketches, inverses, *pieces, low)


def after(value, *others):
    return lax.optimization_barrier((value,) + others)[0]


def on_device(slab, gauss, pivots, block_inverses):
    rows = lax.axis_size("row")
    cols = lax.axis_size("col")
    bits = rows.bit_length() - 1
    tops = bits - 2
    share = K // (rows * cols)
    r, c = lax.axis_index("row"), lax.axis_index("col")
    meta = jnp.stack([r, c]).astype(I32)

    def swap(value, bit_of):
        perm = [(2 * i + k, 2 * (i ^ (1 << bit_of[k])) + k) for i in range(rows) for k in range(2)]
        return lax.ppermute(value, ("row", "col"), perm)

    def swap_cores(value):
        return lax.ppermute(value, "col", [(0, 1), (1, 0)])

    near, far = (0, 1), (1, 0)
    climb = [(2 + s, 2 + (s + 1) % tops) for s in range(tops)]

    gauss_theirs = swap_cores(gauss)
    packed, place, slab_away = pick(meta, pivots.reshape(1, K), slab, share)
    packed_theirs = swap_cores(packed + gauss_theirs[:1] * 0)
    slab_away, mark = lax.optimization_barrier((slab_away, packed_theirs[:SUB, :BLK]))
    slab_theirs = swap_cores(slab_away)
    u_keep, u_send, l_keep, l_send = pivot_rows(
        meta, place, packed, packed_theirs, gauss, gauss_theirs, share)


    parts = 2

    def sketch_part(part, later):
        return sketch_rows(meta, slab, slab_theirs, gauss, gauss_theirs, part, parts, later)

    size, l_shape = u_keep[0].size // BLK, l_keep.shape[1:]

    def join(upper, lower):
        count = upper.shape[0]
        return jnp.concatenate(
            [upper.reshape(count, -1, BLK), lower.astype(I16).reshape(count, -1, BLK)], axis=1)

    keep, send = join(u_keep, l_keep), join(u_send, l_send)
    sketch, mark = sketch_part(0, mark)
    sketches = [sketch]
    got = swap(send, near) + mark[:1]
    send = keep[1:2] + got[1:2]
    kept = keep[0:1] + got[0:1]
    sketch, mark = sketch_part(1, send)
    sketches.append(sketch)
    kept = kept + (swap(send, far) + mark[:1])
    total = kept[:, :size].reshape(u_keep[:1].shape)
    low = kept[0, size:].reshape(l_shape)
    spread, n = [], 0
    for count in lower_layout(share):
        block = jnp.pad(low[n:n + count], ((0, NBLK - count), (0, 0), (0, 0)))
        spread.append(jnp.concatenate([block, low[-1:]], axis=0))
        n += count
    spread = jnp.stack(spread)
    order = []
    for k in range(1 << tops):
        at = r >> 2
        for s in range(tops):
            if (k >> (tops - 1 - s)) & 1:
                at = at ^ jnp.where(c == 0, 1 << (climb[s][0] - 2), 1 << (climb[s][1] - 2))
        order.append(lax.dynamic_index_in_dim(spread, at, 0, keepdims=False))
    low = jnp.stack(order)
    for bit_of in climb:
        half = low.shape[0] // 2
        both = jnp.concatenate([total.reshape(size, BLK), low[half:].reshape(-1, BLK)], axis=0)
        got = swap(both, bit_of)
        total = total + got[:size].reshape(total.shape)
        low = low[:half] + got[size:].reshape(low[:half].shape)
    piece1 = swap(total, far)
    pair = jnp.concatenate([total, piece1], axis=0)
    piece2 = swap(pair, near)
    piece3 = swap_cores(jnp.concatenate([pair, piece2], axis=0))
    return solve(meta, sketches, block_inverses, (total, piece1, piece2, piece3), low[0], share)


def solution(mesh):
    return jax.shard_map(
        on_device,
        mesh=mesh,
        in_specs=(P("row", "col"), P("col", None), P(), P()),
        out_specs=(P(("row", "col"), None), P(("row", "col"), None)),
        check_vma=False,
    )
```

time: 309 us -> 85.8 us (0.28); the launches traced: 304 us -> 85.5 us
  waiting for transfers between devices: 167 us -> 21.5 us
  matrix products: 95.6 us -> 0 us
  Pallas kernels: 0 us -> 36.7 us
  starting transfers between devices: 0.08 us -> 17 us
  local copies, waits for them, and re-layouts: 22.7 us -> 7.69 us
  between operations: 14.4 us -> 1.08 us
    psum x1 -> x0, waiting for transfers between devices: 139 us -> none  [on_device(): pivot_block = lax.psum(picked, ('row', 'col'))]
    dot_general x16 -> x0, matrix products: 95.6 us -> none  [the longest x7 57.2 us: on_device(): jnp.dot(earlier, coupling, precision=lax.Precision.HIGHEST)]
    pallas_call x0 -> x5, Pallas kernels: none -> 36.7 us  [the longest x1 15 us: solve(): pl.pallas_call(lambda *refs: solve_kernel(share, parts, *refs), out_shape...]
    reduce_scatter x1 -> x0, waiting for transfers between devices: 28.4 us -> none  [on_device(): lax.psum_scatter(jnp.dot(slab, gauss, preferred_element_type=jnp.float32)...]
    ppermute x0 -> x10, waiting for transfers between devices: none -> 21.5 us  [the longest x6 18.5 us: swap(): return lax.ppermute(value, ('row', 'col'), perm)]
    ppermute x0 -> x10, starting transfers between devices: none -> 17 us  [the longest x6 16.1 us: swap(): return lax.ppermute(value, ('row', 'col'), perm)]
    gather x1 -> x0, local copies, waits for them, and re-layouts: 9.71 us -> none  [on_device(): picked = jnp.take(sketch, jnp.clip(local_rows, 0, shard_rows - 1), axis=0)]
    select_n x1 -> x0, other arithmetic: 4.31 us -> none  [on_device(): picked = jnp.where(present[:, None], picked, 0.0)]
  transfers between devices with their start and end apart: 2 -> 10, of which waited for: 2 -> 7; matrix products, arithmetic and copies ran while one was open for 1% -> 1% of each run, Pallas kernels for 0% -> 25%
where the time goes in v2:
time: 85.8 us; the launch traced here: 85.5 us
  Pallas kernels  36.7 us (43%)
  waiting for transfers between devices  21.5 us (25%)
  starting transfers between devices  17 us (20%)
  local copies, waits for them, and re-layouts  7.69 us (9%)
  other arithmetic  1.49 us (2%)
  between operations  1.08 us (1%)
    ppermute x6, waiting for transfers between devices, swap(): return lax.ppermute(value, ('row', 'col'), perm)  18.5 us
    ppermute x6, starting transfers between devices, swap(): return lax.ppermute(value, ('row', 'col'), perm)  16.1 us
    pallas_call x1, Pallas kernels, solve(): pl.pallas_call(lambda *refs: solve_kernel(share, parts, *refs), out_shape...  15 us
    pallas_call x2, Pallas kernels, sketch_rows(): pl.pallas_call(lambda *refs: sketch_kernel(part, *refs), out_shape=(jax.S...  13.5 us
    unnamed x26, local copies, waits for them, and re-layouts  7.57 us
    pallas_call x1, Pallas kernels, pivot_rows(): pl.pallas_call(lambda *refs: pivot_kernel(share, *refs), out_shape=(u_out...  5.55 us
    ppermute x4, waiting for transfers between devices, swap_cores(): return lax.ppermute(value, 'col', [(0, 1), (1, 0)])  3.01 us
    pallas_call x1, Pallas kernels, pick(): pl.pallas_call(lambda *refs: pick_kernel(share, *refs), out_shape=(jax.Sh...  2.62 us
  transfers between devices with their start and end apart: 10, of which 7 were waited for; matrix products, arithmetic and copies ran while one was open for 1% of the time, Pallas kernels for 25%

profile of v2, /device:TPU:0, one launch (start us, length us, event | category | flops | bytes accessed | tf_op | source)
XLA Modules:
  0.0 85.5 jit_solution(667477666968602007)
XLA Ops:
  1.2 3.4 %copy-done = bf16[4096,1024]{1,0:T(8,128)(2,1)S(1)} copy-done((bf16[4096,1024]{1,0:T(8,128)(2,1)S(1)}, bf16[4096,1024]{1,0:T(8,128)(2,1)}, u32[]{:S(2)}) %copy-start) | copy-done | bytes 8388632
  4.6 0.7 copy-done.6
  5.3 2.6 %pick_pivot_rows.1 = (bf16[256,1024]{1,0:T(8,128)(2,1)S(1)}, bf16[2,256,512]{2,1,0:T(8,128)(2,1)S(1)}, bf16[2048,1024]{1,0:T(8,128)(2,1)}) custom-call(s32[2]{0:T(128)S(1)} %pad_add_fusion.12.refs_0_, s32[1,1024]{1,0:T(1,128)S(1)} %bitcast.41, bf16[4096,1024]{1,0:T(8,128)(2,1)S(1)} %copy-done), custom_call_target="tpu_custom_call" | custom-call | flops 4000000000 | bytes 14680064 | tf_op jit(solution)/shard_map/pick_pivot_rows/pallas_call | solution.py:109
  8.1 1.9 %collective-permute-done.1.refs_3_ = bf16[256,1024]{1,0:T(8,128)(2,1)S(1)} collective-permute-done((bf16[256,1024]{1,0:T(8,128)(2,1)S(1)}, bf16[256,1024]{1,0:T(8,128)(2,1)S(1)}, u32[]{:S(2)}, u32[]{:S(2)}) %collective-permute-start.1) | collective-permute-done | bytes 524320 | tf_op jit(solution)/shard_map/ppermute | solution.py:397
  10.1 1.6 %copy-done.2 = bf16[1024,1024]{1,0:T(8,128)(2,1)S(1)} copy-done((bf16[1024,1024]{1,0:T(8,128)(2,1)S(1)}, bf16[1024,1024]{1,0:T(8,128)(2,1)}, u32[]{:S(2)}) %copy-start.2) | copy-done | bytes 2097176
  11.7 1.0 %copy-done.8 = bf16[2,256,512]{2,1,0:T(8,128)(2,1)S(1)} copy-done((bf16[2,256,512]{2,1,0:T(8,128)(2,1)S(1)}, bf16[2,256,512]{2,1,0:T(8,128)(2,1)}, u32[]{:S(2)}) %copy-start.8) | copy-done | bytes 524312
  12.8 5.5 %pivot_rows.1 = (s16[2,29,16,128]{3,2,1,0:T(8,128)(2,1)S(1)}, s16[2,29,16,128]{3,2,1,0:T(8,128)(2,1)S(1)}, s16[2,21,32,128]{3,2,1,0:T(8,128)(2,1)S(1)}, s16[2,21,32,128]{3,2,1,0:T(8,128)(2,1)S(1)}) custom-call(s32[2]{0:T(128)S(1)} %pad_add_fusion.12.refs_0_, bf16[2,256,512]{2,1,0:T(8,128)(2,1)S(1)} %copy-done.8, ...), custom_call_target="tpu_custom_call" | custom-call | flops 3000000000 | bytes 8388608 | tf_op jit(solution)/shard_map/pivot_rows/pallas_call | solution.py:177
  18.4 2.9 %collective-permute-start.3 = (s16[2,1136,128]{2,1,0:T(8,128)(2,1)S(1)}, s16[2,1136,128]{2,1,0:T(8,128)(2,1)S(1)}, u32[]{:S(2)}, u32[]{:S(2)}) collective-permute-start(s16[2,1136,128]{2,1,0:T(8,128)(2,1)S(1)} %pad_add_fusion), channel_id=1, source_target_pairs={{0,2},{1,5},{2,0},{3,7},{4,6},{5,1},{6,4},{7,3},{8,10},{9,13},{10,... | collective-permute-start | bytes 1744904 | tf_op jit(solution)/shard_map/ppermute | solution.py:394
  21.3 6.7 %sketch_rows.2 = (bf16[1024,2048]{1,0:T(8,128)(2,1)S(1)}, s16[16,128]{1,0:T(8,128)(2,1)S(1)}) custom-call(s32[2]{0:T(128)S(1)} %pad_add_fusion.12.refs_0_, bf16[4096,1024]{1,0:T(8,128)(2,1)S(1)} %copy-done.1, bf16[2048,1024]{1,0:T(8,128)(2,1)} %collective-permute-done.2.refs_2_, bf16[1024,1024]{1,0:T(8,128)(2,1)S(1)} %copy-done.2, ...), custom_call_target="tpu_custom_call" | custom-call | flops 4294967296 | bytes 10485760 | tf_op jit(solution)/shard_map/sketch_rows/pallas_call | solution.py:218
  28.0 1.1 %collective-permute-done.3 = s16[2,1136,128]{2,1,0:T(8,128)(2,1)S(1)} collective-permute-done((s16[2,1136,128]{2,1,0:T(8,128)(2,1)S(1)}, s16[2,1136,128]{2,1,0:T(8,128)(2,1)S(1)}, u32[]{:S(2)}, u32[]{:S(2)}) %collective-permute-start.3) | collective-permute-done | bytes 581664 | tf_op jit(solution)/shard_map/ppermute | solution.py:394
  29.3 2.1 %collective-permute-start.4 = (s16[1,1136,128]{2,1,0:T(8,128)(2,1)S(1)}, s16[1,1136,128]{2,1,0:T(8,128)(2,1)S(1)}, u32[]{:S(2)}, u32[]{:S(2)}) collective-permute-start(s16[1,1136,128]{2,1,0:T(8,128)(2,1)S(1)} %fusion.1.refs_5_), channel_id=1, source_target_pairs={{0,4},{1,3},{2,6},{3,1},{4,0},{5,7},{6,2},{7,5},{8,12},{9,11},{10,... | collective-permute-start | bytes 872456 | tf_op jit(solution)/shard_map/ppermute | solution.py:394
  31.4 6.8 %sketch_rows.3 = (bf16[1024,2048]{1,0:T(8,128)(2,1)S(1)}, s16[16,128]{1,0:T(8,128)(2,1)S(1)}) custom-call(s32[2]{0:T(128)S(1)} %pad_add_fusion.12.refs_0_, bf16[4096,1024]{1,0:T(8,128)(2,1)S(1)} %copy-done.1, bf16[2048,1024]{1,0:T(8,128)(2,1)} %collective-permute-done.2.refs_2_, bf16[1024,1024]{1,0:T(8,128)(2,1)S(1)} %copy-done.2, ...), custom_call_target="tpu_custom_call" | custom-call | flops 4294967296 | bytes 10485760 | tf_op jit(solution)/shard_map/sketch_rows/pallas_call | solution.py:218
  38.7 1.7 %collective-permute-start.5 = (s16[1040,128]{1,0:T(8,128)(2,1)S(1)}, s16[1040,128]{1,0:T(8,128)(2,1)S(1)}, u32[]{:S(2)}, u32[]{:S(2)}) collective-permute-start(s16[1040,128]{1,0:T(8,128)(2,1)S(1)} %pad_add_fusion.4), channel_id=1, source_target_pairs={{0,8},{1,17},{2,10},{3,19},{4,12},{5,21},{6,14},{7,23},{8,0},{9,25... | collective-permute-start | bytes 798728 | tf_op jit(solution)/shard_map/ppermute | solution.py:394
  40.3 5.8 %collective-permute-done.5 = s16[1040,128]{1,0:T(8,128)(2,1)S(1)} collective-permute-done((s16[1040,128]{1,0:T(8,128)(2,1)S(1)}, s16[1040,128]{1,0:T(8,128)(2,1)S(1)}, u32[]{:S(2)}, u32[]{:S(2)}) %collective-permute-start.5) | collective-permute-done | bytes 266272 | tf_op jit(solution)/shard_map/ppermute | solution.py:394
  46.3 3.5 %collective-permute-start.6 = (s16[752,128]{1,0:T(8,128)(2,1)S(1)}, s16[752,128]{1,0:T(8,128)(2,1)S(1)}, u32[]{:S(2)}, u32[]{:S(2)}) collective-permute-start(s16[752,128]{1,0:T(8,128)(2,1)S(1)} %pad_add_fusion.6), channel_id=1, source_target_pairs={{0,16},{1,9},{2,18},{3,11},{4,20},{5,13},{6,22},{7,15},{8,24},{9,1... | collective-permute-start | bytes 577544 | tf_op jit(solution)/shard_map/ppermute | solution.py:394
  49.8 3.8 %collective-permute-done.6 = s16[752,128]{1,0:T(8,128)(2,1)S(1)} collective-permute-done((s16[752,128]{1,0:T(8,128)(2,1)S(1)}, s16[752,128]{1,0:T(8,128)(2,1)S(1)}, u32[]{:S(2)}, u32[]{:S(2)}) %collective-permute-start.6) | collective-permute-done | bytes 192544 | tf_op jit(solution)/shard_map/ppermute | solution.py:394
  53.7 1.1 %collective-permute-start.7 = (s16[1,29,16,128]{3,2,1,0:T(8,128)(2,1)S(1)}, s16[1,29,16,128]{3,2,1,0:T(8,128)(2,1)S(1)}, u32[]{:S(2)}, u32[]{:S(2)}) collective-permute-start(s16[1,29,16,128]{3,2,1,0:T(8,128)(2,1)S(1)} %add_add_fusion.1.refs_4_), channel_id=1, source_target_pairs={{0,4},{1,3},{2,6},{3,1},{4,0},{5,7},{6,2},{7,5},{8,12},{9,11},{10,... | collective-permute-start | bytes 356360 | tf_op jit(solution)/shard_map/ppermute | solution.py:394
  54.8 3.8 %collective-permute-done.7.refs_5_ = s16[1,29,16,128]{3,2,1,0:T(8,128)(2,1)S(1)} collective-permute-done((s16[1,29,16,128]{3,2,1,0:T(8,128)(2,1)S(1)}, s16[1,29,16,128]{3,2,1,0:T(8,128)(2,1)S(1)}, u32[]{:S(2)}, u32[]{:S(2)}) %collective-permute-start.7) | collective-permute-done | bytes 118816 | tf_op jit(solution)/shard_map/ppermute | solution.py:394
  58.6 4.8 %collective-permute-start.8 = (s16[2,29,16,128]{3,2,1,0:T(8,128)(2,1)S(1)}, s16[2,29,16,128]{3,2,1,0:T(8,128)(2,1)S(1)}, u32[]{:S(2)}, u32[]{:S(2)}) collective-permute-start(s16[2,29,16,128]{3,2,1,0:T(8,128)(2,1)S(1)} %pad_add_fusion.5), channel_id=1, source_target_pairs={{0,2},{1,5},{2,0},{3,7},{4,6},{5,1},{6,4},{7,3},{8,10},{9,13},{10,... | collective-permute-start | bytes 712712 | tf_op jit(solution)/shard_map/ppermute | solution.py:394
  63.4 4.1 %collective-permute-done.8.refs_6_ = s16[2,29,16,128]{3,2,1,0:T(8,128)(2,1)S(1)} collective-permute-done((s16[2,29,16,128]{3,2,1,0:T(8,128)(2,1)S(1)}, s16[2,29,16,128]{3,2,1,0:T(8,128)(2,1)S(1)}, u32[]{:S(2)}, u32[]{:S(2)}) %collective-permute-start.8) | collective-permute-done | bytes 237600 | tf_op jit(solution)/shard_map/ppermute | solution.py:394
  67.6 0.7 fusion.7.refs_8_
  68.3 1.2 %collective-permute-done.9.refs_7_ = s16[4,29,16,128]{3,2,1,0:T(8,128)(2,1)S(1)} collective-permute-done((s16[4,29,16,128]{3,2,1,0:T(8,128)(2,1)S(1)}, s16[4,29,16,128]{3,2,1,0:T(8,128)(2,1)S(1)}, u32[]{:S(2)}, u32[]{:S(2)}) %collective-permute-start.9) | collective-permute-done | bytes 475168 | tf_op jit(solution)/shard_map/ppermute | solution.py:397
  69.5 0.8 copy-done.12
  70.3 15.0 %blocked_solve.1 = (f32[2048,1024]{1,0:T(8,128)}, f32[32,1024]{1,0:T(8,128)}) custom-call(s32[2]{0:T(128)} %copy-done.3, bf16[1024,2048]{1,0:T(8,128)(2,1)} %copy-done.4, bf16[1024,2048]{1,0:T(8,128)(2,1)} %copy-done.5, f32[8,128,128]{2,1,0:T(8,128)} %refs_3_.5, s16[1,29,16,128]{3,2,1,0:T(8,128)(2,1)} %copy-done.9, s16[1,29,16,128]{3,2,1,0:T(8,128)(2,1)} %copy-done.10, ...), custom_call_target="tpu_custom_call" | custom-call | flops 8000000000 | bytes 20971520 | tf_op jit(solution)/shard_map/blocked_solve/pallas_call | solution.py:359
  (59 shorter events, 1.8 us)
Async XLA Ops:
  0.6 7.3 %collective-permute-start = (bf16[1024,1024]{1,0:T(8,128)(2,1)}, bf16[1024,1024]{1,0:T(8,128)(2,1)S(1)}, u32[]{:S(2)}, u32[]{:S(2)}) collective-permute-start(bf16[1024,1024]{1,0:T(8,128)(2,1)} %refs_3_.4), channel_id=1, source_target_pairs={{0,1},{1,0},{2,3},{3,2},{4,5},{5,4},{6,7},{7,6},{8,9},{9,8},{10,11... | collective-permute-start | bytes 6291464 | tf_op jit(solution)/shard_map/ppermute | solution.py:397
  1.2 30.2 %copy-start.3 = (s32[2]{0:T(128)}, s32[2]{0:T(128)S(1)}, u32[]{:S(2)}) copy-start(s32[2]{0:T(128)S(1)} %pad_add_fusion.12.refs_0_) | copy-start | bytes 28
  1.2 3.4 %copy-start = (bf16[4096,1024]{1,0:T(8,128)(2,1)S(1)}, bf16[4096,1024]{1,0:T(8,128)(2,1)}, u32[]{:S(2)}) copy-start(bf16[4096,1024]{1,0:T(8,128)(2,1)} %refs_1_.3) | copy-start | bytes 25165828
  4.6 0.7 copy-start.6
  7.9 2.1 %copy-start.7 = (bf16[2,256,512]{2,1,0:T(8,128)(2,1)}, bf16[2,256,512]{2,1,0:T(8,128)(2,1)S(1)}, u32[]{:S(2)}) copy-start(bf16[2,256,512]{2,1,0:T(8,128)(2,1)S(1)} %get-tuple-element.20.refs_1_) | copy-start | bytes 1572868
  8.0 2.0 %collective-permute-start.1 = (bf16[256,1024]{1,0:T(8,128)(2,1)S(1)}, bf16[256,1024]{1,0:T(8,128)(2,1)S(1)}, u32[]{:S(2)}, u32[]{:S(2)}) collective-permute-start(bf16[256,1024]{1,0:T(8,128)(2,1)S(1)} %broadcast_add_fusion.1), channel_id=1, source_target_pairs={{0,1},{1,0},{2,3},{3,2},{4,5},{5,4},{6,7},{7,6},{8,9},{9,8},{10,11... | collective-permute-start | bytes 1572872 | tf_op jit(solution)/shard_map/ppermute | solution.py:397
  10.0 11.3 %collective-permute-start.2 = (bf16[2048,1024]{1,0:T(8,128)(2,1)}, bf16[2048,1024]{1,0:T(8,128)(2,1)}, u32[]{:S(2)}, u32[]{:S(2)}) collective-permute-start(bf16[2048,1024]{1,0:T(8,128)(2,1)} %get-tuple-element.17), channel_id=1, source_target_pairs={{0,1},{1,0},{2,3},{3,2},{4,5},{5,4},{6,7},{7,6},{8,9},{9,8},{10,11... | collective-permute-start | bytes 12582920 | tf_op jit(solution)/shard_map/ppermute | solution.py:397
  10.1 1.6 %copy-start.2 = (bf16[1024,1024]{1,0:T(8,128)(2,1)S(1)}, bf16[1024,1024]{1,0:T(8,128)(2,1)}, u32[]{:S(2)}) copy-start(bf16[1024,1024]{1,0:T(8,128)(2,1)} %refs_3_.4) | copy-start | bytes 6291460
  11.7 1.0 %copy-start.8 = (bf16[2,256,512]{2,1,0:T(8,128)(2,1)S(1)}, bf16[2,256,512]{2,1,0:T(8,128)(2,1)}, u32[]{:S(2)}) copy-start(bf16[2,256,512]{2,1,0:T(8,128)(2,1)} %copy-done.7) | copy-start | bytes 1572868
  12.8 8.5 %copy-start.1 = (bf16[4096,1024]{1,0:T(8,128)(2,1)S(1)}, bf16[4096,1024]{1,0:T(8,128)(2,1)}, u32[]{:S(2)}) copy-start(bf16[4096,1024]{1,0:T(8,128)(2,1)} %refs_1_.3) | copy-start | bytes 25165828
  18.4 10.7 %collective-permute-start.3 = (s16[2,1136,128]{2,1,0:T(8,128)(2,1)S(1)}, s16[2,1136,128]{2,1,0:T(8,128)(2,1)S(1)}, u32[]{:S(2)}, u32[]{:S(2)}) collective-permute-start(s16[2,1136,128]{2,1,0:T(8,128)(2,1)S(1)} %pad_add_fusion), channel_id=1, source_target_pairs={{0,2},{1,5},{2,0},{3,7},{4,6},{5,1},{6,4},{7,3},{8,10},{9,13},{10,... | collective-permute-start | bytes 1744904 | tf_op jit(solution)/shard_map/ppermute | solution.py:394
  28.0 10.3 %copy-start.4 = (bf16[1024,2048]{1,0:T(8,128)(2,1)}, bf16[1024,2048]{1,0:T(8,128)(2,1)S(1)}, u32[]{:S(2)}) copy-start(bf16[1024,2048]{1,0:T(8,128)(2,1)S(1)} %get-tuple-element.19.refs_1_) | copy-start | bytes 12582916
  29.3 9.0 %collective-permute-start.4 = (s16[1,1136,128]{2,1,0:T(8,128)(2,1)S(1)}, s16[1,1136,128]{2,1,0:T(8,128)(2,1)S(1)}, u32[]{:S(2)}, u32[]{:S(2)}) collective-permute-start(s16[1,1136,128]{2,1,0:T(8,128)(2,1)S(1)} %fusion.1.refs_5_), channel_id=1, source_target_pairs={{0,4},{1,3},{2,6},{3,1},{4,0},{5,7},{6,2},{7,5},{8,12},{9,11},{10,... | collective-permute-start | bytes 872456 | tf_op jit(solution)/shard_map/ppermute | solution.py:394
  38.3 29.3 %copy-start.5 = (bf16[1024,2048]{1,0:T(8,128)(2,1)}, bf16[1024,2048]{1,0:T(8,128)(2,1)S(1)}, u32[]{:S(2)}) copy-start(bf16[1024,2048]{1,0:T(8,128)(2,1)S(1)} %get-tuple-element.26.refs_2_) | copy-start | bytes 12582916
  38.7 7.5 %collective-permute-start.5 = (s16[1040,128]{1,0:T(8,128)(2,1)S(1)}, s16[1040,128]{1,0:T(8,128)(2,1)S(1)}, u32[]{:S(2)}, u32[]{:S(2)}) collective-permute-start(s16[1040,128]{1,0:T(8,128)(2,1)S(1)} %pad_add_fusion.4), channel_id=1, source_target_pairs={{0,8},{1,17},{2,10},{3,19},{4,12},{5,21},{6,14},{7,23},{8,0},{9,25... | collective-permute-start | bytes 798728 | tf_op jit(solution)/shard_map/ppermute | solution.py:394
  46.3 7.3 %collective-permute-start.6 = (s16[752,128]{1,0:T(8,128)(2,1)S(1)}, s16[752,128]{1,0:T(8,128)(2,1)S(1)}, u32[]{:S(2)}, u32[]{:S(2)}) collective-permute-start(s16[752,128]{1,0:T(8,128)(2,1)S(1)} %pad_add_fusion.6), channel_id=1, source_target_pairs={{0,16},{1,9},{2,18},{3,11},{4,20},{5,13},{6,22},{7,15},{8,24},{9,1... | collective-permute-start | bytes 577544 | tf_op jit(solution)/shard_map/ppermute | solution.py:394
  53.7 15.8 %copy-start.9 = (s16[1,29,16,128]{3,2,1,0:T(8,128)(2,1)}, s16[1,29,16,128]{3,2,1,0:T(8,128)(2,1)S(1)}, u32[]{:S(2)}) copy-start(s16[1,29,16,128]{3,2,1,0:T(8,128)(2,1)S(1)} %add_add_fusion.1.refs_4_) | copy-start | bytes 356356
  53.7 4.9 %collective-permute-start.7 = (s16[1,29,16,128]{3,2,1,0:T(8,128)(2,1)S(1)}, s16[1,29,16,128]{3,2,1,0:T(8,128)(2,1)S(1)}, u32[]{:S(2)}, u32[]{:S(2)}) collective-permute-start(s16[1,29,16,128]{3,2,1,0:T(8,128)(2,1)S(1)} %add_add_fusion.1.refs_4_), channel_id=1, source_target_pairs={{0,4},{1,3},{2,6},{3,1},{4,0},{5,7},{6,2},{7,5},{8,12},{9,11},{10,... | collective-permute-start | bytes 356360 | tf_op jit(solution)/shard_map/ppermute | solution.py:394
  58.6 10.9 %copy-start.10 = (s16[1,29,16,128]{3,2,1,0:T(8,128)(2,1)}, s16[1,29,16,128]{3,2,1,0:T(8,128)(2,1)S(1)}, u32[]{:S(2)}) copy-start(s16[1,29,16,128]{3,2,1,0:T(8,128)(2,1)S(1)} %collective-permute-done.7.refs_5_) | copy-start | bytes 356356
  58.6 8.9 %collective-permute-start.8 = (s16[2,29,16,128]{3,2,1,0:T(8,128)(2,1)S(1)}, s16[2,29,16,128]{3,2,1,0:T(8,128)(2,1)S(1)}, u32[]{:S(2)}, u32[]{:S(2)}) collective-permute-start(s16[2,29,16,128]{3,2,1,0:T(8,128)(2,1)S(1)} %pad_add_fusion.5), channel_id=1, source_target_pairs={{0,2},{1,5},{2,0},{3,7},{4,6},{5,1},{6,4},{7,3},{8,10},{9,13},{10,... | collective-permute-start | bytes 712712 | tf_op jit(solution)/shard_map/ppermute | solution.py:394
  67.5 2.0 %copy-start.11 = (s16[2,29,16,128]{3,2,1,0:T(8,128)(2,1)}, s16[2,29,16,128]{3,2,1,0:T(8,128)(2,1)S(1)}, u32[]{:S(2)}) copy-start(s16[2,29,16,128]{3,2,1,0:T(8,128)(2,1)S(1)} %collective-permute-done.8.refs_6_) | copy-start | bytes 712708
  67.5 1.9 %collective-permute-start.9 = (s16[4,29,16,128]{3,2,1,0:T(8,128)(2,1)S(1)}, s16[4,29,16,128]{3,2,1,0:T(8,128)(2,1)S(1)}, u32[]{:S(2)}, u32[]{:S(2)}) collective-permute-start(s16[4,29,16,128]{3,2,1,0:T(8,128)(2,1)S(1)} %pad_add_fusion.1), channel_id=1, source_target_pairs={{0,1},{1,0},{2,3},{3,2},{4,5},{5,4},{6,7},{7,6},{8,9},{9,8},{10,11... | collective-permute-start | bytes 1425416 | tf_op jit(solution)/shard_map/ppermute | solution.py:397
  69.4 0.8 copy-start.12

commit v3 on v2

--- a/solution.py
+++ b/solution.py
@@ -116,7 +116,7 @@
         in_specs=[SMEM, VMEM, VMEM],
         out_specs=(VMEM, VMEM, HBM),
         scratch_shapes=[pltpu.SemaphoreType.DMA((8,))],
-        compiler_params=pltpu.CompilerParams(vmem_limit_bytes=28 * MIB),
+        compiler_params=pltpu.CompilerParams(vmem_limit_bytes=22 * MIB),
         cost_estimate=pl.CostEstimate(flops=4 * 10**9, bytes_accessed=14 * MIB, transcendentals=0),
         name="pick_pivot_rows",
     )(meta, piv, slab)
@@ -126,19 +126,23 @@
                  u_keep, u_send, l_keep, l_send, code_v, power_v, u_scr, l_scr):
     r, c = meta[0], meta[1]
     x, y = r & 1, (r >> 1) & 1
-    spread = [dot(place[c], p[...], ((0,), (0,))).astype(BF16) for p in (packed, packed_theirs)]
-    rows = dot(spread[0], gauss[...]) + dot(spread[1], gauss_theirs[...])
-    lane = lax.broadcasted_iota(I32, (K // 2, BLK), 1)
-    powers = jnp.zeros((K // 2, BLK), F32)
+    rows = dot(packed[...], gauss[...]) + dot(packed_theirs[...], gauss_theirs[...])
+    lane = lax.broadcasted_iota(I32, (PICKS, BLK), 1)
+    powers = jnp.zeros((PICKS, BLK), F32)
+    highs, lows = [], []
     for j in range(NBLK):
         part = rows[:, j * BLK:(j + 1) * BLK]
         most = jnp.max(jnp.abs(part), axis=1, keepdims=True)
         power = jnp.where(most > 0.0, jnp.ceil(jnp.log2(jnp.maximum(most, 1e-30)) + 0.001), 0.0)
         code = jnp.floor(part * jnp.exp2(15.0 - power) + 0.5)
         code = jnp.clip(code, -32767.0, 32767.0)
-        code_v[:, pl.ds(j * BLK, BLK)] = code.astype(I32).astype(I16)
+        high = jnp.floor(code * (1.0 / 256.0))
+        highs.append(high.astype(BF16))
+        lows.append((code - 256.0 * high).astype(BF16))
         powers = jnp.where(lane == j, power, powers)
-    power_v[...] = powers
+    spread = dot(place[c], jnp.concatenate(highs + lows + [powers.astype(BF16)], axis=1), ((0,), (0,)))
+    code_v[...] = (spread[:, :K] * 256.0 + spread[:, K:2 * K]).astype(I32).astype(I16)
+    power_v[...] = spread[:, 2 * K:]
 
     columns = lower_layout(share)
     lane = lax.broadcasted_iota(I32, (SUB, BLK), 1)
@@ -185,7 +189,7 @@
             pltpu.VMEM((4,) + u_shape, I16),
             pltpu.VMEM((4,) + l_shape, l_type),
         ],
-        compiler_params=pltpu.CompilerParams(vmem_limit_bytes=32 * MIB),
+        compiler_params=pltpu.CompilerParams(vmem_limit_bytes=24 * MIB),
         cost_estimate=pl.CostEstimate(flops=3 * 10**9, bytes_accessed=8 * MIB, transcendentals=0),
         name="pivot_rows",
     )(meta, place, packed, packed_theirs, gauss, gauss_theirs)
@@ -221,7 +225,7 @@
         in_specs=[SMEM, VMEM, HBM, VMEM, VMEM, HBM],
         out_specs=(VMEM, VMEM),
         scratch_shapes=[pltpu.VMEM((steps, tile, depth), BF16), pltpu.SemaphoreType.DMA((steps, 4))],
-        compiler_params=pltpu.CompilerParams(vmem_limit_bytes=32 * MIB),
+        compiler_params=pltpu.CompilerParams(vmem_limit_bytes=24 * MIB),
         cost_estimate=pl.CostEstimate(
             flops=4 * rows * depth * K // parts, bytes_accessed=20 * MIB // parts, transcendentals=0),
         name="sketch_rows",
@@ -370,7 +374,7 @@
             pltpu.SemaphoreType.DMA((2,)),
             pltpu.SemaphoreType.DMA((2,)),
         ],
-        compiler_params=pltpu.CompilerParams(vmem_limit_bytes=58 * MIB),
+        compiler_params=pltpu.CompilerParams(vmem_limit_bytes=52 * MIB),
         cost_estimate=pl.CostEstimate(flops=8 * 10**9, bytes_accessed=20 * MIB, transcendentals=0),
         name="blocked_solve",
     )(meta, *sketches, inverses, *pieces, low)
@@ -445,13 +449,17 @@
                 at = at ^ jnp.where(c == 0, 1 << (climb[s][0] - 2), 1 << (climb[s][1] - 2))
         order.append(lax.dynamic_index_in_dim(spread, at, 0, keepdims=False))
     low = jnp.stack(order)
+    for s, bit_of in enumerate(climb):
+        got = swap(total, bit_of)
+        if s == 0:
+            low = after(low, got)
+        total = total + got
+    got = swap(total, far)
     for bit_of in climb:
         half = low.shape[0] // 2
-        both = jnp.concatenate([total.reshape(size, BLK), low[half:].reshape(-1, BLK)], axis=0)
-        got = swap(both, bit_of)
-        total = total + got[:size].reshape(total.shape)
-        low = low[:half] + got[size:].reshape(low[:half].shape)
-    piece1 = swap(total, far)
+        low_got = swap(low[half:], bit_of)
+        low = low[:half] + low_got
+    piece1 = after(got, low_got)
     pair = jnp.concatenate([total, piece1], axis=0)
     piece2 = swap(pair, near)
     piece3 = swap_cores(jnp.concatenate([pair, piece2], axis=0))

time: 85.8 us -> 80.4 us (0.937)
  Pallas kernels: 36.7 us -> 33.8 us
  waiting for transfers between devices: 21.5 us -> 19.2 us
  starting transfers between devices: 17 us -> 18.2 us
  local copies, waits for them, and re-layouts: 7.69 us -> 6.82 us
    ppermute x6 -> x8, waiting for transfers between devices: 18.5 us -> 15.5 us  [swap(): return lax.ppermute(value, ('row', 'col'), perm)]
    pallas_call x1, Pallas kernels: 5.55 us -> 3.72 us  [pivot_rows(): pl.pallas_call(lambda *refs: pivot_kernel(share, *refs), out_shape=(u_out...]
    ppermute x6 -> x8, starting transfers between devices: 16.1 us -> 17.3 us  [swap(): return lax.ppermute(value, ('row', 'col'), perm)]
    pallas_call x1, Pallas kernels: 15 us -> 14.1 us  [solve(): pl.pallas_call(lambda *refs: solve_kernel(share, parts, *refs), out_shape...]
    unnamed x26 -> x18, local copies, waits for them, and re-layouts: 7.57 us -> 6.72 us
  transfers between devices with their start and end apart: 10 -> 12, of which waited for: 7 -> 7; matrix products, arithmetic and copies ran while one was open for 1% -> 0% of each run, Pallas kernels for 25% -> 25%
where the time goes in v3:
time: 80.4 us; the launch traced here: 80.1 us
  Pallas kernels  33.8 us (42%)
  waiting for transfers between devices  19.2 us (24%)
  starting transfers between devices  18.2 us (23%)
  local copies, waits for them, and re-layouts  6.82 us (8%)
  between operations  1.05 us (1%)
  other arithmetic  1 us (1%)
    ppermute x8, starting transfers between devices, swap(): return lax.ppermute(value, ('row', 'col'), perm)  17.3 us
    ppermute x8, waiting for transfers between devices, swap(): return lax.ppermute(value, ('row', 'col'), perm)  15.5 us
    pallas_call x1, Pallas kernels, solve(): pl.pallas_call(lambda *refs: solve_kernel(share, parts, *refs), out_shape...  14.1 us
    pallas_call x2, Pallas kernels, sketch_rows(): pl.pallas_call(lambda *refs: sketch_kernel(part, *refs), out_shape=(jax.S...  13.4 us
    unnamed x18, local copies, waits for them, and re-layouts  6.72 us
    pallas_call x1, Pallas kernels, pivot_rows(): pl.pallas_call(lambda *refs: pivot_kernel(share, *refs), out_shape=(u_out...  3.72 us
    ppermute x4, waiting for transfers between devices, swap_cores(): return lax.ppermute(value, 'col', [(0, 1), (1, 0)])  3.65 us
    pallas_call x1, Pallas kernels, pick(): pl.pallas_call(lambda *refs: pick_kernel(share, *refs), out_shape=(jax.Sh...  2.62 us
  transfers between devices with their start and end apart: 12, of which 7 were waited for; matrix products, arithmetic and copies ran while one was open for 0% of the time, Pallas kernels for 25%

profile of v3, /device:TPU:0, one launch (start us, length us, event | category | flops | bytes accessed | tf_op | source)
XLA Modules:
  0.0 80.1 jit_solution(9191119960177869512)
XLA Ops:
  0.6 0.5 collective-permute-start
  1.2 3.4 %copy-done = bf16[4096,1024]{1,0:T(8,128)(2,1)S(1)} copy-done((bf16[4096,1024]{1,0:T(8,128)(2,1)S(1)}, bf16[4096,1024]{1,0:T(8,128)(2,1)}, u32[]{:S(2)}) %copy-start) | copy-done | bytes 8388632
  4.6 0.7 copy-done.6
  5.3 2.6 %pick_pivot_rows.1 = (bf16[256,1024]{1,0:T(8,128)(2,1)S(1)}, bf16[2,256,512]{2,1,0:T(8,128)(2,1)S(1)}, bf16[2048,1024]{1,0:T(8,128)(2,1)}) custom-call(s32[2]{0:T(128)S(1)} %pad_add_fusion.10.refs_0_, s32[1,1024]{1,0:T(1,128)S(1)} %bitcast.32, bf16[4096,1024]{1,0:T(8,128)(2,1)S(1)} %copy-done), custom_call_target="tpu_custom_call" | custom-call | flops 4000000000 | bytes 14680064 | tf_op jit(solution)/shard_map/pick_pivot_rows/pallas_call | solution.py:109
  8.1 1.9 %collective-permute-done.1.refs_3_ = bf16[256,1024]{1,0:T(8,128)(2,1)S(1)} collective-permute-done((bf16[256,1024]{1,0:T(8,128)(2,1)S(1)}, bf16[256,1024]{1,0:T(8,128)(2,1)S(1)}, u32[]{:S(2)}, u32[]{:S(2)}) %collective-permute-start.1) | collective-permute-done | bytes 524320 | tf_op jit(solution)/shard_map/ppermute | solution.py:401
  10.1 1.6 %copy-done.2 = bf16[1024,1024]{1,0:T(8,128)(2,1)S(1)} copy-done((bf16[1024,1024]{1,0:T(8,128)(2,1)S(1)}, bf16[1024,1024]{1,0:T(8,128)(2,1)}, u32[]{:S(2)}) %copy-start.2) | copy-done | bytes 2097176
  11.7 1.0 %copy-done.8 = bf16[2,256,512]{2,1,0:T(8,128)(2,1)S(1)} copy-done((bf16[2,256,512]{2,1,0:T(8,128)(2,1)S(1)}, bf16[2,256,512]{2,1,0:T(8,128)(2,1)}, u32[]{:S(2)}) %copy-start.8) | copy-done | bytes 524312
  12.8 3.7 %pivot_rows.1 = (s16[2,29,16,128]{3,2,1,0:T(8,128)(2,1)S(1)}, s16[2,29,16,128]{3,2,1,0:T(8,128)(2,1)S(1)}, s16[2,21,32,128]{3,2,1,0:T(8,128)(2,1)S(1)}, s16[2,21,32,128]{3,2,1,0:T(8,128)(2,1)S(1)}) custom-call(s32[2]{0:T(128)S(1)} %pad_add_fusion.10.refs_0_, bf16[2,256,512]{2,1,0:T(8,128)(2,1)S(1)} %copy-done.8, ...), custom_call_target="tpu_custom_call" | custom-call | flops 3000000000 | bytes 8388608 | tf_op jit(solution)/shard_map/pivot_rows/pallas_call | solution.py:181
  16.5 2.9 %collective-permute-start.3 = (s16[2,1136,128]{2,1,0:T(8,128)(2,1)S(1)}, s16[2,1136,128]{2,1,0:T(8,128)(2,1)S(1)}, u32[]{:S(2)}, u32[]{:S(2)}) collective-permute-start(s16[2,1136,128]{2,1,0:T(8,128)(2,1)S(1)} %pad_add_fusion), channel_id=1, source_target_pairs={{0,2},{1,5},{2,0},{3,7},{4,6},{5,1},{6,4},{7,3},{8,10},{9,13},{10,... | collective-permute-start | bytes 1744904 | tf_op jit(solution)/shard_map/ppermute | solution.py:398
  19.5 6.7 %sketch_rows.2 = (bf16[1024,2048]{1,0:T(8,128)(2,1)S(1)}, s16[16,128]{1,0:T(8,128)(2,1)S(1)}) custom-call(s32[2]{0:T(128)S(1)} %pad_add_fusion.10.refs_0_, bf16[4096,1024]{1,0:T(8,128)(2,1)S(1)} %copy-done.1, bf16[2048,1024]{1,0:T(8,128)(2,1)} %collective-permute-done.2.refs_2_, bf16[1024,1024]{1,0:T(8,128)(2,1)S(1)} %copy-done.2, ...), custom_call_target="tpu_custom_call" | custom-call | flops 4294967296 | bytes 10485760 | tf_op jit(solution)/shard_map/sketch_rows/pallas_call | solution.py:222
  26.2 1.1 %collective-permute-done.3 = s16[2,1136,128]{2,1,0:T(8,128)(2,1)S(1)} collective-permute-done((s16[2,1136,128]{2,1,0:T(8,128)(2,1)S(1)}, s16[2,1136,128]{2,1,0:T(8,128)(2,1)S(1)}, u32[]{:S(2)}, u32[]{:S(2)}) %collective-permute-start.3) | collective-permute-done | bytes 581664 | tf_op jit(solution)/shard_map/ppermute | solution.py:398
  27.5 2.1 %collective-permute-start.4 = (s16[1,1136,128]{2,1,0:T(8,128)(2,1)S(1)}, s16[1,1136,128]{2,1,0:T(8,128)(2,1)S(1)}, u32[]{:S(2)}, u32[]{:S(2)}) collective-permute-start(s16[1,1136,128]{2,1,0:T(8,128)(2,1)S(1)} %fusion.1.refs_5_), channel_id=1, source_target_pairs={{0,4},{1,3},{2,6},{3,1},{4,0},{5,7},{6,2},{7,5},{8,12},{9,11},{10,... | collective-permute-start | bytes 872456 | tf_op jit(solution)/shard_map/ppermute | solution.py:398
  29.6 6.7 %sketch_rows.3 = (bf16[1024,2048]{1,0:T(8,128)(2,1)S(1)}, s16[16,128]{1,0:T(8,128)(2,1)S(1)}) custom-call(s32[2]{0:T(128)S(1)} %pad_add_fusion.10.refs_0_, bf16[4096,1024]{1,0:T(8,128)(2,1)S(1)} %copy-done.1, bf16[2048,1024]{1,0:T(8,128)(2,1)} %collective-permute-done.2.refs_2_, bf16[1024,1024]{1,0:T(8,128)(2,1)S(1)} %copy-done.2, ...), custom_call_target="tpu_custom_call" | custom-call | flops 4294967296 | bytes 10485760 | tf_op jit(solution)/shard_map/sketch_rows/pallas_call | solution.py:222
  36.7 1.6 %collective-permute-start.5 = (s16[1,29,16,128]{3,2,1,0:T(8,128)(2,1)S(1)}, s16[1,29,16,128]{3,2,1,0:T(8,128)(2,1)S(1)}, u32[]{:S(2)}, u32[]{:S(2)}) collective-permute-start(s16[1,29,16,128]{3,2,1,0:T(8,128)(2,1)S(1)} %bitcast.33), channel_id=1, source_target_pairs={{0,8},{1,17},{2,10},{3,19},{4,12},{5,21},{6,14},{7,23},{8,0},{9,25... | collective-permute-start | bytes 356360 | tf_op jit(solution)/shard_map/ppermute | solution.py:398
  38.5 3.2 %collective-permute-done.5 = s16[1,29,16,128]{3,2,1,0:T(8,128)(2,1)S(1)} collective-permute-done((s16[1,29,16,128]{3,2,1,0:T(8,128)(2,1)S(1)}, s16[1,29,16,128]{3,2,1,0:T(8,128)(2,1)S(1)}, u32[]{:S(2)}, u32[]{:S(2)}) %collective-permute-start.5) | collective-permute-done | bytes 118816 | tf_op jit(solution)/shard_map/ppermute | solution.py:398
  41.7 1.9 %collective-permute-start.8 = (s16[2,9,32,128]{3,2,1,0:T(8,128)(2,1)S(1)}, s16[2,9,32,128]{3,2,1,0:T(8,128)(2,1)S(1)}, u32[]{:S(2)}, u32[]{:S(2)}) collective-permute-start(s16[2,9,32,128]{3,2,1,0:T(8,128)(2,1)S(1)} %slice.95), channel_id=1, source_target_pairs={{0,8},{1,17},{2,10},{3,19},{4,12},{5,21},{6,14},{7,23},{8,0},{9,25... | collective-permute-start | bytes 442376 | tf_op jit(solution)/shard_map/ppermute | solution.py:398
  43.6 3.5 %collective-permute-start.6 = (s16[1,29,16,128]{3,2,1,0:T(8,128)(2,1)S(1)}, s16[1,29,16,128]{3,2,1,0:T(8,128)(2,1)S(1)}, u32[]{:S(2)}, u32[]{:S(2)}) collective-permute-start(s16[1,29,16,128]{3,2,1,0:T(8,128)(2,1)S(1)} %add.82), channel_id=1, source_target_pairs={{0,16},{1,9},{2,18},{3,11},{4,20},{5,13},{6,22},{7,15},{8,24},{9,1... | collective-permute-start | bytes 356360 | tf_op jit(solution)/shard_map/ppermute | solution.py:398
  47.1 2.9 %collective-permute-done.6 = s16[1,29,16,128]{3,2,1,0:T(8,128)(2,1)S(1)} collective-permute-done((s16[1,29,16,128]{3,2,1,0:T(8,128)(2,1)S(1)}, s16[1,29,16,128]{3,2,1,0:T(8,128)(2,1)S(1)}, u32[]{:S(2)}, u32[]{:S(2)}) %collective-permute-start.6) | collective-permute-done | bytes 118816 | tf_op jit(solution)/shard_map/ppermute | solution.py:398
  50.0 1.7 %collective-permute-start.7 = (s16[1,29,16,128]{3,2,1,0:T(8,128)(2,1)S(1)}, s16[1,29,16,128]{3,2,1,0:T(8,128)(2,1)S(1)}, u32[]{:S(2)}, u32[]{:S(2)}) collective-permute-start(s16[1,29,16,128]{3,2,1,0:T(8,128)(2,1)S(1)} %add.83.refs_4_), channel_id=1, source_target_pairs={{0,4},{1,3},{2,6},{3,1},{4,0},{5,7},{6,2},{7,5},{8,12},{9,11},{10,... | collective-permute-start | bytes 356360 | tf_op jit(solution)/shard_map/ppermute | solution.py:398
  51.8 3.4 %collective-permute-start.9 = (s16[1,9,32,128]{3,2,1,0:T(8,128)(2,1)S(1)}, s16[1,9,32,128]{3,2,1,0:T(8,128)(2,1)S(1)}, u32[]{:S(2)}, u32[]{:S(2)}) collective-permute-start(s16[1,9,32,128]{3,2,1,0:T(8,128)(2,1)S(1)} %slice.110), channel_id=1, source_target_pairs={{0,16},{1,9},{2,18},{3,11},{4,20},{5,13},{6,22},{7,15},{8,24},{9,1... | collective-permute-start | bytes 221192 | tf_op jit(solution)/shard_map/ppermute | solution.py:398
  55.3 2.3 %collective-permute-done.9 = s16[1,9,32,128]{3,2,1,0:T(8,128)(2,1)S(1)} collective-permute-done((s16[1,9,32,128]{3,2,1,0:T(8,128)(2,1)S(1)}, s16[1,9,32,128]{3,2,1,0:T(8,128)(2,1)S(1)}, u32[]{:S(2)}, u32[]{:S(2)}) %collective-permute-start.9) | collective-permute-done | bytes 73760 | tf_op jit(solution)/shard_map/ppermute | solution.py:398
  57.7 6.1 %collective-permute-done.10.refs_6_ = s16[2,29,16,128]{3,2,1,0:T(8,128)(2,1)S(1)} collective-permute-done((s16[2,29,16,128]{3,2,1,0:T(8,128)(2,1)S(1)}, s16[2,29,16,128]{3,2,1,0:T(8,128)(2,1)S(1)}, u32[]{:S(2)}, u32[]{:S(2)}) %collective-permute-start.10) | collective-permute-done | bytes 237600 | tf_op jit(solution)/shard_map/ppermute | solution.py:398
  64.0 1.8 %collective-permute-done.11.refs_7_ = s16[4,29,16,128]{3,2,1,0:T(8,128)(2,1)S(1)} collective-permute-done((s16[4,29,16,128]{3,2,1,0:T(8,128)(2,1)S(1)}, s16[4,29,16,128]{3,2,1,0:T(8,128)(2,1)S(1)}, u32[]{:S(2)}, u32[]{:S(2)}) %collective-permute-start.11) | collective-permute-done | bytes 475168 | tf_op jit(solution)/shard_map/ppermute | solution.py:401
  65.8 14.1 %blocked_solve.1 = (f32[2048,1024]{1,0:T(8,128)}, f32[32,1024]{1,0:T(8,128)}) custom-call(s32[2]{0:T(128)S(1)} %pad_add_fusion.10.refs_0_, bf16[1024,2048]{1,0:T(8,128)(2,1)} %copy-done.3, bf16[1024,2048]{1,0:T(8,128)(2,1)} %copy-done.4, f32[8,128,128]{2,1,0:T(8,128)S(1)} %copy-done.5, s16[1,29,16,128]{3,2,1,0:T(8,128)(2,1)S(1)} %add.83.refs_4_, ...), custom_call_target="tpu_custom_call" | custom-call | flops 8000000000 | bytes 20971520 | tf_op jit(solution)/shard_map/blocked_solve/pallas_call | solution.py:363
  (51 shorter events, 1.5 us)
Async XLA Ops:
  0.6 7.3 %collective-permute-start = (bf16[1024,1024]{1,0:T(8,128)(2,1)}, bf16[1024,1024]{1,0:T(8,128)(2,1)S(1)}, u32[]{:S(2)}, u32[]{:S(2)}) collective-permute-start(bf16[1024,1024]{1,0:T(8,128)(2,1)} %refs_3_.4), channel_id=1, source_target_pairs={{0,1},{1,0},{2,3},{3,2},{4,5},{5,4},{6,7},{7,6},{8,9},{9,8},{10,11... | collective-permute-start | bytes 6291464 | tf_op jit(solution)/shard_map/ppermute | solution.py:401
  1.2 3.4 %copy-start = (bf16[4096,1024]{1,0:T(8,128)(2,1)S(1)}, bf16[4096,1024]{1,0:T(8,128)(2,1)}, u32[]{:S(2)}) copy-start(bf16[4096,1024]{1,0:T(8,128)(2,1)} %refs_1_.3) | copy-start | bytes 25165828
  4.6 0.7 copy-start.6
  7.9 2.1 %copy-start.7 = (bf16[2,256,512]{2,1,0:T(8,128)(2,1)}, bf16[2,256,512]{2,1,0:T(8,128)(2,1)S(1)}, u32[]{:S(2)}) copy-start(bf16[2,256,512]{2,1,0:T(8,128)(2,1)S(1)} %get-tuple-element.22.refs_1_) | copy-start | bytes 1572868
  8.0 2.0 %collective-permute-start.1 = (bf16[256,1024]{1,0:T(8,128)(2,1)S(1)}, bf16[256,1024]{1,0:T(8,128)(2,1)S(1)}, u32[]{:S(2)}, u32[]{:S(2)}) collective-permute-start(bf16[256,1024]{1,0:T(8,128)(2,1)S(1)} %broadcast_add_fusion.1), channel_id=1, source_target_pairs={{0,1},{1,0},{2,3},{3,2},{4,5},{5,4},{6,7},{7,6},{8,9},{9,8},{10,11... | collective-permute-start | bytes 1572872 | tf_op jit(solution)/shard_map/ppermute | solution.py:401
  10.0 9.5 %collective-permute-start.2 = (bf16[2048,1024]{1,0:T(8,128)(2,1)}, bf16[2048,1024]{1,0:T(8,128)(2,1)}, u32[]{:S(2)}, u32[]{:S(2)}) collective-permute-start(bf16[2048,1024]{1,0:T(8,128)(2,1)} %get-tuple-element.19), channel_id=1, source_target_pairs={{0,1},{1,0},{2,3},{3,2},{4,5},{5,4},{6,7},{7,6},{8,9},{9,8},{10,11... | collective-permute-start | bytes 12582920 | tf_op jit(solution)/shard_map/ppermute | solution.py:401
  10.1 1.6 %copy-start.2 = (bf16[1024,1024]{1,0:T(8,128)(2,1)S(1)}, bf16[1024,1024]{1,0:T(8,128)(2,1)}, u32[]{:S(2)}) copy-start(bf16[1024,1024]{1,0:T(8,128)(2,1)} %refs_3_.4) | copy-start | bytes 6291460
  11.7 1.0 %copy-start.8 = (bf16[2,256,512]{2,1,0:T(8,128)(2,1)S(1)}, bf16[2,256,512]{2,1,0:T(8,128)(2,1)}, u32[]{:S(2)}) copy-start(bf16[2,256,512]{2,1,0:T(8,128)(2,1)} %copy-done.7) | copy-start | bytes 1572868
  12.8 6.7 %copy-start.1 = (bf16[4096,1024]{1,0:T(8,128)(2,1)S(1)}, bf16[4096,1024]{1,0:T(8,128)(2,1)}, u32[]{:S(2)}) copy-start(bf16[4096,1024]{1,0:T(8,128)(2,1)} %refs_1_.3) | copy-start | bytes 25165828
  16.5 10.7 %collective-permute-start.3 = (s16[2,1136,128]{2,1,0:T(8,128)(2,1)S(1)}, s16[2,1136,128]{2,1,0:T(8,128)(2,1)S(1)}, u32[]{:S(2)}, u32[]{:S(2)}) collective-permute-start(s16[2,1136,128]{2,1,0:T(8,128)(2,1)S(1)} %pad_add_fusion), channel_id=1, source_target_pairs={{0,2},{1,5},{2,0},{3,7},{4,6},{5,1},{6,4},{7,3},{8,10},{9,13},{10,... | collective-permute-start | bytes 1744904 | tf_op jit(solution)/shard_map/ppermute | solution.py:398
  26.2 10.1 %copy-start.3 = (bf16[1024,2048]{1,0:T(8,128)(2,1)}, bf16[1024,2048]{1,0:T(8,128)(2,1)S(1)}, u32[]{:S(2)}) copy-start(bf16[1024,2048]{1,0:T(8,128)(2,1)S(1)} %get-tuple-element.21.refs_1_) | copy-start | bytes 12582916
  27.5 8.9 %collective-permute-start.4 = (s16[1,1136,128]{2,1,0:T(8,128)(2,1)S(1)}, s16[1,1136,128]{2,1,0:T(8,128)(2,1)S(1)}, u32[]{:S(2)}, u32[]{:S(2)}) collective-permute-start(s16[1,1136,128]{2,1,0:T(8,128)(2,1)S(1)} %fusion.1.refs_5_), channel_id=1, source_target_pairs={{0,4},{1,3},{2,6},{3,1},{4,0},{5,7},{6,2},{7,5},{8,12},{9,11},{10,... | collective-permute-start | bytes 872456 | tf_op jit(solution)/shard_map/ppermute | solution.py:398
  36.3 27.6 %copy-start.4 = (bf16[1024,2048]{1,0:T(8,128)(2,1)}, bf16[1024,2048]{1,0:T(8,128)(2,1)S(1)}, u32[]{:S(2)}) copy-start(bf16[1024,2048]{1,0:T(8,128)(2,1)S(1)} %get-tuple-element.28.refs_2_) | copy-start | bytes 12582916
  36.3 29.5 %copy-start.5 = (f32[8,128,128]{2,1,0:T(8,128)S(1)}, f32[8,128,128]{2,1,0:T(8,128)}, u32[]{:S(2)}) copy-start(f32[8,128,128]{2,1,0:T(8,128)} %refs_3_.5) | copy-start | bytes 1572868
  36.7 4.9 %collective-permute-start.5 = (s16[1,29,16,128]{3,2,1,0:T(8,128)(2,1)S(1)}, s16[1,29,16,128]{3,2,1,0:T(8,128)(2,1)S(1)}, u32[]{:S(2)}, u32[]{:S(2)}) collective-permute-start(s16[1,29,16,128]{3,2,1,0:T(8,128)(2,1)S(1)} %bitcast.33), channel_id=1, source_target_pairs={{0,8},{1,17},{2,10},{3,19},{4,12},{5,21},{6,14},{7,23},{8,0},{9,25... | collective-permute-start | bytes 356360 | tf_op jit(solution)/shard_map/ppermute | solution.py:398
  41.7 10.1 %collective-permute-start.8 = (s16[2,9,32,128]{3,2,1,0:T(8,128)(2,1)S(1)}, s16[2,9,32,128]{3,2,1,0:T(8,128)(2,1)S(1)}, u32[]{:S(2)}, u32[]{:S(2)}) collective-permute-start(s16[2,9,32,128]{3,2,1,0:T(8,128)(2,1)S(1)} %slice.95), channel_id=1, source_target_pairs={{0,8},{1,17},{2,10},{3,19},{4,12},{5,21},{6,14},{7,23},{8,0},{9,25... | collective-permute-start | bytes 442376 | tf_op jit(solution)/shard_map/ppermute | solution.py:398
  43.6 6.4 %collective-permute-start.6 = (s16[1,29,16,128]{3,2,1,0:T(8,128)(2,1)S(1)}, s16[1,29,16,128]{3,2,1,0:T(8,128)(2,1)S(1)}, u32[]{:S(2)}, u32[]{:S(2)}) collective-permute-start(s16[1,29,16,128]{3,2,1,0:T(8,128)(2,1)S(1)} %add.82), channel_id=1, source_target_pairs={{0,16},{1,9},{2,18},{3,11},{4,20},{5,13},{6,22},{7,15},{8,24},{9,1... | collective-permute-start | bytes 356360 | tf_op jit(solution)/shard_map/ppermute | solution.py:398
  50.0 7.6 %collective-permute-start.7 = (s16[1,29,16,128]{3,2,1,0:T(8,128)(2,1)S(1)}, s16[1,29,16,128]{3,2,1,0:T(8,128)(2,1)S(1)}, u32[]{:S(2)}, u32[]{:S(2)}) collective-permute-start(s16[1,29,16,128]{3,2,1,0:T(8,128)(2,1)S(1)} %add.83.refs_4_), channel_id=1, source_target_pairs={{0,4},{1,3},{2,6},{3,1},{4,0},{5,7},{6,2},{7,5},{8,12},{9,11},{10,... | collective-permute-start | bytes 356360 | tf_op jit(solution)/shard_map/ppermute | solution.py:398
  51.8 5.8 %collective-permute-start.9 = (s16[1,9,32,128]{3,2,1,0:T(8,128)(2,1)S(1)}, s16[1,9,32,128]{3,2,1,0:T(8,128)(2,1)S(1)}, u32[]{:S(2)}, u32[]{:S(2)}) collective-permute-start(s16[1,9,32,128]{3,2,1,0:T(8,128)(2,1)S(1)} %slice.110), channel_id=1, source_target_pairs={{0,16},{1,9},{2,18},{3,11},{4,20},{5,13},{6,22},{7,15},{8,24},{9,1... | collective-permute-start | bytes 221192 | tf_op jit(solution)/shard_map/ppermute | solution.py:398
  57.7 6.2 %collective-permute-start.10 = (s16[2,29,16,128]{3,2,1,0:T(8,128)(2,1)S(1)}, s16[2,29,16,128]{3,2,1,0:T(8,128)(2,1)S(1)}, u32[]{:S(2)}, u32[]{:S(2)}) collective-permute-start(s16[2,29,16,128]{3,2,1,0:T(8,128)(2,1)S(1)} %pad_add_fusion.5), channel_id=1, source_target_pairs={{0,2},{1,5},{2,0},{3,7},{4,6},{5,1},{6,4},{7,3},{8,10},{9,13},{10,... | collective-permute-start | bytes 712712 | tf_op jit(solution)/shard_map/ppermute | solution.py:398
  63.9 1.9 %collective-permute-start.11 = (s16[4,29,16,128]{3,2,1,0:T(8,128)(2,1)S(1)}, s16[4,29,16,128]{3,2,1,0:T(8,128)(2,1)S(1)}, u32[]{:S(2)}, u32[]{:S(2)}) collective-permute-start(s16[4,29,16,128]{3,2,1,0:T(8,128)(2,1)S(1)} %pad_add_fusion.1), channel_id=1, source_target_pairs={{0,1},{1,0},{2,3},{3,2},{4,5},{5,4},{6,7},{7,6},{8,9},{9,8},{10,11... | collective-permute-start | bytes 1425416 | tf_op jit(solution)/shard_map/ppermute | solution.py:401

commit v4 on v3

--- a/solution.py
+++ b/solution.py
@@ -13,6 +13,7 @@
 SHARD_ROWS = 2048
 PIV_MOST = 128
 PICKS = 2 * PIV_MOST
+PIECE = 256
 SUB = 16
 UPPER = [(i, j) for i in range(NBLK) for j in range(i + 1, NBLK)]
 F32 = jnp.float32
@@ -195,39 +196,35 @@
     )(meta, place, packed, packed_theirs, gauss, gauss_theirs)
 
 
-def sketch_kernel(part, meta, slab, theirs, gauss, gauss_theirs, later, out, mark, theirs_v, sems):
+def sketch_kernel(first, meta, slab, theirs, gauss, gauss_theirs, later, out, mark, theirs_v, sems):
     rows = out.shape[0]
-    tile = theirs_v.shape[1]
-    steps = rows // tile
-    here = [part * rows + t * tile for t in range(steps)]
-    loads = [Copies(theirs.at[pl.ds(here[t], tile)], theirs_v.at[t], sems.at[t]) for t in range(steps)]
+    tiles = [pl.ds(t, min(2 * PIECE, rows - t)) for t in range(0, rows, 2 * PIECE)]
+    loads = [Copies(theirs.at[pl.ds(first + t.start, t.size)], theirs_v.at[t], sems.at[n]) for n, t in enumerate(tiles)]
     for copy in loads:
         copy.start()
     mark[...] = jnp.zeros_like(mark)
-    for t in range(steps):
-        mine = pl.ds(pl.multiple_of(meta[1] * theirs.shape[0] + here[t], tile), tile)
+    for n, t in enumerate(tiles):
+        mine = pl.ds(pl.multiple_of(meta[1] * theirs.shape[0] + first + t.start, PIECE), t.size)
         total = dot(slab[mine, :], gauss[...])
-        loads[t].wait()
-        high, low = split(total + dot(theirs_v[t], gauss_theirs[...]))
+        loads[n].wait()
+        high, low = split(total + dot(theirs_v[t, :], gauss_theirs[...]))
         for s in range(NWIDE):
             cols = slice(s * WIDE, (s + 1) * WIDE)
-            out[pl.ds(t * tile, tile), pl.ds(2 * s * WIDE, WIDE)] = high[:, cols]
-            out[pl.ds(t * tile, tile), pl.ds((2 * s + 1) * WIDE, WIDE)] = low[:, cols]
-
-
-def sketch_rows(meta, slab, theirs, gauss, gauss_theirs, part, parts, later):
-    rows, depth = theirs.shape
-    tile = 512
-    steps = rows // parts // tile
+            out[t, pl.ds(2 * s * WIDE, WIDE)] = high[:, cols]
+            out[t, pl.ds((2 * s + 1) * WIDE, WIDE)] = low[:, cols]
+
+
+def sketch_rows(meta, slab, theirs, gauss, gauss_theirs, first, rows, later):
+    depth = theirs.shape[1]
     return pl.pallas_call(
-        lambda *refs: sketch_kernel(part, *refs),
-        out_shape=(jax.ShapeDtypeStruct((rows // parts, 2 * K), BF16), jax.ShapeDtypeStruct((SUB, BLK), I16)),
+        lambda *refs: sketch_kernel(first, *refs),
+        out_shape=(jax.ShapeDtypeStruct((rows, 2 * K), BF16), jax.ShapeDtypeStruct((SUB, BLK), I16)),
         in_specs=[SMEM, VMEM, HBM, VMEM, VMEM, HBM],
         out_specs=(VMEM, VMEM),
-        scratch_shapes=[pltpu.VMEM((steps, tile, depth), BF16), pltpu.SemaphoreType.DMA((steps, 4))],
-        compiler_params=pltpu.CompilerParams(vmem_limit_bytes=24 * MIB),
+        scratch_shapes=[pltpu.VMEM((rows, depth), BF16), pltpu.SemaphoreType.DMA((-(-rows // (2 * PIECE)), 4))],
+        compiler_params=pltpu.CompilerParams(vmem_limit_bytes=26 * MIB),
         cost_estimate=pl.CostEstimate(
-            flops=4 * rows * depth * K // parts, bytes_accessed=20 * MIB // parts, transcendentals=0),
+            flops=4 * rows * depth * K, bytes_accessed=10 * MIB, transcendentals=0),
         name="sketch_rows",
     )(meta, slab, theirs, gauss, gauss_theirs, later)
 
@@ -242,7 +239,6 @@
 def prepare(share, r, c, inverses, pieces, low, own_rows, coupling, weights):
     x, y = r & 1, (r >> 1) & 1
     lane = lax.broadcasted_iota(I32, (SUB, BLK), 1)
-    coupling[...] = jnp.zeros_like(coupling)
     slot = 0
     chunk = min(SUB, share)
     for piece in pieces:
@@ -251,7 +247,7 @@
             high, less = (slot >> 1) & 1, slot & 1
             dx, dy = jnp.where(gc == 0, high, less), jnp.where(gc == 0, less, high)
             quarter = (y ^ dy) * 2 + (x ^ dx)
-            tail = piece[k, len(UPPER)].astype(I32).astype(F32)
+            scales = jnp.exp2(piece[k, len(UPPER)].astype(I32).astype(F32) - 15.0) * (-1.0 / K**0.5)
             for i in range(NBLK - 1):
                 starts = []
                 for part in range(SUB // chunk):
@@ -261,8 +257,7 @@
                 for n, (row_block, j) in enumerate(UPPER):
                     if row_block != i:
                         continue
-                    scale = jnp.exp2(tail[:, n:n + 1] - 15.0) * (-1.0 / K**0.5)
-                    value = piece[k, n].astype(I32).astype(F32) * scale
+                    value = piece[k, n].astype(I32).astype(F32) * scales[:, n:n + 1]
                     for part in range(SUB // chunk):
                         coupling[pl.ds(starts[part], chunk), pl.ds(j * BLK, BLK)] = (
                             value[part * chunk:(part + 1) * chunk])
@@ -299,16 +294,21 @@
     (inverses, p0, p1, p2, p3, low, out, own_rows,
      coupling, weights, earlier, pair_v, out_v, in_sems, out_sems) = refs
     tile = out_v.shape[1]
-    each = sketches[0].shape[0] // tile
-    steps = each * parts
+    steps = out.shape[0] // tile
 
     def start_in(step):
         slot = lax.rem(step, 2)
-        for part in range(parts):
-            @pl.when(lax.div(step, each) == part)
-            def _():
-                where = pl.ds(pl.multiple_of((step - part * each) * tile, tile), tile)
-                pltpu.make_async_copy(sketches[part].at[where], pair_v.at[slot], in_sems.at[slot]).start()
+        for h in range(tile // PIECE):
+            piece, first = step * (tile // PIECE) + h, 0
+            for sketch in sketches:
+                count = sketch.shape[0] // PIECE
+
+                @pl.when((piece >= first) & (piece < first + count))
+                def _():
+                    where = pl.ds(pl.multiple_of((piece - first) * PIECE, PIECE), PIECE)
+                    pltpu.make_async_copy(
+                        sketch.at[where], pair_v.at[slot, pl.ds(h * PIECE, PIECE)], in_sems.at[slot, h]).start()
+                first += count
 
     def copy_out(step):
         slot = lax.rem(step, 2)
@@ -328,7 +328,9 @@
         def _():
             copy_out(step - 2).wait()
 
-        pltpu.make_async_copy(sketches[0].at[pl.ds(0, tile)], pair_v.at[slot], in_sems.at[slot]).wait()
+        for h in range(tile // PIECE):
+            pltpu.make_async_copy(
+                sketches[0].at[pl.ds(0, PIECE)], pair_v.at[slot, pl.ds(h * PIECE, PIECE)], in_sems.at[slot, h]).wait()
         for s in range(NWIDE):
             cols = pl.ds(s * WIDE, WIDE)
             for q in range(tile // sub):
@@ -371,7 +373,7 @@
             pltpu.VMEM((tile, 3 * (NWIDE - 1) * WIDE), BF16),
             pltpu.VMEM((2, tile, 2 * K), BF16),
             pltpu.VMEM((2, tile, K), F32),
-            pltpu.SemaphoreType.DMA((2,)),
+            pltpu.SemaphoreType.DMA((2, tile // PIECE)),
             pltpu.SemaphoreType.DMA((2,)),
         ],
         compiler_params=pltpu.CompilerParams(vmem_limit_bytes=52 * MIB),
@@ -412,10 +414,12 @@
         meta, place, packed, packed_theirs, gauss, gauss_theirs, share)
 
 
-    parts = 2
+    rest = slab.shape[0] // cols * 3 // 8
+    bounds = (0, slab.shape[0] // cols - rest, slab.shape[0] // cols)
 
     def sketch_part(part, later):
-        return sketch_rows(meta, slab, slab_theirs, gauss, gauss_theirs, part, parts, later)
+        first, end = bounds[part:part + 2]
+        return sketch_rows(meta, slab, slab_theirs, gauss, gauss_theirs, first, end - first, later)
 
     size, l_shape = u_keep[0].size // BLK, l_keep.shape[1:]
 
@@ -459,9 +463,9 @@
         half = low.shape[0] // 2
         low_got = swap(low[half:], bit_of)
         low = low[:half] + low_got
-    piece1 = after(got, low_got)
+    piece1 = got
     pair = jnp.concatenate([total, piece1], axis=0)
-    piece2 = swap(pair, near)
+    piece2 = after(swap(pair, near), low_got)
     piece3 = swap_cores(jnp.concatenate([pair, piece2], axis=0))
     return solve(meta, sketches, block_inverses, (total, piece1, piece2, piece3), low[0], share)
 

time: 80.4 us -> 76.2 us (0.948)
  waiting for transfers between devices: 19.2 us -> 16.3 us
  starting transfers between devices: 18.2 us -> 16.2 us
    ppermute x8, waiting for transfers between devices: 15.5 us -> 12.6 us  [swap(): return lax.ppermute(value, ('row', 'col'), perm)]
    ppermute x8, starting transfers between devices: 17.3 us -> 15.4 us  [swap(): return lax.ppermute(value, ('row', 'col'), perm)]
    unnamed x18 -> x20, local copies, waits for them, and re-layouts: 6.72 us -> 6.73 us
  transfers between devices with their start and end apart: 12 -> 12, of which waited for: 7 -> 7; matrix products, arithmetic and copies ran while one was open for 0% -> 0% of each run, Pallas kernels for 25% -> 27%
where the time goes in v4:
time: 76.2 us; the launch traced here: 75.5 us
  Pallas kernels  34.3 us (45%)
  waiting for transfers between devices  16.3 us (21%)
  starting transfers between devices  16.2 us (21%)
  local copies, waits for them, and re-layouts  6.81 us (9%)
  between operations  1.05 us (1%)
  other arithmetic  0.82 us (1%)
    ppermute x8, starting transfers between devices, swap(): return lax.ppermute(value, ('row', 'col'), perm)  15.4 us
    pallas_call x2, Pallas kernels, sketch_rows(): pl.pallas_call(lambda *refs: sketch_kernel(first, *refs), out_shape=(jax....  14 us
    pallas_call x1, Pallas kernels, solve(): pl.pallas_call(lambda *refs: solve_kernel(share, parts, *refs), out_shape...  14 us
    ppermute x8, waiting for transfers between devices, swap(): return lax.ppermute(value, ('row', 'col'), perm)  12.6 us
    unnamed x20, local copies, waits for them, and re-layouts  6.73 us
    pallas_call x1, Pallas kernels, pivot_rows(): pl.pallas_call(lambda *refs: pivot_kernel(share, *refs), out_shape=(u_out...  3.72 us
    ppermute x4, waiting for transfers between devices, swap_cores(): return lax.ppermute(value, 'col', [(0, 1), (1, 0)])  3.65 us
    pallas_call x1, Pallas kernels, pick(): pl.pallas_call(lambda *refs: pick_kernel(share, *refs), out_shape=(jax.Sh...  2.62 us
  transfers between devices with their start and end apart: 12, of which 7 were waited for; matrix products, arithmetic and copies ran while one was open for 0% of the time, Pallas kernels for 27%

profile of v4, /device:TPU:0, one launch (start us, length us, event | category | flops | bytes accessed | tf_op | source)
XLA Modules:
  0.0 75.5 jit_solution(17389973145082412807)
XLA Ops:
  0.6 0.5 collective-permute-start
  1.2 3.4 %copy-done = bf16[4096,1024]{1,0:T(8,128)(2,1)S(1)} copy-done((bf16[4096,1024]{1,0:T(8,128)(2,1)S(1)}, bf16[4096,1024]{1,0:T(8,128)(2,1)}, u32[]{:S(2)}) %copy-start) | copy-done | bytes 8388632
  4.6 0.7 copy-done.6
  5.3 2.6 %pick_pivot_rows.1 = (bf16[256,1024]{1,0:T(8,128)(2,1)S(1)}, bf16[2,256,512]{2,1,0:T(8,128)(2,1)S(1)}, bf16[2048,1024]{1,0:T(8,128)(2,1)}) custom-call(s32[2]{0:T(128)S(1)} %pad_add_fusion.10.refs_0_, s32[1,1024]{1,0:T(1,128)S(1)} %bitcast.32, bf16[4096,1024]{1,0:T(8,128)(2,1)S(1)} %copy-done), custom_call_target="tpu_custom_call" | custom-call | flops 4000000000 | bytes 14680064 | tf_op jit(solution)/shard_map/pick_pivot_rows/pallas_call | solution.py:110
  8.1 1.9 %collective-permute-done.1.refs_3_ = bf16[256,1024]{1,0:T(8,128)(2,1)S(1)} collective-permute-done((bf16[256,1024]{1,0:T(8,128)(2,1)S(1)}, bf16[256,1024]{1,0:T(8,128)(2,1)S(1)}, u32[]{:S(2)}, u32[]{:S(2)}) %collective-permute-start.1) | collective-permute-done | bytes 524320 | tf_op jit(solution)/shard_map/ppermute | solution.py:403
  10.1 1.6 %copy-done.2 = bf16[1024,1024]{1,0:T(8,128)(2,1)S(1)} copy-done((bf16[1024,1024]{1,0:T(8,128)(2,1)S(1)}, bf16[1024,1024]{1,0:T(8,128)(2,1)}, u32[]{:S(2)}) %copy-start.2) | copy-done | bytes 2097176
  11.7 1.0 %copy-done.9 = bf16[2,256,512]{2,1,0:T(8,128)(2,1)S(1)} copy-done((bf16[2,256,512]{2,1,0:T(8,128)(2,1)S(1)}, bf16[2,256,512]{2,1,0:T(8,128)(2,1)}, u32[]{:S(2)}) %copy-start.9) | copy-done | bytes 524312
  12.8 3.7 %pivot_rows.1 = (s16[2,29,16,128]{3,2,1,0:T(8,128)(2,1)S(1)}, s16[2,29,16,128]{3,2,1,0:T(8,128)(2,1)S(1)}, s16[2,21,32,128]{3,2,1,0:T(8,128)(2,1)S(1)}, s16[2,21,32,128]{3,2,1,0:T(8,128)(2,1)S(1)}) custom-call(s32[2]{0:T(128)S(1)} %pad_add_fusion.10.refs_0_, bf16[2,256,512]{2,1,0:T(8,128)(2,1)S(1)} %copy-done.9, ...), custom_call_target="tpu_custom_call" | custom-call | flops 3000000000 | bytes 8388608 | tf_op jit(solution)/shard_map/pivot_rows/pallas_call | solution.py:182
  16.6 2.9 %collective-permute-start.3 = (s16[2,1136,128]{2,1,0:T(8,128)(2,1)S(1)}, s16[2,1136,128]{2,1,0:T(8,128)(2,1)S(1)}, u32[]{:S(2)}, u32[]{:S(2)}) collective-permute-start(s16[2,1136,128]{2,1,0:T(8,128)(2,1)S(1)} %pad_add_fusion), channel_id=1, source_target_pairs={{0,2},{1,5},{2,0},{3,7},{4,6},{5,1},{6,4},{7,3},{8,10},{9,13},{10,... | collective-permute-start | bytes 1744904 | tf_op jit(solution)/shard_map/ppermute | solution.py:400
  19.5 8.2 %sketch_rows.2 = (bf16[1280,2048]{1,0:T(8,128)(2,1)S(1)}, s16[16,128]{1,0:T(8,128)(2,1)S(1)}) custom-call(s32[2]{0:T(128)S(1)} %pad_add_fusion.10.refs_0_, bf16[4096,1024]{1,0:T(8,128)(2,1)S(1)} %copy-done.1, bf16[2048,1024]{1,0:T(8,128)(2,1)} %collective-permute-done.2.refs_2_, bf16[1024,1024]{1,0:T(8,128)(2,1)S(1)} %copy-done.3, ...), custom_call_target="tpu_custom_call" | custom-call | flops 5368709120 | bytes 10485760 | tf_op jit(solution)/shard_map/sketch_rows/pallas_call | solution.py:219
  28.0 1.6 %collective-permute-start.4 = (s16[1,1136,128]{2,1,0:T(8,128)(2,1)S(1)}, s16[1,1136,128]{2,1,0:T(8,128)(2,1)S(1)}, u32[]{:S(2)}, u32[]{:S(2)}) collective-permute-start(s16[1,1136,128]{2,1,0:T(8,128)(2,1)S(1)} %fusion.1.refs_5_), channel_id=1, source_target_pairs={{0,4},{1,3},{2,6},{3,1},{4,0},{5,7},{6,2},{7,5},{8,12},{9,11},{10,... | collective-permute-start | bytes 872456 | tf_op jit(solution)/shard_map/ppermute | solution.py:400
  29.6 5.8 %sketch_rows.3 = (bf16[768,2048]{1,0:T(8,128)(2,1)S(1)}, s16[16,128]{1,0:T(8,128)(2,1)S(1)}) custom-call(s32[2]{0:T(128)S(1)} %pad_add_fusion.10.refs_0_, bf16[4096,1024]{1,0:T(8,128)(2,1)S(1)} %copy-done.1, bf16[2048,1024]{1,0:T(8,128)(2,1)} %collective-permute-done.2.refs_2_, bf16[1024,1024]{1,0:T(8,128)(2,1)S(1)} %copy-done.3, ...), custom_call_target="tpu_custom_call" | custom-call | flops 3221225472 | bytes 10485760 | tf_op jit(solution)/shard_map/sketch_rows/pallas_call | solution.py:219
  35.6 1.7 %collective-permute-start.5 = (s16[1,29,16,128]{3,2,1,0:T(8,128)(2,1)S(1)}, s16[1,29,16,128]{3,2,1,0:T(8,128)(2,1)S(1)}, u32[]{:S(2)}, u32[]{:S(2)}) collective-permute-start(s16[1,29,16,128]{3,2,1,0:T(8,128)(2,1)S(1)} %bitcast.33), channel_id=1, source_target_pairs={{0,8},{1,17},{2,10},{3,19},{4,12},{5,21},{6,14},{7,23},{8,0},{9,25... | collective-permute-start | bytes 356360 | tf_op jit(solution)/shard_map/ppermute | solution.py:400
  37.3 3.8 %collective-permute-done.5 = s16[1,29,16,128]{3,2,1,0:T(8,128)(2,1)S(1)} collective-permute-done((s16[1,29,16,128]{3,2,1,0:T(8,128)(2,1)S(1)}, s16[1,29,16,128]{3,2,1,0:T(8,128)(2,1)S(1)}, u32[]{:S(2)}, u32[]{:S(2)}) %collective-permute-start.5) | collective-permute-done | bytes 118816 | tf_op jit(solution)/shard_map/ppermute | solution.py:400
  41.1 2.3 %collective-permute-start.6 = (s16[1,29,16,128]{3,2,1,0:T(8,128)(2,1)S(1)}, s16[1,29,16,128]{3,2,1,0:T(8,128)(2,1)S(1)}, u32[]{:S(2)}, u32[]{:S(2)}) collective-permute-start(s16[1,29,16,128]{3,2,1,0:T(8,128)(2,1)S(1)} %add.82), channel_id=1, source_target_pairs={{0,16},{1,9},{2,18},{3,11},{4,20},{5,13},{6,22},{7,15},{8,24},{9,1... | collective-permute-start | bytes 356360 | tf_op jit(solution)/shard_map/ppermute | solution.py:400
  43.5 3.5 %collective-permute-done.6 = s16[1,29,16,128]{3,2,1,0:T(8,128)(2,1)S(1)} collective-permute-done((s16[1,29,16,128]{3,2,1,0:T(8,128)(2,1)S(1)}, s16[1,29,16,128]{3,2,1,0:T(8,128)(2,1)S(1)}, u32[]{:S(2)}, u32[]{:S(2)}) %collective-permute-start.6) | collective-permute-done | bytes 118816 | tf_op jit(solution)/shard_map/ppermute | solution.py:400
  47.0 1.2 %collective-permute-start.7 = (s16[1,29,16,128]{3,2,1,0:T(8,128)(2,1)S(1)}, s16[1,29,16,128]{3,2,1,0:T(8,128)(2,1)S(1)}, u32[]{:S(2)}, u32[]{:S(2)}) collective-permute-start(s16[1,29,16,128]{3,2,1,0:T(8,128)(2,1)S(1)} %add.83.refs_4_), channel_id=1, source_target_pairs={{0,4},{1,3},{2,6},{3,1},{4,0},{5,7},{6,2},{7,5},{8,12},{9,11},{10,... | collective-permute-start | bytes 356360 | tf_op jit(solution)/shard_map/ppermute | solution.py:400
  48.3 1.9 %collective-permute-start.9 = (s16[2,9,32,128]{3,2,1,0:T(8,128)(2,1)S(1)}, s16[2,9,32,128]{3,2,1,0:T(8,128)(2,1)S(1)}, u32[]{:S(2)}, u32[]{:S(2)}) collective-permute-start(s16[2,9,32,128]{3,2,1,0:T(8,128)(2,1)S(1)} %slice.95), channel_id=1, source_target_pairs={{0,8},{1,17},{2,10},{3,19},{4,12},{5,21},{6,14},{7,23},{8,0},{9,25... | collective-permute-start | bytes 442376 | tf_op jit(solution)/shard_map/ppermute | solution.py:400
  50.2 2.3 %collective-permute-done.7.refs_5_ = s16[1,29,16,128]{3,2,1,0:T(8,128)(2,1)S(1)} collective-permute-done((s16[1,29,16,128]{3,2,1,0:T(8,128)(2,1)S(1)}, s16[1,29,16,128]{3,2,1,0:T(8,128)(2,1)S(1)}, u32[]{:S(2)}, u32[]{:S(2)}) %collective-permute-start.7) | collective-permute-done | bytes 118816 | tf_op jit(solution)/shard_map/ppermute | solution.py:400
  52.5 1.3 %collective-permute-start.8 = (s16[2,29,16,128]{3,2,1,0:T(8,128)(2,1)S(1)}, s16[2,29,16,128]{3,2,1,0:T(8,128)(2,1)S(1)}, u32[]{:S(2)}, u32[]{:S(2)}) collective-permute-start(s16[2,29,16,128]{3,2,1,0:T(8,128)(2,1)S(1)} %pad_add_fusion.5), channel_id=1, source_target_pairs={{0,2},{1,5},{2,0},{3,7},{4,6},{5,1},{6,4},{7,3},{8,10},{9,13},{10,... | collective-permute-start | bytes 712712 | tf_op jit(solution)/shard_map/ppermute | solution.py:400
  54.1 2.5 %collective-permute-start.10 = (s16[1,9,32,128]{3,2,1,0:T(8,128)(2,1)S(1)}, s16[1,9,32,128]{3,2,1,0:T(8,128)(2,1)S(1)}, u32[]{:S(2)}, u32[]{:S(2)}) collective-permute-start(s16[1,9,32,128]{3,2,1,0:T(8,128)(2,1)S(1)} %slice.110), channel_id=1, source_target_pairs={{0,16},{1,9},{2,18},{3,11},{4,20},{5,13},{6,22},{7,15},{8,24},{9,1... | collective-permute-start | bytes 221192 | tf_op jit(solution)/shard_map/ppermute | solution.py:400
  56.5 2.9 %collective-permute-done.10 = s16[1,9,32,128]{3,2,1,0:T(8,128)(2,1)S(1)} collective-permute-done((s16[1,9,32,128]{3,2,1,0:T(8,128)(2,1)S(1)}, s16[1,9,32,128]{3,2,1,0:T(8,128)(2,1)S(1)}, u32[]{:S(2)}, u32[]{:S(2)}) %collective-permute-start.10) | collective-permute-done | bytes 73760 | tf_op jit(solution)/shard_map/ppermute | solution.py:400
  59.5 1.8 %collective-permute-done.11.refs_7_ = s16[4,29,16,128]{3,2,1,0:T(8,128)(2,1)S(1)} collective-permute-done((s16[4,29,16,128]{3,2,1,0:T(8,128)(2,1)S(1)}, s16[4,29,16,128]{3,2,1,0:T(8,128)(2,1)S(1)}, u32[]{:S(2)}, u32[]{:S(2)}) %collective-permute-start.11) | collective-permute-done | bytes 475168 | tf_op jit(solution)/shard_map/ppermute | solution.py:403
  61.3 14.0 %blocked_solve.1 = (f32[2048,1024]{1,0:T(8,128)}, f32[32,1024]{1,0:T(8,128)}) custom-call(s32[2]{0:T(128)S(1)} %pad_add_fusion.10.refs_0_, bf16[1280,2048]{1,0:T(8,128)(2,1)} %copy-done.7, bf16[768,2048]{1,0:T(8,128)(2,1)} %copy-done.4, f32[8,128,128]{2,1,0:T(8,128)S(1)} %copy-done.5, s16[1,29,16,128]{3,2,1,0:T(8,128)(2,1)S(1)} %add.83.refs_4_, ...), custom_call_target="tpu_custom_call" | custom-call | flops 8000000000 | bytes 20971520 | tf_op jit(solution)/shard_map/blocked_solve/pallas_call | solution.py:365
  (53 shorter events, 1.5 us)
Async XLA Ops:
  0.6 7.3 %collective-permute-start = (bf16[1024,1024]{1,0:T(8,128)(2,1)}, bf16[1024,1024]{1,0:T(8,128)(2,1)S(1)}, u32[]{:S(2)}, u32[]{:S(2)}) collective-permute-start(bf16[1024,1024]{1,0:T(8,128)(2,1)} %refs_3_.4), channel_id=1, source_target_pairs={{0,1},{1,0},{2,3},{3,2},{4,5},{5,4},{6,7},{7,6},{8,9},{9,8},{10,11... | collective-permute-start | bytes 6291464 | tf_op jit(solution)/shard_map/ppermute | solution.py:403
  1.2 3.4 %copy-start = (bf16[4096,1024]{1,0:T(8,128)(2,1)S(1)}, bf16[4096,1024]{1,0:T(8,128)(2,1)}, u32[]{:S(2)}) copy-start(bf16[4096,1024]{1,0:T(8,128)(2,1)} %refs_1_.3) | copy-start | bytes 25165828
  4.6 0.7 copy-start.6
  7.9 2.1 %copy-start.8 = (bf16[2,256,512]{2,1,0:T(8,128)(2,1)}, bf16[2,256,512]{2,1,0:T(8,128)(2,1)S(1)}, u32[]{:S(2)}) copy-start(bf16[2,256,512]{2,1,0:T(8,128)(2,1)S(1)} %get-tuple-element.22.refs_1_) | copy-start | bytes 1572868
  8.0 2.0 %collective-permute-start.1 = (bf16[256,1024]{1,0:T(8,128)(2,1)S(1)}, bf16[256,1024]{1,0:T(8,128)(2,1)S(1)}, u32[]{:S(2)}, u32[]{:S(2)}) collective-permute-start(bf16[256,1024]{1,0:T(8,128)(2,1)S(1)} %broadcast_add_fusion.1), channel_id=1, source_target_pairs={{0,1},{1,0},{2,3},{3,2},{4,5},{5,4},{6,7},{7,6},{8,9},{9,8},{10,11... | collective-permute-start | bytes 1572872 | tf_op jit(solution)/shard_map/ppermute | solution.py:403
  10.0 9.5 %collective-permute-start.2 = (bf16[2048,1024]{1,0:T(8,128)(2,1)}, bf16[2048,1024]{1,0:T(8,128)(2,1)}, u32[]{:S(2)}, u32[]{:S(2)}) collective-permute-start(bf16[2048,1024]{1,0:T(8,128)(2,1)} %get-tuple-element.19), channel_id=1, source_target_pairs={{0,1},{1,0},{2,3},{3,2},{4,5},{5,4},{6,7},{7,6},{8,9},{9,8},{10,11... | collective-permute-start | bytes 12582920 | tf_op jit(solution)/shard_map/ppermute | solution.py:403
  10.1 1.6 %copy-start.2 = (bf16[1024,1024]{1,0:T(8,128)(2,1)S(1)}, bf16[1024,1024]{1,0:T(8,128)(2,1)}, u32[]{:S(2)}) copy-start(bf16[1024,1024]{1,0:T(8,128)(2,1)} %refs_3_.4) | copy-start | bytes 6291460
  11.7 1.0 %copy-start.9 = (bf16[2,256,512]{2,1,0:T(8,128)(2,1)S(1)}, bf16[2,256,512]{2,1,0:T(8,128)(2,1)}, u32[]{:S(2)}) copy-start(bf16[2,256,512]{2,1,0:T(8,128)(2,1)} %copy-done.8) | copy-start | bytes 1572868
  12.8 6.7 %copy-start.1 = (bf16[4096,1024]{1,0:T(8,128)(2,1)S(1)}, bf16[4096,1024]{1,0:T(8,128)(2,1)}, u32[]{:S(2)}) copy-start(bf16[4096,1024]{1,0:T(8,128)(2,1)} %refs_1_.3) | copy-start | bytes 25165828
  12.8 6.7 %copy-start.3 = (bf16[1024,1024]{1,0:T(8,128)(2,1)S(1)}, bf16[1024,1024]{1,0:T(8,128)(2,1)}, u32[]{:S(2)}) copy-start(bf16[1024,1024]{1,0:T(8,128)(2,1)} %refs_3_.4) | copy-start | bytes 6291460
  16.6 11.2 %collective-permute-start.3 = (s16[2,1136,128]{2,1,0:T(8,128)(2,1)S(1)}, s16[2,1136,128]{2,1,0:T(8,128)(2,1)S(1)}, u32[]{:S(2)}, u32[]{:S(2)}) collective-permute-start(s16[2,1136,128]{2,1,0:T(8,128)(2,1)S(1)} %pad_add_fusion), channel_id=1, source_target_pairs={{0,2},{1,5},{2,0},{3,7},{4,6},{5,1},{6,4},{7,3},{8,10},{9,13},{10,... | collective-permute-start | bytes 1744904 | tf_op jit(solution)/shard_map/ppermute | solution.py:400
  27.7 7.6 %copy-start.7 = (bf16[1280,2048]{1,0:T(8,128)(2,1)}, bf16[1280,2048]{1,0:T(8,128)(2,1)S(1)}, u32[]{:S(2)}) copy-start(bf16[1280,2048]{1,0:T(8,128)(2,1)S(1)} %get-tuple-element.21.refs_1_) | copy-start | bytes 15728644
  28.0 7.4 %collective-permute-start.4 = (s16[1,1136,128]{2,1,0:T(8,128)(2,1)S(1)}, s16[1,1136,128]{2,1,0:T(8,128)(2,1)S(1)}, u32[]{:S(2)}, u32[]{:S(2)}) collective-permute-start(s16[1,1136,128]{2,1,0:T(8,128)(2,1)S(1)} %fusion.1.refs_5_), channel_id=1, source_target_pairs={{0,4},{1,3},{2,6},{3,1},{4,0},{5,7},{6,2},{7,5},{8,12},{9,11},{10,... | collective-permute-start | bytes 872456 | tf_op jit(solution)/shard_map/ppermute | solution.py:400
  35.3 24.1 %copy-start.4 = (bf16[768,2048]{1,0:T(8,128)(2,1)}, bf16[768,2048]{1,0:T(8,128)(2,1)S(1)}, u32[]{:S(2)}) copy-start(bf16[768,2048]{1,0:T(8,128)(2,1)S(1)} %get-tuple-element.28.refs_2_) | copy-start | bytes 9437188
  35.4 26.0 %copy-start.5 = (f32[8,128,128]{2,1,0:T(8,128)S(1)}, f32[8,128,128]{2,1,0:T(8,128)}, u32[]{:S(2)}) copy-start(f32[8,128,128]{2,1,0:T(8,128)} %refs_3_.5) | copy-start | bytes 1572868
  35.6 5.5 %collective-permute-start.5 = (s16[1,29,16,128]{3,2,1,0:T(8,128)(2,1)S(1)}, s16[1,29,16,128]{3,2,1,0:T(8,128)(2,1)S(1)}, u32[]{:S(2)}, u32[]{:S(2)}) collective-permute-start(s16[1,29,16,128]{3,2,1,0:T(8,128)(2,1)S(1)} %bitcast.33), channel_id=1, source_target_pairs={{0,8},{1,17},{2,10},{3,19},{4,12},{5,21},{6,14},{7,23},{8,0},{9,25... | collective-permute-start | bytes 356360 | tf_op jit(solution)/shard_map/ppermute | solution.py:400
  41.1 5.8 %collective-permute-start.6 = (s16[1,29,16,128]{3,2,1,0:T(8,128)(2,1)S(1)}, s16[1,29,16,128]{3,2,1,0:T(8,128)(2,1)S(1)}, u32[]{:S(2)}, u32[]{:S(2)}) collective-permute-start(s16[1,29,16,128]{3,2,1,0:T(8,128)(2,1)S(1)} %add.82), channel_id=1, source_target_pairs={{0,16},{1,9},{2,18},{3,11},{4,20},{5,13},{6,22},{7,15},{8,24},{9,1... | collective-permute-start | bytes 356360 | tf_op jit(solution)/shard_map/ppermute | solution.py:400
  47.0 5.5 %collective-permute-start.7 = (s16[1,29,16,128]{3,2,1,0:T(8,128)(2,1)S(1)}, s16[1,29,16,128]{3,2,1,0:T(8,128)(2,1)S(1)}, u32[]{:S(2)}, u32[]{:S(2)}) collective-permute-start(s16[1,29,16,128]{3,2,1,0:T(8,128)(2,1)S(1)} %add.83.refs_4_), channel_id=1, source_target_pairs={{0,4},{1,3},{2,6},{3,1},{4,0},{5,7},{6,2},{7,5},{8,12},{9,11},{10,... | collective-permute-start | bytes 356360 | tf_op jit(solution)/shard_map/ppermute | solution.py:400
  48.3 5.7 %collective-permute-start.9 = (s16[2,9,32,128]{3,2,1,0:T(8,128)(2,1)S(1)}, s16[2,9,32,128]{3,2,1,0:T(8,128)(2,1)S(1)}, u32[]{:S(2)}, u32[]{:S(2)}) collective-permute-start(s16[2,9,32,128]{3,2,1,0:T(8,128)(2,1)S(1)} %slice.95), channel_id=1, source_target_pairs={{0,8},{1,17},{2,10},{3,19},{4,12},{5,21},{6,14},{7,23},{8,0},{9,25... | collective-permute-start | bytes 442376 | tf_op jit(solution)/shard_map/ppermute | solution.py:400
  52.5 6.9 %collective-permute-start.8 = (s16[2,29,16,128]{3,2,1,0:T(8,128)(2,1)S(1)}, s16[2,29,16,128]{3,2,1,0:T(8,128)(2,1)S(1)}, u32[]{:S(2)}, u32[]{:S(2)}) collective-permute-start(s16[2,29,16,128]{3,2,1,0:T(8,128)(2,1)S(1)} %pad_add_fusion.5), channel_id=1, source_target_pairs={{0,2},{1,5},{2,0},{3,7},{4,6},{5,1},{6,4},{7,3},{8,10},{9,13},{10,... | collective-permute-start | bytes 712712 | tf_op jit(solution)/shard_map/ppermute | solution.py:400
  54.1 5.3 %collective-permute-start.10 = (s16[1,9,32,128]{3,2,1,0:T(8,128)(2,1)S(1)}, s16[1,9,32,128]{3,2,1,0:T(8,128)(2,1)S(1)}, u32[]{:S(2)}, u32[]{:S(2)}) collective-permute-start(s16[1,9,32,128]{3,2,1,0:T(8,128)(2,1)S(1)} %slice.110), channel_id=1, source_target_pairs={{0,16},{1,9},{2,18},{3,11},{4,20},{5,13},{6,22},{7,15},{8,24},{9,1... | collective-permute-start | bytes 221192 | tf_op jit(solution)/shard_map/ppermute | solution.py:400
  59.4 1.9 %collective-permute-start.11 = (s16[4,29,16,128]{3,2,1,0:T(8,128)(2,1)S(1)}, s16[4,29,16,128]{3,2,1,0:T(8,128)(2,1)S(1)}, u32[]{:S(2)}, u32[]{:S(2)}) collective-permute-start(s16[4,29,16,128]{3,2,1,0:T(8,128)(2,1)S(1)} %pad_add_fusion.1), channel_id=1, source_target_pairs={{0,1},{1,0},{2,3},{3,2},{4,5},{5,4},{6,7},{7,6},{8,9},{9,8},{10,11... | collective-permute-start | bytes 1425416 | tf_op jit(solution)/shard_map/ppermute | solution.py:403

commit v5 on v4

--- a/solution.py
+++ b/solution.py
@@ -291,7 +291,7 @@
 
 def solve_kernel(share, parts, meta, *refs):
     sketches, refs = refs[:parts], refs[parts:]
-    (inverses, p0, p1, p2, p3, low, out, own_rows,
+    (inverses, p0, p1, p2, p3, p4, low, out, own_rows,
      coupling, weights, earlier, pair_v, out_v, in_sems, out_sems) = refs
     tile = out_v.shape[1]
     steps = out.shape[0] // tile
@@ -317,7 +317,7 @@
 
     start_in(jnp.int32(0))
     start_in(jnp.int32(1))
-    prepare(share, meta[0], meta[1], inverses, (p0, p1, p2, p3), low, own_rows, coupling, weights)
+    prepare(share, meta[0], meta[1], inverses, (p0, p1, p2, p3, p4), low, own_rows, coupling, weights)
     sub = 256
 
     @pl.loop(0, steps)
@@ -466,8 +466,8 @@
     piece1 = got
     pair = jnp.concatenate([total, piece1], axis=0)
     piece2 = after(swap(pair, near), low_got)
-    piece3 = swap_cores(jnp.concatenate([pair, piece2], axis=0))
-    return solve(meta, sketches, block_inverses, (total, piece1, piece2, piece3), low[0], share)
+    piece3, piece4 = swap_cores(pair), swap_cores(piece2)
+    return solve(meta, sketches, block_inverses, (total, piece1, piece2, piece3, piece4), low[0], share)
 
 
 def solution(mesh):

time: 76.2 us -> 75.7 us (level)
    ppermute x4 -> x5, waiting for transfers between devices: 3.65 us -> 3.31 us  [swap_cores(): return lax.ppermute(value, 'col', [(0, 1), (1, 0)])]
  transfers between devices with their start and end apart: 12 -> 13, of which waited for: 7 -> 7; matrix products, arithmetic and copies ran while one was open for 0% -> 0% of each run, Pallas kernels for 27% -> 27%
where the time goes in v5:
time: 75.7 us; the launch traced here: 75 us
  Pallas kernels  34.3 us (45%)
  starting transfers between devices  16.2 us (21%)
  waiting for transfers between devices  15.9 us (21%)
  local copies, waits for them, and re-layouts  6.81 us (9%)
  between operations  1.06 us (1%)
    ppermute x8, starting transfers between devices, swap(): return lax.ppermute(value, ('row', 'col'), perm)  15.4 us
    pallas_call x2, Pallas kernels, sketch_rows(): pl.pallas_call(lambda *refs: sketch_kernel(first, *refs), out_shape=(jax....  14 us
    pallas_call x1, Pallas kernels, solve(): pl.pallas_call(lambda *refs: solve_kernel(share, parts, *refs), out_shape...  14 us
    ppermute x8, waiting for transfers between devices, swap(): return lax.ppermute(value, ('row', 'col'), perm)  12.6 us
    unnamed x20, local copies, waits for them, and re-layouts  6.73 us
    pallas_call x1, Pallas kernels, pivot_rows(): pl.pallas_call(lambda *refs: pivot_kernel(share, *refs), out_shape=(u_out...  3.72 us
    ppermute x5, waiting for transfers between devices, swap_cores(): return lax.ppermute(value, 'col', [(0, 1), (1, 0)])  3.31 us
    pallas_call x1, Pallas kernels, pick(): pl.pallas_call(lambda *refs: pick_kernel(share, *refs), out_shape=(jax.Sh...  2.62 us
  transfers between devices with their start and end apart: 13, of which 7 were waited for; matrix products, arithmetic and copies ran while one was open for 0% of the time, Pallas kernels for 27%

profile of v5, /device:TPU:0, one launch (start us, length us, event | category | flops | bytes accessed | tf_op | source)
XLA Modules:
  0.0 75.0 jit_solution(7504791610574147167)
XLA Ops:
  0.6 0.5 collective-permute-start
  1.2 3.4 %copy-done = bf16[4096,1024]{1,0:T(8,128)(2,1)S(1)} copy-done((bf16[4096,1024]{1,0:T(8,128)(2,1)S(1)}, bf16[4096,1024]{1,0:T(8,128)(2,1)}, u32[]{:S(2)}) %copy-start) | copy-done | bytes 8388632
  4.6 0.7 copy-done.6
  5.3 2.6 %pick_pivot_rows.1 = (bf16[256,1024]{1,0:T(8,128)(2,1)S(1)}, bf16[2,256,512]{2,1,0:T(8,128)(2,1)S(1)}, bf16[2048,1024]{1,0:T(8,128)(2,1)}) custom-call(s32[2]{0:T(128)S(1)} %pad_add_fusion.9.refs_0_, s32[1,1024]{1,0:T(1,128)S(1)} %bitcast.32, bf16[4096,1024]{1,0:T(8,128)(2,1)S(1)} %copy-done), custom_call_target="tpu_custom_call" | custom-call | flops 4000000000 | bytes 14680064 | tf_op jit(solution)/shard_map/pick_pivot_rows/pallas_call | solution.py:110
  8.1 1.9 %collective-permute-done.1.refs_3_ = bf16[256,1024]{1,0:T(8,128)(2,1)S(1)} collective-permute-done((bf16[256,1024]{1,0:T(8,128)(2,1)S(1)}, bf16[256,1024]{1,0:T(8,128)(2,1)S(1)}, u32[]{:S(2)}, u32[]{:S(2)}) %collective-permute-start.1) | collective-permute-done | bytes 524320 | tf_op jit(solution)/shard_map/ppermute | solution.py:403
  10.1 1.6 %copy-done.2 = bf16[1024,1024]{1,0:T(8,128)(2,1)S(1)} copy-done((bf16[1024,1024]{1,0:T(8,128)(2,1)S(1)}, bf16[1024,1024]{1,0:T(8,128)(2,1)}, u32[]{:S(2)}) %copy-start.2) | copy-done | bytes 2097176
  11.7 1.0 %copy-done.9 = bf16[2,256,512]{2,1,0:T(8,128)(2,1)S(1)} copy-done((bf16[2,256,512]{2,1,0:T(8,128)(2,1)S(1)}, bf16[2,256,512]{2,1,0:T(8,128)(2,1)}, u32[]{:S(2)}) %copy-start.9) | copy-done | bytes 524312
  12.8 3.7 %pivot_rows.1 = (s16[2,29,16,128]{3,2,1,0:T(8,128)(2,1)S(1)}, s16[2,29,16,128]{3,2,1,0:T(8,128)(2,1)S(1)}, s16[2,21,32,128]{3,2,1,0:T(8,128)(2,1)S(1)}, s16[2,21,32,128]{3,2,1,0:T(8,128)(2,1)S(1)}) custom-call(s32[2]{0:T(128)S(1)} %pad_add_fusion.9.refs_0_, bf16[2,256,512]{2,1,0:T(8,128)(2,1)S(1)} %copy-done.9, ...), custom_call_target="tpu_custom_call" | custom-call | flops 3000000000 | bytes 8388608 | tf_op jit(solution)/shard_map/pivot_rows/pallas_call | solution.py:182
  16.6 2.9 %collective-permute-start.3 = (s16[2,1136,128]{2,1,0:T(8,128)(2,1)S(1)}, s16[2,1136,128]{2,1,0:T(8,128)(2,1)S(1)}, u32[]{:S(2)}, u32[]{:S(2)}) collective-permute-start(s16[2,1136,128]{2,1,0:T(8,128)(2,1)S(1)} %pad_add_fusion), channel_id=1, source_target_pairs={{0,2},{1,5},{2,0},{3,7},{4,6},{5,1},{6,4},{7,3},{8,10},{9,13},{10,... | collective-permute-start | bytes 1744904 | tf_op jit(solution)/shard_map/ppermute | solution.py:400
  19.5 8.2 %sketch_rows.2 = (bf16[1280,2048]{1,0:T(8,128)(2,1)S(1)}, s16[16,128]{1,0:T(8,128)(2,1)S(1)}) custom-call(s32[2]{0:T(128)S(1)} %pad_add_fusion.9.refs_0_, bf16[4096,1024]{1,0:T(8,128)(2,1)S(1)} %copy-done.1, bf16[2048,1024]{1,0:T(8,128)(2,1)} %collective-permute-done.2.refs_2_, bf16[1024,1024]{1,0:T(8,128)(2,1)S(1)} %copy-done.3, ...), custom_call_target="tpu_custom_call" | custom-call | flops 5368709120 | bytes 10485760 | tf_op jit(solution)/shard_map/sketch_rows/pallas_call | solution.py:219
  28.0 1.6 %collective-permute-start.4 = (s16[1,1136,128]{2,1,0:T(8,128)(2,1)S(1)}, s16[1,1136,128]{2,1,0:T(8,128)(2,1)S(1)}, u32[]{:S(2)}, u32[]{:S(2)}) collective-permute-start(s16[1,1136,128]{2,1,0:T(8,128)(2,1)S(1)} %fusion.1.refs_5_), channel_id=1, source_target_pairs={{0,4},{1,3},{2,6},{3,1},{4,0},{5,7},{6,2},{7,5},{8,12},{9,11},{10,... | collective-permute-start | bytes 872456 | tf_op jit(solution)/shard_map/ppermute | solution.py:400
  29.6 5.8 %sketch_rows.3 = (bf16[768,2048]{1,0:T(8,128)(2,1)S(1)}, s16[16,128]{1,0:T(8,128)(2,1)S(1)}) custom-call(s32[2]{0:T(128)S(1)} %pad_add_fusion.9.refs_0_, bf16[4096,1024]{1,0:T(8,128)(2,1)S(1)} %copy-done.1, bf16[2048,1024]{1,0:T(8,128)(2,1)} %collective-permute-done.2.refs_2_, bf16[1024,1024]{1,0:T(8,128)(2,1)S(1)} %copy-done.3, ...), custom_call_target="tpu_custom_call" | custom-call | flops 3221225472 | bytes 10485760 | tf_op jit(solution)/shard_map/sketch_rows/pallas_call | solution.py:219
  35.6 1.7 %collective-permute-start.5 = (s16[1,29,16,128]{3,2,1,0:T(8,128)(2,1)S(1)}, s16[1,29,16,128]{3,2,1,0:T(8,128)(2,1)S(1)}, u32[]{:S(2)}, u32[]{:S(2)}) collective-permute-start(s16[1,29,16,128]{3,2,1,0:T(8,128)(2,1)S(1)} %bitcast.33), channel_id=1, source_target_pairs={{0,8},{1,17},{2,10},{3,19},{4,12},{5,21},{6,14},{7,23},{8,0},{9,25... | collective-permute-start | bytes 356360 | tf_op jit(solution)/shard_map/ppermute | solution.py:400
  37.3 3.8 %collective-permute-done.5 = s16[1,29,16,128]{3,2,1,0:T(8,128)(2,1)S(1)} collective-permute-done((s16[1,29,16,128]{3,2,1,0:T(8,128)(2,1)S(1)}, s16[1,29,16,128]{3,2,1,0:T(8,128)(2,1)S(1)}, u32[]{:S(2)}, u32[]{:S(2)}) %collective-permute-start.5) | collective-permute-done | bytes 118816 | tf_op jit(solution)/shard_map/ppermute | solution.py:400
  41.1 2.3 %collective-permute-start.6 = (s16[1,29,16,128]{3,2,1,0:T(8,128)(2,1)S(1)}, s16[1,29,16,128]{3,2,1,0:T(8,128)(2,1)S(1)}, u32[]{:S(2)}, u32[]{:S(2)}) collective-permute-start(s16[1,29,16,128]{3,2,1,0:T(8,128)(2,1)S(1)} %add.82), channel_id=1, source_target_pairs={{0,16},{1,9},{2,18},{3,11},{4,20},{5,13},{6,22},{7,15},{8,24},{9,1... | collective-permute-start | bytes 356360 | tf_op jit(solution)/shard_map/ppermute | solution.py:400
  43.5 3.5 %collective-permute-done.6 = s16[1,29,16,128]{3,2,1,0:T(8,128)(2,1)S(1)} collective-permute-done((s16[1,29,16,128]{3,2,1,0:T(8,128)(2,1)S(1)}, s16[1,29,16,128]{3,2,1,0:T(8,128)(2,1)S(1)}, u32[]{:S(2)}, u32[]{:S(2)}) %collective-permute-start.6) | collective-permute-done | bytes 118816 | tf_op jit(solution)/shard_map/ppermute | solution.py:400
  47.0 1.2 %collective-permute-start.7 = (s16[1,29,16,128]{3,2,1,0:T(8,128)(2,1)S(1)}, s16[1,29,16,128]{3,2,1,0:T(8,128)(2,1)S(1)}, u32[]{:S(2)}, u32[]{:S(2)}) collective-permute-start(s16[1,29,16,128]{3,2,1,0:T(8,128)(2,1)S(1)} %add.83.refs_4_), channel_id=1, source_target_pairs={{0,4},{1,3},{2,6},{3,1},{4,0},{5,7},{6,2},{7,5},{8,12},{9,11},{10,... | collective-permute-start | bytes 356360 | tf_op jit(solution)/shard_map/ppermute | solution.py:400
  48.3 1.9 %collective-permute-start.9 = (s16[2,9,32,128]{3,2,1,0:T(8,128)(2,1)S(1)}, s16[2,9,32,128]{3,2,1,0:T(8,128)(2,1)S(1)}, u32[]{:S(2)}, u32[]{:S(2)}) collective-permute-start(s16[2,9,32,128]{3,2,1,0:T(8,128)(2,1)S(1)} %slice.95), channel_id=1, source_target_pairs={{0,8},{1,17},{2,10},{3,19},{4,12},{5,21},{6,14},{7,23},{8,0},{9,25... | collective-permute-start | bytes 442376 | tf_op jit(solution)/shard_map/ppermute | solution.py:400
  50.2 2.3 %collective-permute-done.7.refs_5_ = s16[1,29,16,128]{3,2,1,0:T(8,128)(2,1)S(1)} collective-permute-done((s16[1,29,16,128]{3,2,1,0:T(8,128)(2,1)S(1)}, s16[1,29,16,128]{3,2,1,0:T(8,128)(2,1)S(1)}, u32[]{:S(2)}, u32[]{:S(2)}) %collective-permute-start.7) | collective-permute-done | bytes 118816 | tf_op jit(solution)/shard_map/ppermute | solution.py:400
  52.5 1.3 %collective-permute-start.8 = (s16[2,29,16,128]{3,2,1,0:T(8,128)(2,1)S(1)}, s16[2,29,16,128]{3,2,1,0:T(8,128)(2,1)S(1)}, u32[]{:S(2)}, u32[]{:S(2)}) collective-permute-start(s16[2,29,16,128]{3,2,1,0:T(8,128)(2,1)S(1)} %pad_add_fusion.4), channel_id=1, source_target_pairs={{0,2},{1,5},{2,0},{3,7},{4,6},{5,1},{6,4},{7,3},{8,10},{9,13},{10,... | collective-permute-start | bytes 712712 | tf_op jit(solution)/shard_map/ppermute | solution.py:400
  54.0 2.5 %collective-permute-start.10 = (s16[1,9,32,128]{3,2,1,0:T(8,128)(2,1)S(1)}, s16[1,9,32,128]{3,2,1,0:T(8,128)(2,1)S(1)}, u32[]{:S(2)}, u32[]{:S(2)}) collective-permute-start(s16[1,9,32,128]{3,2,1,0:T(8,128)(2,1)S(1)} %slice.110), channel_id=1, source_target_pairs={{0,16},{1,9},{2,18},{3,11},{4,20},{5,13},{6,22},{7,15},{8,24},{9,1... | collective-permute-start | bytes 221192 | tf_op jit(solution)/shard_map/ppermute | solution.py:400
  56.5 2.9 %collective-permute-done.10 = s16[1,9,32,128]{3,2,1,0:T(8,128)(2,1)S(1)} collective-permute-done((s16[1,9,32,128]{3,2,1,0:T(8,128)(2,1)S(1)}, s16[1,9,32,128]{3,2,1,0:T(8,128)(2,1)S(1)}, u32[]{:S(2)}, u32[]{:S(2)}) %collective-permute-start.10) | collective-permute-done | bytes 73760 | tf_op jit(solution)/shard_map/ppermute | solution.py:400
  59.4 1.4 %collective-permute-done.12.refs_8_ = s16[2,29,16,128]{3,2,1,0:T(8,128)(2,1)S(1)} collective-permute-done((s16[2,29,16,128]{3,2,1,0:T(8,128)(2,1)S(1)}, s16[2,29,16,128]{3,2,1,0:T(8,128)(2,1)S(1)}, u32[]{:S(2)}, u32[]{:S(2)}) %collective-permute-start.12) | collective-permute-done | bytes 237600 | tf_op jit(solution)/shard_map/ppermute | solution.py:403
  60.9 14.0 %blocked_solve.1 = (f32[2048,1024]{1,0:T(8,128)}, f32[32,1024]{1,0:T(8,128)}) custom-call(s32[2]{0:T(128)S(1)} %pad_add_fusion.9.refs_0_, bf16[1280,2048]{1,0:T(8,128)(2,1)} %copy-done.7, bf16[768,2048]{1,0:T(8,128)(2,1)} %copy-done.4, f32[8,128,128]{2,1,0:T(8,128)S(1)} %copy-done.5, s16[1,29,16,128]{3,2,1,0:T(8,128)(2,1)S(1)} %add.83.refs_4_, ...), custom_call_target="tpu_custom_call" | custom-call | flops 8000000000 | bytes 20971520 | tf_op jit(solution)/shard_map/blocked_solve/pallas_call | solution.py:365
  (54 shorter events, 1.3 us)
Async XLA Ops:
  0.6 7.3 %collective-permute-start = (bf16[1024,1024]{1,0:T(8,128)(2,1)}, bf16[1024,1024]{1,0:T(8,128)(2,1)S(1)}, u32[]{:S(2)}, u32[]{:S(2)}) collective-permute-start(bf16[1024,1024]{1,0:T(8,128)(2,1)} %refs_3_.4), channel_id=1, source_target_pairs={{0,1},{1,0},{2,3},{3,2},{4,5},{5,4},{6,7},{7,6},{8,9},{9,8},{10,11... | collective-permute-start | bytes 6291464 | tf_op jit(solution)/shard_map/ppermute | solution.py:403
  1.2 3.4 %copy-start = (bf16[4096,1024]{1,0:T(8,128)(2,1)S(1)}, bf16[4096,1024]{1,0:T(8,128)(2,1)}, u32[]{:S(2)}) copy-start(bf16[4096,1024]{1,0:T(8,128)(2,1)} %refs_1_.3) | copy-start | bytes 25165828
  4.6 0.7 copy-start.6
  7.9 2.1 %copy-start.8 = (bf16[2,256,512]{2,1,0:T(8,128)(2,1)}, bf16[2,256,512]{2,1,0:T(8,128)(2,1)S(1)}, u32[]{:S(2)}) copy-start(bf16[2,256,512]{2,1,0:T(8,128)(2,1)S(1)} %get-tuple-element.22.refs_1_) | copy-start | bytes 1572868
  8.0 2.0 %collective-permute-start.1 = (bf16[256,1024]{1,0:T(8,128)(2,1)S(1)}, bf16[256,1024]{1,0:T(8,128)(2,1)S(1)}, u32[]{:S(2)}, u32[]{:S(2)}) collective-permute-start(bf16[256,1024]{1,0:T(8,128)(2,1)S(1)} %broadcast_add_fusion.1), channel_id=1, source_target_pairs={{0,1},{1,0},{2,3},{3,2},{4,5},{5,4},{6,7},{7,6},{8,9},{9,8},{10,11... | collective-permute-start | bytes 1572872 | tf_op jit(solution)/shard_map/ppermute | solution.py:403
  10.0 9.5 %collective-permute-start.2 = (bf16[2048,1024]{1,0:T(8,128)(2,1)}, bf16[2048,1024]{1,0:T(8,128)(2,1)}, u32[]{:S(2)}, u32[]{:S(2)}) collective-permute-start(bf16[2048,1024]{1,0:T(8,128)(2,1)} %get-tuple-element.19), channel_id=1, source_target_pairs={{0,1},{1,0},{2,3},{3,2},{4,5},{5,4},{6,7},{7,6},{8,9},{9,8},{10,11... | collective-permute-start | bytes 12582920 | tf_op jit(solution)/shard_map/ppermute | solution.py:403
  10.1 1.6 %copy-start.2 = (bf16[1024,1024]{1,0:T(8,128)(2,1)S(1)}, bf16[1024,1024]{1,0:T(8,128)(2,1)}, u32[]{:S(2)}) copy-start(bf16[1024,1024]{1,0:T(8,128)(2,1)} %refs_3_.4) | copy-start | bytes 6291460
  11.7 1.0 %copy-start.9 = (bf16[2,256,512]{2,1,0:T(8,128)(2,1)S(1)}, bf16[2,256,512]{2,1,0:T(8,128)(2,1)}, u32[]{:S(2)}) copy-start(bf16[2,256,512]{2,1,0:T(8,128)(2,1)} %copy-done.8) | copy-start | bytes 1572868
  12.8 6.7 %copy-start.1 = (bf16[4096,1024]{1,0:T(8,128)(2,1)S(1)}, bf16[4096,1024]{1,0:T(8,128)(2,1)}, u32[]{:S(2)}) copy-start(bf16[4096,1024]{1,0:T(8,128)(2,1)} %refs_1_.3) | copy-start | bytes 25165828
  12.8 6.7 %copy-start.3 = (bf16[1024,1024]{1,0:T(8,128)(2,1)S(1)}, bf16[1024,1024]{1,0:T(8,128)(2,1)}, u32[]{:S(2)}) copy-start(bf16[1024,1024]{1,0:T(8,128)(2,1)} %refs_3_.4) | copy-start | bytes 6291460
  16.6 11.2 %collective-permute-start.3 = (s16[2,1136,128]{2,1,0:T(8,128)(2,1)S(1)}, s16[2,1136,128]{2,1,0:T(8,128)(2,1)S(1)}, u32[]{:S(2)}, u32[]{:S(2)}) collective-permute-start(s16[2,1136,128]{2,1,0:T(8,128)(2,1)S(1)} %pad_add_fusion), channel_id=1, source_target_pairs={{0,2},{1,5},{2,0},{3,7},{4,6},{5,1},{6,4},{7,3},{8,10},{9,13},{10,... | collective-permute-start | bytes 1744904 | tf_op jit(solution)/shard_map/ppermute | solution.py:400
  27.7 7.6 %copy-start.7 = (bf16[1280,2048]{1,0:T(8,128)(2,1)}, bf16[1280,2048]{1,0:T(8,128)(2,1)S(1)}, u32[]{:S(2)}) copy-start(bf16[1280,2048]{1,0:T(8,128)(2,1)S(1)} %get-tuple-element.21.refs_1_) | copy-start | bytes 15728644
  28.0 7.4 %collective-permute-start.4 = (s16[1,1136,128]{2,1,0:T(8,128)(2,1)S(1)}, s16[1,1136,128]{2,1,0:T(8,128)(2,1)S(1)}, u32[]{:S(2)}, u32[]{:S(2)}) collective-permute-start(s16[1,1136,128]{2,1,0:T(8,128)(2,1)S(1)} %fusion.1.refs_5_), channel_id=1, source_target_pairs={{0,4},{1,3},{2,6},{3,1},{4,0},{5,7},{6,2},{7,5},{8,12},{9,11},{10,... | collective-permute-start | bytes 872456 | tf_op jit(solution)/shard_map/ppermute | solution.py:400
  35.3 24.0 %copy-start.4 = (bf16[768,2048]{1,0:T(8,128)(2,1)}, bf16[768,2048]{1,0:T(8,128)(2,1)S(1)}, u32[]{:S(2)}) copy-start(bf16[768,2048]{1,0:T(8,128)(2,1)S(1)} %get-tuple-element.28.refs_2_) | copy-start | bytes 9437188
  35.4 25.5 %copy-start.5 = (f32[8,128,128]{2,1,0:T(8,128)S(1)}, f32[8,128,128]{2,1,0:T(8,128)}, u32[]{:S(2)}) copy-start(f32[8,128,128]{2,1,0:T(8,128)} %refs_3_.5) | copy-start | bytes 1572868
  35.6 5.5 %collective-permute-start.5 = (s16[1,29,16,128]{3,2,1,0:T(8,128)(2,1)S(1)}, s16[1,29,16,128]{3,2,1,0:T(8,128)(2,1)S(1)}, u32[]{:S(2)}, u32[]{:S(2)}) collective-permute-start(s16[1,29,16,128]{3,2,1,0:T(8,128)(2,1)S(1)} %bitcast.33), channel_id=1, source_target_pairs={{0,8},{1,17},{2,10},{3,19},{4,12},{5,21},{6,14},{7,23},{8,0},{9,25... | collective-permute-start | bytes 356360 | tf_op jit(solution)/shard_map/ppermute | solution.py:400
  41.1 5.8 %collective-permute-start.6 = (s16[1,29,16,128]{3,2,1,0:T(8,128)(2,1)S(1)}, s16[1,29,16,128]{3,2,1,0:T(8,128)(2,1)S(1)}, u32[]{:S(2)}, u32[]{:S(2)}) collective-permute-start(s16[1,29,16,128]{3,2,1,0:T(8,128)(2,1)S(1)} %add.82), channel_id=1, source_target_pairs={{0,16},{1,9},{2,18},{3,11},{4,20},{5,13},{6,22},{7,15},{8,24},{9,1... | collective-permute-start | bytes 356360 | tf_op jit(solution)/shard_map/ppermute | solution.py:400
  47.0 5.5 %collective-permute-start.7 = (s16[1,29,16,128]{3,2,1,0:T(8,128)(2,1)S(1)}, s16[1,29,16,128]{3,2,1,0:T(8,128)(2,1)S(1)}, u32[]{:S(2)}, u32[]{:S(2)}) collective-permute-start(s16[1,29,16,128]{3,2,1,0:T(8,128)(2,1)S(1)} %add.83.refs_4_), channel_id=1, source_target_pairs={{0,4},{1,3},{2,6},{3,1},{4,0},{5,7},{6,2},{7,5},{8,12},{9,11},{10,... | collective-permute-start | bytes 356360 | tf_op jit(solution)/shard_map/ppermute | solution.py:400
  48.3 5.7 %collective-permute-start.9 = (s16[2,9,32,128]{3,2,1,0:T(8,128)(2,1)S(1)}, s16[2,9,32,128]{3,2,1,0:T(8,128)(2,1)S(1)}, u32[]{:S(2)}, u32[]{:S(2)}) collective-permute-start(s16[2,9,32,128]{3,2,1,0:T(8,128)(2,1)S(1)} %slice.95), channel_id=1, source_target_pairs={{0,8},{1,17},{2,10},{3,19},{4,12},{5,21},{6,14},{7,23},{8,0},{9,25... | collective-permute-start | bytes 442376 | tf_op jit(solution)/shard_map/ppermute | solution.py:400
  52.5 6.9 %collective-permute-start.8 = (s16[2,29,16,128]{3,2,1,0:T(8,128)(2,1)S(1)}, s16[2,29,16,128]{3,2,1,0:T(8,128)(2,1)S(1)}, u32[]{:S(2)}, u32[]{:S(2)}) collective-permute-start(s16[2,29,16,128]{3,2,1,0:T(8,128)(2,1)S(1)} %pad_add_fusion.4), channel_id=1, source_target_pairs={{0,2},{1,5},{2,0},{3,7},{4,6},{5,1},{6,4},{7,3},{8,10},{9,13},{10,... | collective-permute-start | bytes 712712 | tf_op jit(solution)/shard_map/ppermute | solution.py:400
  54.0 5.3 %collective-permute-start.10 = (s16[1,9,32,128]{3,2,1,0:T(8,128)(2,1)S(1)}, s16[1,9,32,128]{3,2,1,0:T(8,128)(2,1)S(1)}, u32[]{:S(2)}, u32[]{:S(2)}) collective-permute-start(s16[1,9,32,128]{3,2,1,0:T(8,128)(2,1)S(1)} %slice.110), channel_id=1, source_target_pairs={{0,16},{1,9},{2,18},{3,11},{4,20},{5,13},{6,22},{7,15},{8,24},{9,1... | collective-permute-start | bytes 221192 | tf_op jit(solution)/shard_map/ppermute | solution.py:400
  56.5 2.9 %collective-permute-start.11 = (s16[2,29,16,128]{3,2,1,0:T(8,128)(2,1)S(1)}, s16[2,29,16,128]{3,2,1,0:T(8,128)(2,1)S(1)}, u32[]{:S(2)}, u32[]{:S(2)}) collective-permute-start(s16[2,29,16,128]{3,2,1,0:T(8,128)(2,1)S(1)} %pad_add_fusion.4), channel_id=1, source_target_pairs={{0,1},{1,0},{2,3},{3,2},{4,5},{5,4},{6,7},{7,6},{8,9},{9,8},{10,11... | collective-permute-start | bytes 712712 | tf_op jit(solution)/shard_map/ppermute | solution.py:403
  59.4 1.5 %collective-permute-start.12 = (s16[2,29,16,128]{3,2,1,0:T(8,128)(2,1)S(1)}, s16[2,29,16,128]{3,2,1,0:T(8,128)(2,1)S(1)}, u32[]{:S(2)}, u32[]{:S(2)}) collective-permute-start(s16[2,29,16,128]{3,2,1,0:T(8,128)(2,1)S(1)} %collective-permute-done.8.refs_6_), channel_id=1, source_target_pairs={{0,1},{1,0},{2,3},{3,2},{4,5},{5,4},{6,7},{7,6},{8,9},{9,8},{10,11... | collective-permute-start | bytes 712712 | tf_op jit(solution)/shard_map/ppermute | solution.py:403
